TPU v7x, 32 devices: a whole 2x2x4 slice. The times are simulated.
32 devices in a mesh: dp: 8 (over y, x, core), tensor: 4 (over z).
Axes of the slice: x: 2, y: 2, z: 4, core: 2. Of those that a mesh axis runs over, the one named last changes fastest.
Arguments:
- tokens: bfloat16 [8192, 2048], P(('dp', 'tensor')), may hold values from -6 to 6
- first_gain: float32 [2048], replicated, may hold values from 0.1 to 1.9
- first_bias: float32 [2048], replicated, may hold values from -3 to 3
- query_weight: bfloat16 [2048, 2048], P(None, 'tensor'), may hold values from -0.125 to 0.125
- key_weight: bfloat16 [2048, 2048], P(None, 'tensor'), may hold values from -0.125 to 0.125
- value_weight: bfloat16 [2048, 3456], P(None, 'tensor'), may hold values from -0.125 to 0.125
- gate_weight: bfloat16 [2048, 3456], P(None, 'tensor'), may hold values from -0.125 to 0.125
- out_weight: bfloat16 [3456, 2048], P('tensor'), may hold values from -0.21875 to 0.21875
- second_gain: float32 [2048], replicated, may hold values from 0.1 to 1.9
- second_bias: float32 [2048], replicated, may hold values from -3 to 3
- hidden_gate: bfloat16 [2048, 3456], P(None, 'tensor'), may hold values from -0.125 to 0.125
- hidden_up: bfloat16 [2048, 3456], P(None, 'tensor'), may hold values from -0.125 to 0.125
- hidden_down: bfloat16 [3456, 2048], P('tensor'), may hold values from -0.21875 to 0.21875
- segments: int32 [8, 1024], P('dp'), may hold values from 0 to 5, as said below
- cotangent: bfloat16 [8192, 2048], P(('dp', 'tensor')), may hold values from -6 to 6
Outputs:
- output: bfloat16 [8192, 2048], P(('dp', 'tensor'))
- grad_tokens: float32 [8192, 2048], P(('dp', 'tensor'))
- grad_first_gain: float32 [2048], replicated
- grad_first_bias: float32 [2048], replicated
- grad_query: float32 [2048, 2048], P(None, 'tensor')
- grad_key: float32 [2048, 2048], P(None, 'tensor')
- grad_value: float32 [2048, 3456], P(None, 'tensor')
- grad_gate: float32 [2048, 3456], P(None, 'tensor')
- grad_out: float32 [3456, 2048], P('tensor')
- grad_second_gain: float32 [2048], replicated
- grad_second_bias: float32 [2048], replicated
- grad_hidden_gate: float32 [2048, 3456], P(None, 'tensor')
- grad_hidden_up: float32 [2048, 3456], P(None, 'tensor')
- grad_hidden_down: float32 [3456, 2048], P('tensor')
Inputs may be any that keep to these rules, and one draw needn't show every extreme that they name: `segments`: along each packed sequence the document numbers start at 0 and never fall; every document but the last of a sequence covers 1024 // 5 to 2048 positions.
All inputs are finite; a program needn't handle non-finite values.
Results may differ from a plain program's by a relative error of at most 0.019.
The roundings to bfloat16 on the way count: a program that leaves them out, or rounds other values in their place, can miss the bound.
Values may be sent and summed in bfloat16 or wider, within the bound.
A program may use at most 256 MiB of HBM per device.

v0:
```python
import jax
import jax.numpy as jnp
from jax import lax
from jax.sharding import PartitionSpec as P

KD = 256
VD = 432


EPS = 1e-05
GROUP_EPS = 0.1


def norm_parts(rows, gain, bias):
    centered = rows - jnp.mean(rows, axis=-1, keepdims=True)
    scale = lax.rsqrt(jnp.mean(centered * centered, axis=-1, keepdims=True) + EPS)
    normed = centered * scale
    return (normed * gain + bias, normed, scale)


def norm_back(grad_out, gain, normed, scale):
    shaped = grad_out * gain
    return scale * (
        shaped
        - jnp.mean(shaped, axis=-1, keepdims=True)
        - normed * jnp.mean(shaped * normed, axis=-1, keepdims=True)
    )


def decay_table(segments, rates):
    place = jnp.arange(segments.shape[-1], dtype=jnp.int32)
    offset = place[:, None] - place[None, :]
    same_doc = (segments[..., :, None] == segments[..., None, :]) & (offset >= 0)
    distance = jnp.maximum(offset, 0).astype(jnp.float32)
    decay = jnp.where(same_doc[..., None, :, :], jnp.exp(-rates[:, None, None] * distance), 0.0)
    return decay * lax.rsqrt(jnp.sum(decay, axis=-1, keepdims=True))


def normalize_scores(scores, table):
    weighted = scores * table
    total = jnp.sum(weighted, axis=-1, keepdims=True)
    return weighted * lax.rsqrt(total * total + 1.0)


def gated_norm(gates, retained):
    centered = retained - jnp.mean(retained, axis=-1, keepdims=True)
    normed = centered * lax.rsqrt(jnp.mean(centered * centered, axis=-1, keepdims=True) + GROUP_EPS)
    return jax.nn.silu(gates) * normed


def gelu_product(gate_in, lin_in):
    return jax.nn.gelu(gate_in) * lin_in


def product(left, right):
    return jnp.dot(left, right, preferred_element_type=jnp.float32)


def product_nt(left, right):
    return lax.dot_general(
        left, right, (((1,), (1,)), ((), ())), preferred_element_type=jnp.float32
    )


def product_tn(left, right):
    return lax.dot_general(
        left, right, (((0,), (0,)), ((), ())), preferred_element_type=jnp.float32
    )


def per_device(
    tokens,
    first_gain,
    first_bias,
    query_weight,
    key_weight,
    value_weight,
    gate_weight,
    out_weight,
    second_gain,
    second_bias,
    hidden_gate,
    hidden_up,
    hidden_down,
    segments,
    cotangent,
):
    seq_count, seq_len = segments.shape
    group_rows = seq_count * seq_len
    head_local = query_weight.shape[1] // KD
    scale_factor = KD ** (-0.5)
    inputs = tokens.astype(jnp.float32)
    first_out, first_normed, first_scale = norm_parts(inputs, first_gain, first_bias)
    first_all = lax.all_gather(first_out.astype(jnp.bfloat16), "tensor", axis=0, tiled=True)
    queries = product(first_all, query_weight).astype(jnp.bfloat16)
    keys_low = product(first_all, key_weight).astype(jnp.bfloat16)
    values = product(first_all, value_weight).astype(jnp.bfloat16)
    gates = product(first_all, gate_weight)
    head_index = (lax.axis_index("tensor") * head_local + jnp.arange(head_local)).astype(
        jnp.float32
    )
    rates = -jnp.log1p(-jnp.exp2(-5.0 - head_index))
    table = decay_table(segments, rates)
    query_heads = queries.reshape(seq_count, seq_len, head_local, KD)
    key_heads = keys_low.reshape(seq_count, seq_len, head_local, KD)
    value_heads = values.reshape(seq_count, seq_len, head_local, VD)
    scores = (
        jnp.einsum("bnhk,bmhk->bhnm", query_heads, key_heads, preferred_element_type=jnp.float32)
        * scale_factor
    )

    def score_step(raw):
        return normalize_scores(raw, table)

    retain_full, score_pull = jax.vjp(score_step, scores)
    retain = retain_full.astype(jnp.bfloat16)
    retained = jnp.einsum(
        "bhnm,bmhv->bnhv", retain, value_heads, preferred_element_type=jnp.float32
    )
    gate_heads = gates.reshape(seq_count, seq_len, head_local, VD)
    mixed_full, mix_pull = jax.vjp(gated_norm, gate_heads, retained)
    mixed = mixed_full.reshape(group_rows, head_local * VD).astype(jnp.bfloat16)
    middle = inputs + lax.psum_scatter(
        product(mixed, out_weight), "tensor", scatter_dimension=0, tiled=True
    )
    second_out, second_normed, second_scale = norm_parts(middle, second_gain, second_bias)
    second_all = lax.all_gather(second_out.astype(jnp.bfloat16), "tensor", axis=0, tiled=True)
    gate_in = product(second_all, hidden_gate)
    lin_in = product(second_all, hidden_up)
    inner_full, inner_pull = jax.vjp(gelu_product, gate_in, lin_in)
    inner = inner_full.astype(jnp.bfloat16)
    output = (
        middle
        + lax.psum_scatter(product(inner, hidden_down), "tensor", scatter_dimension=0, tiled=True)
    ).astype(jnp.bfloat16)
    seed_all = lax.all_gather(cotangent, "tensor", axis=0, tiled=True)
    grad_inner = product_nt(seed_all, hidden_down)
    grad_hdown = product_tn(inner, seed_all)
    grad_gate_in, grad_lin_in = inner_pull(grad_inner)
    gate_in_low = grad_gate_in.astype(jnp.bfloat16)
    lin_in_low = grad_lin_in.astype(jnp.bfloat16)
    grad_hgate = product_tn(second_all, gate_in_low)
    grad_hup = product_tn(second_all, lin_in_low)
    grad_second = lax.psum_scatter(
        product_nt(gate_in_low, hidden_gate) + product_nt(lin_in_low, hidden_up),
        "tensor",
        scatter_dimension=0,
        tiled=True,
    )
    grad_sgain = jnp.sum(grad_second * second_normed, axis=0)
    grad_sbias = jnp.sum(grad_second, axis=0)
    grad_middle = cotangent.astype(jnp.float32) + norm_back(
        grad_second, second_gain, second_normed, second_scale
    )
    branch_all = lax.all_gather(grad_middle.astype(jnp.bfloat16), "tensor", axis=0, tiled=True)
    grad_mixed = product_nt(branch_all, out_weight)
    grad_outw = product_tn(mixed, branch_all)
    grad_gates, grad_retained = mix_pull(grad_mixed.reshape(seq_count, seq_len, head_local, VD))
    gates_low = grad_gates.reshape(group_rows, head_local * VD).astype(jnp.bfloat16)
    retained_low = grad_retained.astype(jnp.bfloat16)
    grad_retain = jnp.einsum(
        "bnhv,bmhv->bhnm", retained_low, value_heads, preferred_element_type=jnp.float32
    )
    grad_values = jnp.einsum(
        "bhnm,bnhv->bmhv", retain, retained_low, preferred_element_type=jnp.float32
    )
    values_low = grad_values.reshape(group_rows, head_local * VD).astype(jnp.bfloat16)
    (grad_scores,) = score_pull(grad_retain)
    scores_low = grad_scores.astype(jnp.bfloat16)
    grad_queries = (
        jnp.einsum("bhnm,bmhk->bnhk", scores_low, key_heads, preferred_element_type=jnp.float32)
        * scale_factor
    )
    grad_keys = (
        jnp.einsum("bhnm,bnhk->bmhk", scores_low, query_heads, preferred_element_type=jnp.float32)
        * scale_factor
    )
    queries_low = grad_queries.reshape(group_rows, head_local * KD).astype(jnp.bfloat16)
    keys_back = grad_keys.reshape(group_rows, head_local * KD).astype(jnp.bfloat16)
    grad_queryw = product_tn(first_all, queries_low)
    grad_keyw = product_tn(first_all, keys_back)
    grad_valuew = product_tn(first_all, values_low)
    grad_gatew = product_tn(first_all, gates_low)
    total = product_nt(queries_low, query_weight)
    total = total + product_nt(keys_back, key_weight)
    total = total + product_nt(values_low, value_weight)
    grad_first = lax.psum_scatter(
        (total + product_nt(gates_low, gate_weight)).astype(jnp.bfloat16),
        "tensor",
        scatter_dimension=0,
        tiled=True,
    ).astype(jnp.float32)
    grad_fgain = jnp.sum(grad_first * first_normed, axis=0)
    grad_fbias = jnp.sum(grad_first, axis=0)
    grad_tokens = grad_middle + norm_back(grad_first, first_gain, first_normed, first_scale)
    grad_queryw, grad_keyw, grad_valuew, grad_gatew, grad_outw, grad_hgate, grad_hup, grad_hdown = (
        lax.psum(grad_queryw.astype(jnp.bfloat16), "dp").astype(jnp.float32),
        lax.psum(grad_keyw.astype(jnp.bfloat16), "dp").astype(jnp.float32),
        lax.psum(grad_valuew.astype(jnp.bfloat16), "dp").astype(jnp.float32),
        lax.psum(grad_gatew.astype(jnp.bfloat16), "dp").astype(jnp.float32),
        lax.psum(grad_outw.astype(jnp.bfloat16), "dp").astype(jnp.float32),
        lax.psum(grad_hgate.astype(jnp.bfloat16), "dp").astype(jnp.float32),
        lax.psum(grad_hup.astype(jnp.bfloat16), "dp").astype(jnp.float32),
        lax.psum(grad_hdown.astype(jnp.bfloat16), "dp").astype(jnp.float32),
    )
    grad_fgain, grad_fbias, grad_sgain, grad_sbias = lax.psum(
        (grad_fgain, grad_fbias, grad_sgain, grad_sbias), ("dp", "tensor")
    )
    return (
        output,
        grad_tokens,
        grad_fgain,
        grad_fbias,
        grad_queryw,
        grad_keyw,
        grad_valuew,
        grad_gatew,
        grad_outw,
        grad_sgain,
        grad_sbias,
        grad_hgate,
        grad_hup,
        grad_hdown,
    )


def solution(mesh):
    return jax.shard_map(
        per_device,
        mesh=mesh,
        in_specs=(
            P(("dp", "tensor"), None),
            P(),
            P(),
            P(None, "tensor"),
            P(None, "tensor"),
            P(None, "tensor"),
            P(None, "tensor"),
            P("tensor", None),
            P(),
            P(),
            P(None, "tensor"),
            P(None, "tensor"),
            P("tensor", None),
            P("dp", None),
            P(("dp", "tensor"), None),
        ),
        out_specs=(
            P(("dp", "tensor"), None),
            P(("dp", "tensor"), None),
            P(),
            P(),
            P(None, "tensor"),
            P(None, "tensor"),
            P(None, "tensor"),
            P(None, "tensor"),
            P("tensor", None),
            P(),
            P(),
            P(None, "tensor"),
            P(None, "tensor"),
            P("tensor", None),
        ),
        check_vma=False,
    )
```

profile of v0, /device:TPU:0, one launch (start us, length us, event | category | flops | bytes accessed | tf_op | source)
XLA Modules:
  0.0 1342.4 jit_solution(5603979112980502329)
XLA Ops:
  31.4 66.0 %all-gather.5.cloned.1.call-done = bf16[1024,2048]{1,0:T(8,128)(2,1)} async-done(((bf16[256,2048]{1,0:T(8,128)(2,1)}), bf16[1024,2048]{1,0:T(8,128)(2,1)}) %all-gather.5.cloned.1.call-update) | async-done | bytes 4194320 | tf_op jit(solution)/shard_map/all_gather | solution.py:94
  127.6 6.8 fusion.41
  134.7 142.9 %reduce-scatter.5.cloned.1.call-done = f32[256,2048]{1,0:T(8,128)} async-done(((f32[1024,2048]{1,0:T(8,128)}), f32[256,2048]{1,0:T(8,128)}) %reduce-scatter.5.cloned.1.call-update) | async-done | bytes 2097168 | tf_op jit(solution)/shard_map/reduce_scatter | solution.py:123
  283.7 81.0 %all-gather.7.cloned.1.call-done = bf16[1024,2048]{1,0:T(8,128)(2,1)} async-done(((bf16[256,2048]{1,0:T(8,128)(2,1)}), bf16[1024,2048]{1,0:T(8,128)(2,1)}) %all-gather.7.cloned.1.call-update) | async-done | bytes 4194320 | tf_op jit(solution)/shard_map/all_gather | solution.py:127
  364.7 9.1 fusion.42
  373.8 5.7 fusion.43
  379.5 66.0 %all-gather.9.cloned.1.call-done = bf16[1024,2048]{1,0:T(8,128)(2,1)} async-done(((bf16[256,2048]{1,0:T(8,128)(2,1)}), bf16[1024,2048]{1,0:T(8,128)(2,1)}) %all-gather.9.cloned.1.call-update) | async-done | bytes 4194320 | tf_op jit(solution)/shard_map/all_gather | solution.py:136
  445.5 10.9 multiply_convert_fusion.2
  461.1 7.1 convolution_add_fusion
  468.3 8.2 fusion.44
  477.1 134.3 %reduce-scatter.9.cloned.1.call-done = f32[256,2048]{1,0:T(8,128)} async-done(((f32[1024,2048]{1,0:T(8,128)}), f32[256,2048]{1,0:T(8,128)}) %reduce-scatter.9.cloned.1.call-update) | async-done | bytes 2097168 | tf_op jit(solution)/shard_map/reduce_scatter | solution.py:144
  614.5 144.3 %reduce-scatter.7.cloned.1.call-done = f32[256,2048]{1,0:T(8,128)} async-done(((f32[1024,2048]{1,0:T(8,128)}), f32[256,2048]{1,0:T(8,128)}) %reduce-scatter.7.cloned.1.call-update) | async-done | bytes 2097168 | tf_op jit(solution)/shard_map/reduce_scatter | solution.py:134
  764.2 81.6 %all-gather.11.cloned.1.call-done = bf16[1024,2048]{1,0:T(8,128)(2,1)} async-done(((bf16[256,2048]{1,0:T(8,128)(2,1)}), bf16[1024,2048]{1,0:T(8,128)(2,1)}) %all-gather.11.cloned.1.call-update) | async-done | bytes 4194320 | tf_op jit(solution)/shard_map/all_gather | solution.py:155
  845.8 6.8 fusion.46
  859.0 6.0 multiply_reduce_fusion
  874.1 6.8 fusion.49
  880.9 6.8 fusion.48
  887.6 5.7 fusion.47
  893.3 12.7 add_convert_fusion
  907.5 7.8 convolution_convert_fusion.1
  938.5 5.5 convolution_convert_fusion.2
  949.2 32.2 %reduce-scatter.11.cloned.1.call-done = bf16[256,2048]{1,0:T(8,128)(2,1)} async-done(((bf16[1024,2048]{1,0:T(8,128)(2,1)}), bf16[256,2048]{1,0:T(8,128)(2,1)}) %reduce-scatter.11.cloned.1.call-update) | async-done | bytes 1048592 | tf_op jit(solution)/shard_map/reduce_scatter | solution.py:187
  983.8 42.3 %all-reduce = (f32[2048]{0:T(1024)}, f32[2048]{0:T(1024)}, f32[2048]{0:T(1024)}, f32[2048]{0:T(1024)}) all-reduce(f32[2048]{0:T(1024)S(1)} %get-tuple-element.17, f32[2048]{0:T(1024)S(1)} %get-tuple-element.21, f32[2048]{0:T(1024)S(1)} %copy-done.42, f32[2048]{0:T(1024)S(1)} %copy-done.43), channel_id=1, replica_groups=mesh['dp'=8,'tensor'=4] {'dp','tensor'}, use_global_device_ids=true, to_apply=%region_20.21 | all-reduce | flops 8192 | bytes 65536 | tf_op jit(solution)/shard_map/psum | solution.py:206
  1029.4 275.3 %all-reduce.4.cloned.1.call-done = (bf16[2048,512]{1,0:T(8,128)(2,1)}, bf16[2048,512]{1,0:T(8,128)(2,1)}, bf16[2048,864]{0,1:T(8,128)(2,1)}, bf16[2048,864]{0,1:...) async-done(((bf16[2048,512]{1,0:T(8,128)(2,1)}, bf16[2048,512]{1,0:T(8,128)(2,1)}, ...) | async-done | bytes 25427984 | tf_op jit(solution)/shard_map/psum | solution.py:197
  (250 shorter events, 155.4 us)
Async XLA Ops:
  7.2 438.3 %copy-start = (bf16[864,2048]{1,0:T(8,128)(2,1)S(1)}, bf16[864,2048]{1,0:T(8,128)(2,1)}, u32[]{:S(2)}) copy-start(bf16[864,2048]{1,0:T(8,128)(2,1)} %param.27) | copy-start | bytes 10616836
  7.2 90.2 %all-gather.5.cloned.1.call-start = ((), (), s32[]{:S(2)}) async-start(), calls=%async_computation.4 | async-start | bytes 5242880 | tf_op jit(solution)/shard_map/all_gather | solution.py:94
  13.8 263.8 %reduce-scatter.5.cloned.1.call-start = ((), (), s32[]{:S(2)}) async-start(), calls=%async_computation.5 | async-start | bytes 10485760 | tf_op jit(solution)/shard_map/reduce_scatter | solution.py:123
  27.2 78.1 %copy-start.56 = (f32[2]{0:T(128)}, f32[2]{0:T(128)S(1)}, u32[]{:S(2)}) copy-start(f32[2]{0:T(128)S(1)} %negate_log-plus-one_fusion) | copy-start | bytes 28
  31.4 73.9 %copy-start.40 = (f32[2,1024]{1,0:T(2,128)}, f32[2,1024]{1,0:T(2,128)S(1)}, u32[]{:S(2)}) copy-start(f32[2,1024]{1,0:T(2,128)S(1)} %rsqrt.47) | copy-start | bytes 24580
  134.4 230.3 %all-gather.7.cloned.1.call-start = ((), (), s32[]{:S(2)}) async-start(), calls=%async_computation.6 | async-start | bytes 5242880 | tf_op jit(solution)/shard_map/all_gather | solution.py:127
  283.1 162.4 %all-gather.9.cloned.1.call-start = ((), (), s32[]{:S(2)}) async-start(), calls=%async_computation.8 | async-start | bytes 5242880 | tf_op jit(solution)/shard_map/all_gather | solution.py:136
  283.7 327.7 %reduce-scatter.9.cloned.1.call-start = ((), (), s32[]{:S(2)}) async-start(), calls=%async_computation.9 | async-start | bytes 10485760 | tf_op jit(solution)/shard_map/reduce_scatter | solution.py:144
  468.3 290.6 %reduce-scatter.7.cloned.1.call-start = ((), (), s32[]{:S(2)}) async-start(), calls=%async_computation.7 | async-start | bytes 10485760 | tf_op jit(solution)/shard_map/reduce_scatter | solution.py:134
  476.6 134.9 %copy-start.6 = (f32[256,2048]{1,0:T(8,128)S(1)}, f32[256,2048]{1,0:T(8,128)}, u32[]{:S(2)}) copy-start(f32[256,2048]{1,0:T(8,128)} %copy-done.5) | copy-start | bytes 6291460
  476.6 134.9 %copy-start.34 = (f32[2048]{0:T(1024)S(1)}, f32[2048]{0:T(1024)}, u32[]{:S(2)}) copy-start(f32[2048]{0:T(1024)} %param.23) | copy-start | bytes 24580
  476.6 134.9 %copy-start.47 = (f32[256]{0:T(256)S(1)}, f32[256]{0:T(256)}, u32[]{:S(2)}) copy-start(f32[256]{0:T(256)} %copy-done.46) | copy-start | bytes 3076
  476.6 134.9 %copy-start.52 = (f32[256]{0:T(256)S(1)}, f32[256]{0:T(256)}, u32[]{:S(2)}) copy-start(f32[256]{0:T(256)} %copy-done.51) | copy-start | bytes 3076
  476.6 282.3 %copy-start.17 = (bf16[256,2048]{1,0:T(8,128)(2,1)S(1)}, bf16[256,2048]{1,0:T(8,128)(2,1)}, u32[]{:S(2)}) copy-start(bf16[256,2048]{1,0:T(8,128)(2,1)} %param.29) | copy-start | bytes 3145732
  476.6 369.2 %all-gather.11.cloned.1.call-start = ((), (), s32[]{:S(2)}) async-start(), calls=%async_computation.10 | async-start | bytes 5242880 | tf_op jit(solution)/shard_map/all_gather | solution.py:155
  764.2 88.5 %copy-start.3 = (f32[2,432,1024]{2,1,0:T(8,128)S(1)}, f32[2,432,1024]{2,1,0:T(8,128)}, u32[]{:S(2)}) copy-start(f32[2,432,1024]{2,1,0:T(8,128)} %copy-done.2) | copy-start | bytes 10616836
  764.2 217.3 %reduce-scatter.11.cloned.1.call-start = ((), (), s32[]{:S(2)}) async-start(), calls=%async_computation.11 | async-start | bytes 5242880 | tf_op jit(solution)/shard_map/reduce_scatter | solution.py:187
  906.0 398.7 %all-reduce.4.cloned.1.call-start = ((), (), s32[]{:S(2)}) async-start(), calls=%async_computation.12 | async-start | bytes 50855936 | tf_op jit(solution)/shard_map/psum | solution.py:197
  949.2 32.3 %copy-start.35 = (f32[2048]{0:T(1024)S(1)}, f32[2048]{0:T(1024)}, u32[]{:S(2)}) copy-start(f32[2048]{0:T(1024)} %param.16) | copy-start | bytes 24580
  949.2 32.3 %copy-start.49 = (f32[256]{0:T(256)S(1)}, f32[256]{0:T(256)}, u32[]{:S(2)}) copy-start(f32[256]{0:T(256)} %copy-done.48) | copy-start | bytes 3076
  949.2 32.3 %copy-start.54 = (f32[256]{0:T(256)S(1)}, f32[256]{0:T(256)}, u32[]{:S(2)}) copy-start(f32[256]{0:T(256)} %copy-done.53) | copy-start | bytes 3076
  949.2 34.6 %copy-start.42 = (f32[2048]{0:T(1024)S(1)}, f32[2048]{0:T(1024)}, u32[]{:S(2)}) copy-start(f32[2048]{0:T(1024)} %get-tuple-element.14) | copy-start | bytes 24580
  949.2 34.6 %copy-start.43 = (f32[2048]{0:T(1024)S(1)}, f32[2048]{0:T(1024)}, u32[]{:S(2)}) copy-start(f32[2048]{0:T(1024)} %get-tuple-element.19) | copy-start | bytes 24580
  949.2 76.9 %copy-start.14 = (f32[256,2048]{1,0:T(8,128)S(1)}, f32[256,2048]{1,0:T(8,128)}, u32[]{:S(2)}) copy-start(f32[256,2048]{1,0:T(8,128)} %get-tuple-element.37) | copy-start | bytes 6291460
  (71 other events, 375.0 us)
Sparse Core Ops, SparseCore 0:
  13.9 83.4 all-gather.4
  134.6 142.9 reduce-scatter.4
  283.2 81.4 all-gather.6
  366.2 79.2 all-gather.8
  468.4 142.9 reduce-scatter.8
  613.6 145.1 reduce-scatter.6
  764.3 81.4 all-gather.10
  906.2 75.2 reduce-scatter.10
  988.4 316.3 all-reduce.3
where the time goes:
time: 1350 us; the launch traced here: 1340 us
  waiting for transfers between devices  1020 us (76%)
  matrix products  166 us (12%)
  other arithmetic  73.2 us (5%)
  blocking collectives  42.3 us (3%)
  local copies, waits for them, and re-layouts  20.5 us (2%)
  between operations  15.1 us (1%)
    psum x1, waiting for transfers between devices, per_device(): lax.psum(grad_queryw.astype(jnp.bfloat16), 'dp').astype(jnp.float32)  275 us
    reduce_scatter x1, waiting for transfers between devices, per_device(): lax.psum_scatter(product(inner, hidden_down), 'tensor', scatter_dimension...  144 us
    reduce_scatter x1, waiting for transfers between devices, per_device(): lax.psum_scatter(product(mixed, out_weight), 'tensor', scatter_dimension=...  143 us
    reduce_scatter x1, waiting for transfers between devices, per_device(): lax.psum_scatter(product_nt(gate_in_low, hidden_gate) + product_nt(lin_in...  134 us
    all_gather x1, waiting for transfers between devices, per_device(): lax.all_gather(grad_middle.astype(jnp.bfloat16), 'tensor', axis=0, tiled=...  81.6 us
    all_gather x1, waiting for transfers between devices, per_device(): lax.all_gather(second_out.astype(jnp.bfloat16), 'tensor', axis=0, tiled=T...  81 us
    all_gather x1, waiting for transfers between devices, per_device(): lax.all_gather(first_out.astype(jnp.bfloat16), 'tensor', axis=0, tiled=True)  66 us
    all_gather x1, waiting for transfers between devices, per_device(): seed_all = lax.all_gather(cotangent, 'tensor', axis=0, tiled=True)  66 us
  transfers between devices with their start and end apart: 9, of which 9 were waited for; matrix products, arithmetic and copies ran while one was open for 7% of the time, Pallas kernels for 0%

commit v1 on v0

--- a/solution.py
+++ b/solution.py
@@ -66,6 +66,20 @@
     return lax.dot_general(
         left, right, (((0,), (0,)), ((), ())), preferred_element_type=jnp.float32
     )
+
+
+def scatter_rows(partial):
+    summed = lax.psum_scatter(
+        partial.astype(jnp.bfloat16), "tensor", scatter_dimension=0, tiled=True
+    )
+    return summed.astype(jnp.float32)
+
+
+def sum_dp(after, *grads):
+    lows = tuple(grad.astype(jnp.bfloat16) for grad in grads)
+    if after:
+        lows = lax.optimization_barrier(tuple(after) + lows)[len(after) :]
+    return lax.psum(lows, "dp")
 
 
 def per_device(
@@ -90,6 +104,7 @@
     head_local = query_weight.shape[1] // KD
     scale_factor = KD ** (-0.5)
     inputs = tokens.astype(jnp.float32)
+    seed_all = lax.all_gather(cotangent, "tensor", axis=0, tiled=True)
     first_out, first_normed, first_scale = norm_parts(inputs, first_gain, first_bias)
     first_all = lax.all_gather(first_out.astype(jnp.bfloat16), "tensor", axis=0, tiled=True)
     queries = product(first_all, query_weight).astype(jnp.bfloat16)
@@ -120,9 +135,7 @@
     gate_heads = gates.reshape(seq_count, seq_len, head_local, VD)
     mixed_full, mix_pull = jax.vjp(gated_norm, gate_heads, retained)
     mixed = mixed_full.reshape(group_rows, head_local * VD).astype(jnp.bfloat16)
-    middle = inputs + lax.psum_scatter(
-        product(mixed, out_weight), "tensor", scatter_dimension=0, tiled=True
-    )
+    middle = inputs + scatter_rows(product(mixed, out_weight))
     second_out, second_normed, second_scale = norm_parts(middle, second_gain, second_bias)
     second_all = lax.all_gather(second_out.astype(jnp.bfloat16), "tensor", axis=0, tiled=True)
     gate_in = product(second_all, hidden_gate)
@@ -131,9 +144,8 @@
     inner = inner_full.astype(jnp.bfloat16)
     output = (
         middle
-        + lax.psum_scatter(product(inner, hidden_down), "tensor", scatter_dimension=0, tiled=True)
+        + scatter_rows(product(inner, hidden_down))
     ).astype(jnp.bfloat16)
-    seed_all = lax.all_gather(cotangent, "tensor", axis=0, tiled=True)
     grad_inner = product_nt(seed_all, hidden_down)
     grad_hdown = product_tn(inner, seed_all)
     grad_gate_in, grad_lin_in = inner_pull(grad_inner)
@@ -141,12 +153,8 @@
     lin_in_low = grad_lin_in.astype(jnp.bfloat16)
     grad_hgate = product_tn(second_all, gate_in_low)
     grad_hup = product_tn(second_all, lin_in_low)
-    grad_second = lax.psum_scatter(
-        product_nt(gate_in_low, hidden_gate) + product_nt(lin_in_low, hidden_up),
-        "tensor",
-        scatter_dimension=0,
-        tiled=True,
-    )
+    grad_second = scatter_rows(product_nt(gate_in_low, hidden_gate) + product_nt(lin_in_low, hidden_up))
+    grad_hdown, grad_hgate, grad_hup = sum_dp((), grad_hdown, grad_hgate, grad_hup)
     grad_sgain = jnp.sum(grad_second * second_normed, axis=0)
     grad_sbias = jnp.sum(grad_second, axis=0)
     grad_middle = cotangent.astype(jnp.float32) + norm_back(
@@ -155,6 +163,7 @@
     branch_all = lax.all_gather(grad_middle.astype(jnp.bfloat16), "tensor", axis=0, tiled=True)
     grad_mixed = product_nt(branch_all, out_weight)
     grad_outw = product_tn(mixed, branch_all)
+    (grad_outw,) = sum_dp((grad_hdown, grad_hgate, grad_hup), grad_outw)
     grad_gates, grad_retained = mix_pull(grad_mixed.reshape(seq_count, seq_len, head_local, VD))
     gates_low = grad_gates.reshape(group_rows, head_local * VD).astype(jnp.bfloat16)
     retained_low = grad_retained.astype(jnp.bfloat16)
@@ -184,24 +193,25 @@
     total = product_nt(queries_low, query_weight)
     total = total + product_nt(keys_back, key_weight)
     total = total + product_nt(values_low, value_weight)
-    grad_first = lax.psum_scatter(
-        (total + product_nt(gates_low, gate_weight)).astype(jnp.bfloat16),
-        "tensor",
-        scatter_dimension=0,
-        tiled=True,
-    ).astype(jnp.float32)
+    grad_first = scatter_rows(total + product_nt(gates_low, gate_weight))
     grad_fgain = jnp.sum(grad_first * first_normed, axis=0)
     grad_fbias = jnp.sum(grad_first, axis=0)
     grad_tokens = grad_middle + norm_back(grad_first, first_gain, first_normed, first_scale)
+    grad_valuew, grad_gatew, grad_queryw, grad_keyw = sum_dp(
+        (grad_outw,), grad_valuew, grad_gatew, grad_queryw, grad_keyw
+    )
     grad_queryw, grad_keyw, grad_valuew, grad_gatew, grad_outw, grad_hgate, grad_hup, grad_hdown = (
-        lax.psum(grad_queryw.astype(jnp.bfloat16), "dp").astype(jnp.float32),
-        lax.psum(grad_keyw.astype(jnp.bfloat16), "dp").astype(jnp.float32),
-        lax.psum(grad_valuew.astype(jnp.bfloat16), "dp").astype(jnp.float32),
-        lax.psum(grad_gatew.astype(jnp.bfloat16), "dp").astype(jnp.float32),
-        lax.psum(grad_outw.astype(jnp.bfloat16), "dp").astype(jnp.float32),
-        lax.psum(grad_hgate.astype(jnp.bfloat16), "dp").astype(jnp.float32),
-        lax.psum(grad_hup.astype(jnp.bfloat16), "dp").astype(jnp.float32),
-        lax.psum(grad_hdown.astype(jnp.bfloat16), "dp").astype(jnp.float32),
+        item.astype(jnp.float32)
+        for item in (
+            grad_queryw,
+            grad_keyw,
+            grad_valuew,
+            grad_gatew,
+            grad_outw,
+            grad_hgate,
+            grad_hup,
+            grad_hdown,
+        )
     )
     grad_fgain, grad_fbias, grad_sgain, grad_sbias = lax.psum(
         (grad_fgain, grad_fbias, grad_sgain, grad_sbias), ("dp", "tensor")

time: 1350 us -> 1140 us (0.84)
  waiting for transfers between devices: 1020 us -> 793 us
    reduce_scatter x4, waiting for transfers between devices: 454 us -> 242 us  [scatter_rows(): lax.psum_scatter(partial.astype(jnp.bfloat16), 'tensor', scatter_dimensio...]
    all_gather x1, waiting for transfers between devices: 81.6 us -> 61.9 us  [per_device(): lax.all_gather(grad_middle.astype(jnp.bfloat16), 'tensor', axis=0, tiled=...]
    psum x1 -> x3, waiting for transfers between devices: 275 us -> 275 us  [sum_dp(): return lax.psum(lows, 'dp')]
  transfers between devices with their start and end apart: 9 -> 11, of which waited for: 9 -> 11; matrix products, arithmetic and copies ran while one was open for 7% -> 17% of each run, Pallas kernels for 0% -> 0%
where the time goes in v1:
time: 1140 us; the launch traced here: 1130 us
  waiting for transfers between devices  793 us (70%)
  matrix products  176 us (15%)
  other arithmetic  82.3 us (7%)
  blocking collectives  46.9 us (4%)
  local copies, waits for them, and re-layouts  19.4 us (2%)
  between operations  15.1 us (1%)
    psum x3, waiting for transfers between devices, sum_dp(): return lax.psum(lows, 'dp')  275 us
    reduce_scatter x4, waiting for transfers between devices, scatter_rows(): lax.psum_scatter(partial.astype(jnp.bfloat16), 'tensor', scatter_dimensio...  242 us
    all_gather x1, waiting for transfers between devices, per_device(): lax.all_gather(second_out.astype(jnp.bfloat16), 'tensor', axis=0, tiled=T...  80.8 us
    all_gather x1, waiting for transfers between devices, per_device(): seed_all = lax.all_gather(cotangent, 'tensor', axis=0, tiled=True)  66.1 us
    all_gather x1, waiting for transfers between devices, per_device(): lax.all_gather(first_out.astype(jnp.bfloat16), 'tensor', axis=0, tiled=True)  66 us
    dot_general x8, matrix products, product_nt(): lax.dot_general(left, right, (((1,), (1,)), ((), ())), preferred_element_...  63.3 us
    all_gather x1, waiting for transfers between devices, per_device(): lax.all_gather(grad_middle.astype(jnp.bfloat16), 'tensor', axis=0, tiled=...  61.9 us
    dot_general x8, matrix products, product_tn(): lax.dot_general(left, right, (((0,), (0,)), ((), ())), preferred_element_...  47.5 us
  transfers between devices with their start and end apart: 11, of which 11 were waited for; matrix products, arithmetic and copies ran while one was open for 17% of the time, Pallas kernels for 0%

profile of v1, /device:TPU:0, one launch (start us, length us, event | category | flops | bytes accessed | tf_op | source)
XLA Modules:
  0.0 1133.9 jit_solution(6501126093345124998)
XLA Ops:
  31.4 66.0 %all-gather.5.cloned.1.call-done = bf16[1024,2048]{1,0:T(8,128)(2,1)} async-done(((bf16[256,2048]{1,0:T(8,128)(2,1)}), bf16[1024,2048]{1,0:T(8,128)(2,1)}) %all-gather.5.cloned.1.call-update) | async-done | bytes 4194320 | tf_op jit(solution)/shard_map/all_gather | solution.py:109
  134.0 75.0 %reduce-scatter.5.cloned.1.call-done = bf16[256,2048]{1,0:T(8,128)(2,1)} async-done(((bf16[1024,2048]{1,0:T(8,128)(2,1)}), bf16[256,2048]{1,0:T(8,128)(2,1)}) %reduce-scatter.5.cloned.1.call-update) | async-done | bytes 1048592 | tf_op jit(solution)/shard_map/reduce_scatter | solution.py:72
  215.9 80.8 %all-gather.7.cloned.1.call-done = bf16[1024,2048]{1,0:T(8,128)(2,1)} async-done(((bf16[256,2048]{1,0:T(8,128)(2,1)}), bf16[1024,2048]{1,0:T(8,128)(2,1)}) %all-gather.7.cloned.1.call-update) | async-done | bytes 4194320 | tf_op jit(solution)/shard_map/all_gather | solution.py:140
  296.7 9.1 fusion.49
  311.5 66.1 %all-gather.9.cloned.1.call-done = bf16[1024,2048]{1,0:T(8,128)(2,1)} async-done(((bf16[256,2048]{1,0:T(8,128)(2,1)}), bf16[1024,2048]{1,0:T(8,128)(2,1)}) %all-gather.9.cloned.1.call-update) | async-done | bytes 4194320 | tf_op jit(solution)/shard_map/all_gather | solution.py:107
  377.6 10.9 multiply_convert_fusion.2
  393.2 6.4 add_convert_fusion.1
  399.6 75.4 %reduce-scatter.9.cloned.1.call-done = bf16[256,2048]{1,0:T(8,128)(2,1)} async-done(((bf16[1024,2048]{1,0:T(8,128)(2,1)}), bf16[256,2048]{1,0:T(8,128)(2,1)}) %reduce-scatter.9.cloned.1.call-update) | async-done | bytes 1048592 | tf_op jit(solution)/shard_map/reduce_scatter | solution.py:72
  483.3 8.5 convolution_convert_fusion.5
  502.3 61.9 %all-gather.11.cloned.1.call-done = bf16[1024,2048]{1,0:T(8,128)(2,1)} async-done(((bf16[256,2048]{1,0:T(8,128)(2,1)}), bf16[1024,2048]{1,0:T(8,128)(2,1)}) %all-gather.11.cloned.1.call-update) | async-done | bytes 4194320 | tf_op jit(solution)/shard_map/all_gather | solution.py:163
  564.2 6.9 fusion.52
  597.1 7.8 convolution_convert_fusion.6
  605.0 114.5 %all-reduce.11.cloned.1.call-done = (bf16[864,2048]{1,0:T(8,128)(2,1)}, bf16[2048,864]{0,1:T(8,128)(2,1)}, bf16[2048,864]{0,1:T(8,128)(2,1)}) async-done(((bf16[864,2048]{1,0:T(8,128)(2,1)}, bf16[2048,864]{0,1:T(8,128)(2,1)}, bf16[2048,864]{0,1:T(8,128)(2,1)}), (bf16[864,2048]{1,0:T(8,128)(2,1)}, bf16[2048,864]{0,1:T(8,128)(2,1)}, bf16[2048,864]{0,1:T(8,128)(2,1)})) %all-reduce.11.cloned.1.call-update) | async-done | bytes 10616848 | tf_op jit(solution)/shard_map/psum | solution.py:82
  719.5 6.4 convolution_convert_fusion.9
  740.3 57.3 %all-reduce.7.cloned.1.call-done = bf16[864,2048]{1,0:T(8,128)(2,1)} async-done(((bf16[864,2048]{1,0:T(8,128)(2,1)}), bf16[864,2048]{1,0:T(8,128)(2,1)}) %all-reduce.7.cloned.1.call-update) | async-done | bytes 3538960 | tf_op jit(solution)/shard_map/psum | solution.py:82
  797.7 7.7 fusion.53
  805.4 6.8 fusion.55
  812.2 6.8 fusion.54
  819.0 13.3 %add_convert_fusion = bf16[1024,2048]{1,0:T(8,128)(2,1)} fusion(f32[1024,2048]{1,0:T(8,128)} %fusion.55, f32[1024,2048]{1,0:T(8,128)} %fusion.54, f32[1024,2048]{1,0:T(8,128)} %fusion.53, bf16[1024,512]{0,1:T(8,128)(2,1)S(1)} %bitcast.117, bf16[2048,512]{1,0:T(8,128)(2,1)S(1)} %copy-done.23), kind=kOutput, calls=%fused_computation | convolution fusion | flops 2155872256 | bytes 32505856 | tf_op jit(solution)/shard_map/dot_general | solution.py:60
  832.4 8.2 convolution_convert_fusion
  858.2 103.7 %all-reduce.9.cloned.1.call-done = (bf16[2048,512]{1,0:T(8,128)(2,1)}, bf16[2048,512]{1,0:T(8,128)(2,1)}, bf16[2048,864]{0,1:T(8,128)(2,1)}, bf16[2048,864]{0,1:T(8,128)(2,1)}) async-done(((bf16[2048,512]{1,0:T(8,128)(2,1)}, bf16[2048,512]{1,0:T(8,128)(2,1)}, bf16[2048,864]{0,1:T(8,128)(2,1)}, bf16[2048,864]{0,1:T(8,128)(2,1)}), (bf16[2048,512]{1,0:T(8,128)(2,1)}, bf16[2048,512]{1,0:T(8,128)(2,1)}, ...) | async-done | bytes 11272208 | tf_op jit(solution)/shard_map/psum | solution.py:82
  977.3 63.7 %reduce-scatter.11.cloned.1.call-done = bf16[256,2048]{1,0:T(8,128)(2,1)} async-done(((bf16[1024,2048]{1,0:T(8,128)(2,1)}), bf16[256,2048]{1,0:T(8,128)(2,1)}) %reduce-scatter.11.cloned.1.call-update) | async-done | bytes 1048592 | tf_op jit(solution)/shard_map/reduce_scatter | solution.py:72
  1044.2 46.9 %all-reduce = (f32[2048]{0:T(1024)}, f32[2048]{0:T(1024)}, f32[2048]{0:T(1024)}, f32[2048]{0:T(1024)}) all-reduce(f32[2048]{0:T(1024)} %get-tuple-element.26, f32[2048]{0:T(1024)} %get-tuple-element.31, f32[2048]{0:T(1024)} %get-tuple-element.24, f32[2048]{0:T(1024)} %get-tuple-element.30), channel_id=1, replica_groups=mesh['dp'=8,'tensor'=4] {'dp','tensor'}, use_global_device_ids=true, to_apply=%region_20.21 | all-reduce | flops 8192 | bytes 65536 | tf_op jit(solution)/shard_map/psum | solution.py:216
  1093.6 28.1 %reduce-scatter.7.cloned.1.call-done = bf16[256,2048]{1,0:T(8,128)(2,1)} async-done(((bf16[1024,2048]{1,0:T(8,128)(2,1)}), bf16[256,2048]{1,0:T(8,128)(2,1)}) %reduce-scatter.7.cloned.1.call-update) | async-done | bytes 1048592 | tf_op jit(solution)/shard_map/reduce_scatter | solution.py:72
  (238 shorter events, 180.8 us)
Async XLA Ops:
  7.2 370.4 %copy-start = (bf16[864,2048]{1,0:T(8,128)(2,1)S(1)}, bf16[864,2048]{1,0:T(8,128)(2,1)}, u32[]{:S(2)}) copy-start(bf16[864,2048]{1,0:T(8,128)(2,1)} %param.27) | copy-start | bytes 10616836
  7.2 90.2 %all-gather.5.cloned.1.call-start = ((), (), s32[]{:S(2)}) async-start(), calls=%async_computation.4 | async-start | bytes 5242880 | tf_op jit(solution)/shard_map/all_gather | solution.py:109
  13.8 195.2 %reduce-scatter.5.cloned.1.call-start = ((), (), s32[]{:S(2)}) async-start(), calls=%async_computation.5 | async-start | bytes 5242880 | tf_op jit(solution)/shard_map/reduce_scatter | solution.py:72
  27.2 78.1 %copy-start.52 = (f32[2]{0:T(128)}, f32[2]{0:T(128)S(1)}, u32[]{:S(2)}) copy-start(f32[2]{0:T(128)S(1)} %negate_log-plus-one_fusion) | copy-start | bytes 28
  31.3 74.0 %copy-start.41 = (f32[2,1024]{1,0:T(2,128)}, f32[2,1024]{1,0:T(2,128)S(1)}, u32[]{:S(2)}) copy-start(f32[2,1024]{1,0:T(2,128)S(1)} %rsqrt.47) | copy-start | bytes 24580
  116.3 7.2 copy-start.3
  133.6 163.2 %all-gather.7.cloned.1.call-start = ((), (), s32[]{:S(2)}) async-start(), calls=%async_computation.6 | async-start | bytes 5242880 | tf_op jit(solution)/shard_map/all_gather | solution.py:140
  215.3 162.3 %all-gather.9.cloned.1.call-start = ((), (), s32[]{:S(2)}) async-start(), calls=%async_computation.8 | async-start | bytes 5242880 | tf_op jit(solution)/shard_map/all_gather | solution.py:107
  215.9 259.2 %reduce-scatter.9.cloned.1.call-start = ((), (), s32[]{:S(2)}) async-start(), calls=%async_computation.9 | async-start | bytes 5242880 | tf_op jit(solution)/shard_map/reduce_scatter | solution.py:72
  296.7 9.1 copy-start.56
  296.7 9.1 copy-start.60
  377.6 10.9 copy-start.59
  399.6 164.6 %all-gather.11.cloned.1.call-start = ((), (), s32[]{:S(2)}) async-start(), calls=%async_computation.10 | async-start | bytes 5242880 | tf_op jit(solution)/shard_map/all_gather | solution.py:163
  482.8 236.6 %all-reduce.11.cloned.1.call-start = ((), (), s32[]{:S(2)}) async-start(), calls=%async_computation.14 | async-start | bytes 21233664 | tf_op jit(solution)/shard_map/psum | solution.py:82
  483.3 8.5 copy-start.57
  483.3 8.5 copy-start.73
  502.3 295.4 %all-reduce.7.cloned.1.call-start = ((), (), s32[]{:S(2)}) async-start(), calls=%async_computation.12 | async-start | bytes 7077888 | tf_op jit(solution)/shard_map/psum | solution.py:82
  719.5 242.5 %all-reduce.9.cloned.1.call-start = ((), (), s32[]{:S(2)}) async-start(), calls=%async_computation.13 | async-start | bytes 22544384 | tf_op jit(solution)/shard_map/psum | solution.py:82
  797.6 243.3 %reduce-scatter.11.cloned.1.call-start = ((), (), s32[]{:S(2)}) async-start(), calls=%async_computation.11 | async-start | bytes 5242880 | tf_op jit(solution)/shard_map/reduce_scatter | solution.py:72
  797.7 7.7 copy-start.28
  797.7 7.7 copy-start.64
  832.3 289.4 %reduce-scatter.7.cloned.1.call-start = ((), (), s32[]{:S(2)}) async-start(), calls=%async_computation.7 | async-start | bytes 5242880 | tf_op jit(solution)/shard_map/reduce_scatter | solution.py:72
  973.4 67.5 %copy-start.37 = (f32[2048]{0:T(1024)S(1)}, f32[2048]{0:T(1024)}, u32[]{:S(2)}) copy-start(f32[2048]{0:T(1024)} %param.16) | copy-start | bytes 24580
  973.4 148.3 %copy-start.34 = (f32[2048]{0:T(1024)S(1)}, f32[2048]{0:T(1024)}, u32[]{:S(2)}) copy-start(f32[2048]{0:T(1024)} %param.23) | copy-start | bytes 24580
  (64 other events, 266.4 us)
Sparse Core Ops, SparseCore 0:
  13.9 83.4 all-gather.4
  133.7 75.2 reduce-scatter.4
  215.4 81.2 all-gather.6
  298.2 79.2 all-gather.8
  399.7 75.2 reduce-scatter.8
  482.9 81.2 all-gather.10
  569.3 150.0 all-reduce.10
  723.7 73.8 all-reduce.6
  802.8 159.0 all-reduce.8
  964.1 76.8 reduce-scatter.10
  1043.3 78.3 reduce-scatter.6

commit v2 on v0

--- a/solution.py
+++ b/solution.py
@@ -1,6 +1,11 @@
+import functools
+import itertools
+
 import jax
 import jax.numpy as jnp
 from jax import lax
+from jax.experimental import pallas as pl
+from jax.experimental.pallas import tpu as pltpu
 from jax.sharding import PartitionSpec as P
 
 KD = 256
@@ -9,6 +14,13 @@
 
 EPS = 1e-05
 GROUP_EPS = 0.1
+GELU_SCALE = 0.7978845608028654
+CHUNKS = 4
+
+MESH = pl.DeviceIdType.MESH
+VMEM_BYTES = 60 * 2**20
+TILE = 256
+LINE = 16
 
 
 def norm_parts(rows, gain, bias):
@@ -48,10 +60,6 @@
     return jax.nn.silu(gates) * normed
 
 
-def gelu_product(gate_in, lin_in):
-    return jax.nn.gelu(gate_in) * lin_in
-
-
 def product(left, right):
     return jnp.dot(left, right, preferred_element_type=jnp.float32)
 
@@ -66,6 +74,1043 @@
     return lax.dot_general(
         left, right, (((0,), (0,)), ((), ())), preferred_element_type=jnp.float32
     )
+
+
+def for_columns(width, body):
+    full = width // TILE
+
+    def step(index, carry):
+        body(pl.multiple_of(index * TILE, TILE), TILE)
+        return carry
+
+    if full:
+        lax.fori_loop(0, full, step, 0)
+    if width % TILE:
+        body(full * TILE, width % TILE)
+
+
+def for_rows(count, body):
+    def step(index, carry):
+        body(pl.ds(pl.multiple_of(index * LINE, LINE), LINE))
+        return carry
+
+    lax.fori_loop(0, count // LINE, step, 0)
+
+
+def dot_nn(left, right):
+    return lax.dot_general(left, right, (((1,), (0,)), ((), ())), preferred_element_type=jnp.float32)
+
+
+def dot_nt(left, right):
+    return lax.dot_general(left, right, (((1,), (1,)), ((), ())), preferred_element_type=jnp.float32)
+
+
+def enter(peers, line):
+    barrier = pltpu.get_barrier_semaphore()
+    for peer in peers:
+        pl.semaphore_signal(barrier, inc=1, device_id=peer, device_id_type=MESH)
+    if line is not None:
+        size, me = line
+
+        @pl.when(me > 0)
+        def _():
+            pl.semaphore_signal(barrier, inc=1, device_id={"tensor": me - 1}, device_id_type=MESH)
+
+        @pl.when(me < size - 1)
+        def _():
+            pl.semaphore_signal(barrier, inc=1, device_id={"tensor": me + 1}, device_id_type=MESH)
+
+    count = len(peers)
+    if line is not None:
+        count = count + (me > 0).astype(jnp.int32) + (me < size - 1).astype(jnp.int32)
+    pl.semaphore_wait(barrier, count)
+
+
+class LineScatter:
+    def __init__(self, size, me, rows, part, inbox, send, recv):
+        self.size, self.me, self.rows = size, me, rows
+        self.part, self.inbox, self.send, self.recv = part, inbox, send, recv
+
+    def at(self, chunk):
+        return pl.ds(chunk * self.rows, self.rows)
+
+    def copy(self, target, slot, chunk, device):
+        return pltpu.make_async_remote_copy(
+            src_ref=self.part.at[target, self.at(chunk)],
+            dst_ref=self.inbox.at[slot, self.at(chunk)],
+            send_sem=self.send.at[target, chunk],
+            recv_sem=self.recv.at[slot, chunk],
+            device_id={"tensor": device},
+            device_id_type=MESH,
+        )
+
+    def add(self, target, chunk):
+        def body(rows):
+            at = pl.ds(chunk * self.rows + rows.start, LINE)
+            total = self.part[target, at, :].astype(jnp.float32)
+            total = total + self.inbox[target, at, :].astype(jnp.float32)
+            self.part[target, at, :] = total.astype(jnp.bfloat16)
+
+        for_rows(self.rows, body)
+
+    def go_right(self, chunk, target):
+        self.copy(target, target, chunk, self.me + 1).start()
+
+    def go_left(self, chunk, target):
+        last = self.me - 1 == target
+        self.copy(target, jnp.where(last, self.size, target), chunk, self.me - 1).start()
+
+    def begin(self, chunk):
+        @pl.when(self.me == 0)
+        def _():
+            for target in range(self.size - 1, 0, -1):
+                self.go_right(chunk, target)
+
+        @pl.when(self.me == self.size - 1)
+        def _():
+            for target in range(self.size - 1):
+                self.go_left(chunk, target)
+
+    def put(self, chunk, step):
+        size, me = self.size, self.me
+        right, left = size - 1 - step, step
+
+        @pl.when((me < right) & (me > 0))
+        def _():
+            self.copy(right, right, chunk, me).wait_recv()
+            self.add(right, chunk)
+            self.go_right(chunk, right)
+
+        @pl.when((me > left) & (me < size - 1))
+        def _():
+            self.copy(left, left, chunk, me).wait_recv()
+            self.add(left, chunk)
+            self.go_left(chunk, left)
+
+    def arrive(self, chunk):
+        size, me = self.size, self.me
+
+        @pl.when(me > 0)
+        def _():
+            self.copy(me, me, chunk, me - 1).wait_recv()
+
+        @pl.when(me < size - 1)
+        def _():
+            self.copy(me, size, chunk, me + 1).wait_recv()
+
+    def total(self, rows):
+        size, me = self.size, self.me
+        own = self.part[me, rows, :].astype(jnp.float32)
+        low = self.inbox[me, rows, :].astype(jnp.float32)
+        high = self.inbox[size, rows, :].astype(jnp.float32)
+        return own + jnp.where(me > 0, low, 0.0) + jnp.where(me < size - 1, high, 0.0)
+
+    def drain(self, chunk):
+        for target in range(self.size):
+
+            @pl.when(self.me != target)
+            def _():
+                self.copy(target, target, chunk, self.me).wait_send()
+
+
+class LineGather:
+    def __init__(self, size, me, rows, held, send, recv):
+        self.size, self.me, self.rows = size, me, rows
+        self.held, self.send, self.recv = held, send, recv
+
+    def copy(self, block, chunk, way, device):
+        at = pl.ds(chunk * self.rows, self.rows)
+        return pltpu.make_async_remote_copy(
+            src_ref=self.held.at[block, at],
+            dst_ref=self.held.at[block, at],
+            send_sem=self.send.at[way, block, chunk],
+            recv_sem=self.recv.at[block, chunk],
+            device_id={"tensor": device},
+            device_id_type=MESH,
+        )
+
+    def put(self, chunk, step):
+        size, me = self.size, self.me
+
+        @pl.when(me >= step)
+        def _():
+            if step:
+                self.copy(me - step, chunk, 0, me).wait_recv()
+
+            @pl.when(me < size - 1)
+            def _():
+                self.copy(me - step, chunk, 0, me + 1).start()
+
+        @pl.when(me + step < size)
+        def _():
+            if step:
+                self.copy(me + step, chunk, 1, me).wait_recv()
+
+            @pl.when(me > 0)
+            def _():
+                self.copy(me + step, chunk, 1, me - 1).start()
+
+    def drain(self, chunk):
+        size, me = self.size, self.me
+        for step in range(size):
+
+            @pl.when((me >= step) & (me < size - 1))
+            def _():
+                self.copy(me - step, chunk, 0, me + 1).wait_send()
+
+            @pl.when((me + step < size) & (me > 0))
+            def _():
+                self.copy(me + step, chunk, 1, me - 1).wait_send()
+
+
+class CubeSum:
+    def __init__(self, bits, me, sources, results, parts, firsts, nexts, load, store, send, recv, free):
+        self.bits, self.me = bits, me
+        self.sources, self.results, self.parts = sources, results, parts
+        self.firsts, self.nexts = firsts, nexts
+        self.load_sem, self.store_sem, self.send, self.recv = load, store, send, recv
+        self.free = free
+        self.orders = (tuple(range(bits)), (0,) + tuple(range(bits - 1, 0, -1)))
+        self.mine = [(me // 2**bit) % 2 for bit in range(bits)]
+        self.steps = 2 * bits + 1
+
+    def partner(self, bit):
+        return self.me + (1 - 2 * self.mine[bit]) * 2**bit
+
+    def band(self, which, color):
+        count = self.parts[which].shape[-2]
+        cut = cut_rows(count)
+        return ((0, cut), (cut, count - cut), (0, count))[color]
+
+    def lead(self, fixed):
+        return tuple(fixed.get(bit, slice(None)) for bit in range(self.bits - 1, -1, -1))
+
+    def moved(self, src, dst, which, color, step, bit):
+        return pltpu.make_async_remote_copy(
+            src_ref=src,
+            dst_ref=dst,
+            send_sem=self.send.at[which, color % 2, step],
+            recv_sem=self.recv.at[which, color % 2, step],
+            device_id={"dp": self.partner(bit)},
+            device_id_type=MESH,
+        )
+
+    def halve(self, which, color, step):
+        order = self.orders[color % 2]
+        start, count = self.band(which, color)
+        fixed = {bit: self.mine[bit] for bit in order[:step]}
+        fixed[order[step]] = 1 - self.mine[order[step]]
+        src = self.parts[which].at[self.lead(fixed) + (pl.ds(start, count), slice(None))]
+        dst = self.firsts[which] if step == 0 else self.nexts[which][color][step - 1]
+        return self.moved(src, dst, which, color, step, order[step])
+
+    def double(self, which, color, step):
+        order = self.orders[color % 2]
+        start, count = self.band(which, color)
+        fixed = {bit: self.mine[bit] for bit in order[: step + 1]}
+        held = self.parts[which].at[self.lead(fixed) + (pl.ds(start, count), slice(None))]
+        return self.moved(held, held, which, color, 2 * self.bits - 1 - step, order[step])
+
+    def freed(self, which, color, step):
+        return self.free.at[which, color % 2, step]
+
+    def land(self, which, color, step):
+        copy = self.halve(which, color, step)
+        copy.wait_send()
+        partner = {"dp": self.partner(self.orders[color % 2][step])}
+        pl.semaphore_signal(
+            self.freed(which, color, step), inc=1, device_id=partner, device_id_type=MESH
+        )
+        copy.wait_recv()
+        self.add(which, color, step)
+
+    def grow(self, which, color, step):
+        pl.semaphore_wait(self.freed(which, color, step), 1)
+        self.double(which, color, step).start()
+
+    def add(self, which, color, step):
+        order = self.orders[color % 2]
+        part, (start, count) = self.parts[which], self.band(which, color)
+        box = self.firsts[which] if step == 0 else self.nexts[which][color][step - 1]
+        fixed = {bit: self.mine[bit] for bit in order[: step + 1]}
+        free = [bit for bit in range(self.bits - 1, -1, -1) if bit not in fixed]
+        for choice in itertools.product((0, 1), repeat=len(free)):
+            lead = self.lead({**fixed, **dict(zip(free, choice))})
+
+            def body(begin, size):
+                there = lead + (pl.ds(start + begin, size), slice(None))
+                total = part[there].astype(jnp.float32)
+                total = total + box[choice + (pl.ds(begin, size), slice(None))].astype(jnp.float32)
+                part[there] = total.astype(jnp.bfloat16)
+
+            for_blocks(count, part.shape[-1], body)
+
+    def slices(self, which, ref):
+        rows, columns = self.parts[which].shape[-2:]
+        for index in range(2**self.bits):
+            lead = tuple((index >> bit) & 1 for bit in range(self.bits - 1, -1, -1))
+            if ref.shape[0] == rows:
+                whole = ref.at[:, pl.ds(index * columns, columns)]
+            else:
+                whole = ref.at[pl.ds(index * rows, rows), :]
+            yield index, self.parts[which].at[lead], whole
+
+    def load(self, which):
+        for index, part, whole in self.slices(which, self.sources[which]):
+            pltpu.make_async_copy(whole, part, self.load_sem.at[which, index]).start()
+
+    def step(self, which, stage):
+        bits = self.bits
+        if stage == 0:
+            for index, part, whole in self.slices(which, self.sources[which]):
+                pltpu.make_async_copy(whole, part, self.load_sem.at[which, index]).wait()
+            self.halve(which, 2, 0).start()
+        elif stage < bits:
+            if stage == 1:
+                self.land(which, 2, 0)
+            for color in range(2):
+                if stage > 1:
+                    self.land(which, color, stage - 1)
+                self.halve(which, color, stage).start()
+        elif stage < 2 * bits - 1:
+            back = 2 * bits - 1 - stage
+            for color in range(2):
+                if back == bits - 1:
+                    self.land(which, color, back)
+                else:
+                    self.double(which, color, back + 1).wait_recv()
+                self.grow(which, color, back)
+        elif stage == 2 * bits - 1:
+            for color in range(2):
+                self.double(which, color, 1).wait_recv()
+            self.grow(which, 2, 0)
+        else:
+            self.double(which, 2, 0).wait_recv()
+            for index, part, whole in self.slices(which, self.results[which]):
+                pltpu.make_async_copy(part, whole, self.store_sem.at[which, index]).start()
+
+    def calls(self):
+        for tick in range(len(self.parts) + self.steps - 1):
+            for stage in range(self.steps - 1, -1, -1):
+                if 0 <= tick - stage < len(self.parts):
+                    yield functools.partial(self.step, tick - stage, stage)
+
+    def drain(self):
+        for which in range(len(self.parts)):
+            self.double(which, 2, 0).wait_send()
+            for color in range(2):
+                for step in range(1, self.bits):
+                    self.double(which, color, step).wait_send()
+            for index, part, whole in self.slices(which, self.results[which]):
+                pltpu.make_async_copy(part, whole, self.store_sem.at[which, index]).wait()
+
+
+def cut_rows(count):
+    return count // (2 * LINE) * LINE
+
+
+def for_blocks(count, columns, body):
+    size = LINE
+    while count % (2 * size) == 0 and 2 * size * columns <= 2**14:
+        size *= 2
+    for factor in (3, 5):
+        if count % (factor * size) == 0 and factor * size * columns <= 2**14:
+            size *= factor
+
+    def step(index, carry):
+        body(pl.multiple_of(index * size, LINE), size)
+        return carry
+
+    lax.fori_loop(0, count // size, step, 0)
+
+
+def cube_scratch(bits, shapes):
+    low = jnp.bfloat16
+    parts, firsts, nexts = [], [], []
+    for rows, columns in shapes:
+        if columns >= rows:
+            columns = columns // 2**bits
+        else:
+            rows = rows // 2**bits
+        cut = cut_rows(rows)
+        parts.append(pltpu.VMEM((2,) * bits + (rows, columns), low))
+        firsts.append(pltpu.VMEM((2,) * (bits - 1) + (rows, columns), low))
+        nexts.append(
+            [
+                [
+                    pltpu.VMEM((2,) * (bits - 1 - step) + (count, columns), low)
+                    for step in range(1, bits)
+                ]
+                for count in (cut, rows - cut)
+            ]
+        )
+    dma = pltpu.SemaphoreType.DMA
+    return [
+        parts,
+        firsts,
+        nexts,
+        dma((len(shapes), 2**bits)),
+        dma((len(shapes), 2**bits)),
+        dma((len(shapes), 2, 2 * bits)),
+        dma((len(shapes), 2, 2 * bits)),
+        pltpu.SemaphoreType.REGULAR((len(shapes), 2, bits)),
+    ]
+
+
+def interleave(first, second):
+    places = [((index + 0.5) / len(first), call) for index, call in enumerate(first)]
+    places += [((index + 0.5) / len(second), call) for index, call in enumerate(second)]
+    for _, call in sorted(places, key=lambda item: item[0]):
+        call()
+
+
+def feed_kernel(
+    size,
+    chunks,
+    mixed_hbm,
+    out_hbm,
+    tokens_hbm,
+    seed_hbm,
+    gate_hbm,
+    up_hbm,
+    down_hbm,
+    gain_ref,
+    bias_ref,
+    second_hbm,
+    seeds_hbm,
+    inner_hbm,
+    dgate_hbm,
+    dlin_hbm,
+    dsecond_hbm,
+    outp_hbm,
+    middle_ref,
+    mixed,
+    out_weight,
+    tokens,
+    hidden_gate,
+    hidden_up,
+    hidden_down,
+    second,
+    seeds,
+    part,
+    inbox,
+    gate_in,
+    lin_in,
+    dinner,
+    inner,
+    dgate,
+    dlin,
+    wide,
+    load_sem,
+    store_sem,
+    rs_send,
+    rs_recv,
+    ag_send,
+    ag_recv,
+    seed_send,
+    seed_recv,
+):
+    me = lax.axis_index("tensor")
+    own, depth = tokens.shape
+    rows = own // chunks
+    hidden = inner.shape[-1]
+    loads = [
+        pltpu.make_async_copy(src, dst, load_sem.at[index])
+        for index, (src, dst) in enumerate(
+            (
+                (mixed_hbm, mixed),
+                (out_hbm, out_weight),
+                (seed_hbm, seeds.at[me]),
+                (tokens_hbm, tokens),
+                (gate_hbm, hidden_gate),
+                (up_hbm, hidden_up),
+                (down_hbm, hidden_down),
+            )
+        )
+    ]
+    for load in loads:
+        load.start()
+    enter((), (size, me))
+    scatter = LineScatter(size, me, rows, part, inbox, rs_send, rs_recv)
+    gather = LineGather(size, me, rows, second, ag_send, ag_recv)
+    gather_seed = LineGather(size, me, rows, seeds, seed_send, seed_recv)
+
+    def at(chunk):
+        return pl.ds(chunk * rows, rows)
+
+    def flat(ref, chunk):
+        value = ref[:, at(chunk), :]
+        return value.reshape(size * rows, value.shape[-1])
+
+    def store(kind, chunk):
+        slot = chunk % 2
+        src, dst = (
+            (second.at[:, at(chunk)], second_hbm),
+            (seeds.at[:, at(chunk)], seeds_hbm),
+            (inner.at[slot], inner_hbm),
+            (dgate.at[slot], dgate_hbm),
+            (dlin.at[slot], dlin_hbm),
+            (wide.at[slot, 0], dsecond_hbm),
+            (wide.at[slot, 1], outp_hbm),
+        )[kind]
+        return pltpu.make_async_copy(src, dst.at[:, at(chunk)], store_sem.at[kind, chunk])
+
+    def project(chunk):
+        def body(start, width):
+            value = dot_nn(flat(mixed, chunk), out_weight[:, pl.ds(start, width)])
+            part[:, at(chunk), pl.ds(start, width)] = value.astype(jnp.bfloat16).reshape(
+                size, rows, width
+            )
+
+        for_columns(depth, body)
+
+    def normalize(chunk):
+        scatter.arrive(chunk)
+
+        def body(block):
+            here = pl.ds(chunk * rows + block.start, LINE)
+            middle = tokens[here, :].astype(jnp.float32) + scatter.total(here)
+            middle_ref[here, :] = middle
+            centered = middle - jnp.mean(middle, axis=-1, keepdims=True)
+            scale = lax.rsqrt(jnp.mean(centered * centered, axis=-1, keepdims=True) + EPS)
+            value = centered * scale * gain_ref[...] + bias_ref[...]
+            second[me, here, :] = value.astype(jnp.bfloat16)
+
+        for_rows(rows, body)
+        gather.put(chunk, 0)
+
+    def feed(chunk):
+        slot = chunk % 2
+        if chunk >= 2:
+            for kind in range(2, 7):
+                store(kind, chunk - 2).wait()
+        def body_in(start, width):
+            columns = pl.ds(start, width)
+            left = flat(second, chunk)
+            gate_in[:, columns] = dot_nt(left, hidden_gate[columns, :])
+            lin_in[:, columns] = dot_nt(left, hidden_up[columns, :])
+            dinner[:, columns] = dot_nt(flat(seeds, chunk), hidden_down[columns, :])
+
+        for_columns(hidden, body_in)
+
+        def body_act(block):
+            gate, lin, grad = gate_in[block, :], lin_in[block, :], dinner[block, :]
+            cube = GELU_SCALE * (gate + 0.044715 * (gate * gate * gate))
+            tanh = jnp.tanh(cube)
+            half = 0.5 * (1.0 + tanh)
+            active = gate * half
+            slope = half + 0.5 * gate * (1.0 - tanh * tanh) * (
+                GELU_SCALE * (1.0 + 3.0 * 0.044715 * (gate * gate))
+            )
+            owner = block.start // rows
+            inside = pl.ds(block.start - owner * rows, LINE)
+            inner[slot, owner, inside, :] = (active * lin).astype(jnp.bfloat16)
+            dlin[slot, owner, inside, :] = (grad * active).astype(jnp.bfloat16)
+            dgate[slot, owner, inside, :] = (grad * lin * slope).astype(jnp.bfloat16)
+
+        for_rows(size * rows, body_act)
+        def body_out(start, width):
+            columns = pl.ds(start, width)
+            inner_all = inner[slot].reshape(size * rows, hidden)
+            dgate_all = dgate[slot].reshape(size * rows, hidden)
+            dlin_all = dlin[slot].reshape(size * rows, hidden)
+            grad = dot_nn(dgate_all, hidden_gate[:, columns])
+            grad = grad + dot_nn(dlin_all, hidden_up[:, columns])
+            wide[slot, 0, :, :, columns] = grad.astype(jnp.bfloat16).reshape(size, rows, width)
+            value = dot_nn(inner_all, hidden_down[:, columns])
+            wide[slot, 1, :, :, columns] = value.astype(jnp.bfloat16).reshape(size, rows, width)
+
+        for_columns(depth, body_out)
+        for kind in range(7):
+            store(kind, chunk).start()
+
+    loads[2].wait()
+    gather_seed.put(0, 0)
+    loads[0].wait()
+    loads[1].wait()
+    project(0)
+    scatter.begin(0)
+    for tick in range(chunks + 1):
+        for step in range(size - 1):
+            if tick < chunks:
+                scatter.put(tick, step)
+            if tick:
+                gather.put(tick - 1, step + 1)
+            if tick < chunks and step:
+                gather_seed.put(tick, step)
+        if tick == 0:
+            loads[3].wait()
+        if tick < chunks:
+            normalize(tick)
+            gather_seed.put(tick, size - 1)
+        if tick < chunks - 1:
+            project(tick + 1)
+            scatter.begin(tick + 1)
+            gather_seed.put(tick + 1, 0)
+        if tick == 0:
+            for load in loads[4:]:
+                load.wait()
+        if tick:
+            feed(tick - 1)
+    for chunk in range(chunks):
+        scatter.drain(chunk)
+        gather.drain(chunk)
+        gather_seed.drain(chunk)
+        for kind in range(7 if chunk >= chunks - 2 else 2):
+            store(kind, chunk).wait()
+
+
+def feed_forward(size, chunks, mixed, out_weight, tokens, cotangent, hidden_gate, hidden_up, hidden_down, gain, bias):
+    own, depth = tokens.shape
+    hidden = hidden_gate.shape[0]
+    rows = own // chunks
+    low, full = jnp.bfloat16, jnp.float32
+
+    def blocks(width):
+        return jax.ShapeDtypeStruct((size, own, width), low)
+
+    dma = pltpu.SemaphoreType.DMA
+    wide, thin = (size, own, depth), (2, size, rows, hidden)
+    return pl.pallas_call(
+        functools.partial(feed_kernel, size, chunks),
+        out_shape=(
+            blocks(depth),
+            blocks(depth),
+            blocks(hidden),
+            blocks(hidden),
+            blocks(hidden),
+            blocks(depth),
+            blocks(depth),
+            jax.ShapeDtypeStruct((own, depth), full),
+        ),
+        in_specs=[pl.BlockSpec(memory_space=pl.ANY)] * 7
+        + [pl.BlockSpec(memory_space=pltpu.VMEM)] * 2,
+        out_specs=(pl.BlockSpec(memory_space=pl.ANY),) * 7
+        + (pl.BlockSpec(memory_space=pltpu.VMEM),),
+        scratch_shapes=[
+            pltpu.VMEM((size, own, mixed.shape[-1]), low),
+            pltpu.VMEM(out_weight.shape, low),
+            pltpu.VMEM((own, depth), low),
+            pltpu.VMEM((hidden, depth), low),
+            pltpu.VMEM((hidden, depth), low),
+            pltpu.VMEM((hidden, depth), low),
+            pltpu.VMEM(wide, low),
+            pltpu.VMEM(wide, low),
+            pltpu.VMEM(wide, low),
+            pltpu.VMEM((size + 1, own, depth), low),
+            pltpu.VMEM((size * rows, hidden), full),
+            pltpu.VMEM((size * rows, hidden), full),
+            pltpu.VMEM((size * rows, hidden), full),
+            pltpu.VMEM(thin, low),
+            pltpu.VMEM(thin, low),
+            pltpu.VMEM(thin, low),
+            pltpu.VMEM((2, 2, size, rows, depth), low),
+            dma((7,)),
+            dma((7, chunks)),
+            dma((size, chunks)),
+            dma((size + 1, chunks)),
+            dma((2, size, chunks)),
+            dma((size, chunks)),
+            dma((2, size, chunks)),
+            dma((size, chunks)),
+        ],
+        compiler_params=pltpu.CompilerParams(
+            collective_id=0, has_side_effects=True, vmem_limit_bytes=VMEM_BYTES
+        ),
+        cost_estimate=pl.CostEstimate(
+            flops=14 * size * own * depth * hidden, bytes_accessed=2**26, transcendentals=0
+        ),
+    )(mixed, out_weight, tokens, cotangent, hidden_gate, hidden_up, hidden_down, gain, bias)
+
+
+def back_kernel(
+    size,
+    bits,
+    chunks,
+    dsecond_hbm,
+    out_hbm,
+    middle_ref,
+    seed_ref,
+    gain_ref,
+    grads_hbm,
+    branch_hbm,
+    dmixed_hbm,
+    dmiddle_ref,
+    sums_ref,
+    totals_hbm,
+    part,
+    out_weight,
+    branch,
+    inbox,
+    dmixed,
+    load_sem,
+    store_sem,
+    rs_send,
+    rs_recv,
+    ag_send,
+    ag_recv,
+    cube_parts,
+    cube_firsts,
+    cube_nexts,
+    cube_load,
+    cube_store,
+    cube_send,
+    cube_recv,
+    cube_free,
+):
+    me = lax.axis_index("tensor")
+    own, depth = seed_ref.shape
+    rows = own // chunks
+    load_part = pltpu.make_async_copy(dsecond_hbm, part, load_sem.at[0])
+    load_out = pltpu.make_async_copy(out_hbm, out_weight, load_sem.at[1])
+    load_part.start()
+    cube = CubeSum(
+        bits,
+        lax.axis_index("dp"),
+        grads_hbm,
+        totals_hbm,
+        cube_parts,
+        cube_firsts,
+        cube_nexts,
+        cube_load,
+        cube_store,
+        cube_send,
+        cube_recv,
+        cube_free,
+    )
+    for which in range(len(cube_parts)):
+        cube.load(which)
+    load_out.start()
+    enter([{"dp": cube.partner(bit)} for bit in range(bits)], (size, me))
+    scatter = LineScatter(size, me, rows, part, inbox, rs_send, rs_recv)
+    gather = LineGather(size, me, rows, branch, ag_send, ag_recv)
+
+    def at(chunk):
+        return pl.ds(chunk * rows, rows)
+
+    def store(kind, chunk):
+        if kind == 0:
+            src, dst = branch.at[:, at(chunk)], branch_hbm
+        else:
+            src, dst = dmixed.at[chunk % 2], dmixed_hbm
+        return pltpu.make_async_copy(src, dst.at[:, at(chunk)], store_sem.at[kind, chunk])
+
+    def normalize(chunk):
+        scatter.arrive(chunk)
+
+        def body(block):
+            here = pl.ds(chunk * rows + block.start, LINE)
+            middle = middle_ref[here, :]
+            centered = middle - jnp.mean(middle, axis=-1, keepdims=True)
+            scale = lax.rsqrt(jnp.mean(centered * centered, axis=-1, keepdims=True) + EPS)
+            normed = centered * scale
+            grad = scatter.total(here)
+            shaped = grad * gain_ref[...]
+            sums_ref[0:1, :] += jnp.sum(grad * normed, axis=0, keepdims=True)
+            sums_ref[1:2, :] += jnp.sum(grad, axis=0, keepdims=True)
+            dmiddle = seed_ref[here, :].astype(jnp.float32) + scale * (
+                shaped
+                - jnp.mean(shaped, axis=-1, keepdims=True)
+                - normed * jnp.mean(shaped * normed, axis=-1, keepdims=True)
+            )
+            dmiddle_ref[here, :] = dmiddle
+            branch[me, here, :] = dmiddle.astype(jnp.bfloat16)
+
+        for_rows(rows, body)
+        gather.put(chunk, 0)
+
+    def unproject(chunk):
+        if chunk >= 2:
+            store(1, chunk - 2).wait()
+
+        def body(start, width):
+            columns = pl.ds(start, width)
+            left = branch[:, at(chunk), :].reshape(size * rows, depth)
+            value = dot_nt(left, out_weight[columns, :])
+            dmixed[chunk % 2, :, :, columns] = value.reshape(size, rows, width)
+
+        for_columns(out_weight.shape[0], body)
+        for kind in range(2):
+            store(kind, chunk).start()
+
+    def line_calls():
+        for tick in range(chunks + 1):
+            for step in range(size - 1):
+                if tick < chunks:
+                    yield functools.partial(scatter.put, tick, step)
+                if tick:
+                    yield functools.partial(gather.put, tick - 1, step + 1)
+            if tick < chunks - 1:
+                yield functools.partial(scatter.begin, tick + 1)
+            if tick < chunks:
+                yield functools.partial(normalize, tick)
+            if tick == 0:
+                yield load_out.wait
+            if tick:
+                yield functools.partial(unproject, tick - 1)
+
+    sums_ref[...] = jnp.zeros_like(sums_ref)
+    load_part.wait()
+    scatter.begin(0)
+    interleave(list(cube.calls()), list(line_calls()))
+    for chunk in range(chunks):
+        scatter.drain(chunk)
+        gather.drain(chunk)
+        for kind in range(2 if chunk >= chunks - 2 else 1):
+            store(kind, chunk).wait()
+    cube.drain()
+
+
+def feed_back(size, bits, chunks, dsecond, out_weight, middle, cotangent, gain, grads):
+    own, depth = cotangent.shape
+    rows = own // chunks
+    width = out_weight.shape[0]
+    low, full = jnp.bfloat16, jnp.float32
+    dma = pltpu.SemaphoreType.DMA
+    vmem, anywhere = pl.BlockSpec(memory_space=pltpu.VMEM), pl.BlockSpec(memory_space=pl.ANY)
+    many = [anywhere] * len(grads)
+    return pl.pallas_call(
+        functools.partial(back_kernel, size, bits, chunks),
+        out_shape=(
+            jax.ShapeDtypeStruct((size, own, depth), low),
+            jax.ShapeDtypeStruct((size, own, width), full),
+            jax.ShapeDtypeStruct((own, depth), full),
+            jax.ShapeDtypeStruct((8, depth), full),
+            [jax.ShapeDtypeStruct(grad.shape, low) for grad in grads],
+        ),
+        in_specs=[anywhere, anywhere, vmem, vmem, vmem, many],
+        out_specs=(anywhere, anywhere, vmem, vmem, many),
+        scratch_shapes=[
+            pltpu.VMEM((size, own, depth), low),
+            pltpu.VMEM(out_weight.shape, low),
+            pltpu.VMEM((size, own, depth), low),
+            pltpu.VMEM((size + 1, own, depth), low),
+            pltpu.VMEM((2, size, rows, width), full),
+            dma((2,)),
+            dma((2, chunks)),
+            dma((size, chunks)),
+            dma((size + 1, chunks)),
+            dma((2, size, chunks)),
+            dma((size, chunks)),
+        ]
+        + cube_scratch(bits, [grad.shape for grad in grads]),
+        compiler_params=pltpu.CompilerParams(
+            collective_id=1, has_side_effects=True, vmem_limit_bytes=VMEM_BYTES
+        ),
+        cost_estimate=pl.CostEstimate(
+            flops=2 * size * own * depth * width, bytes_accessed=2**26, transcendentals=0
+        ),
+    )(dsecond, out_weight, middle, cotangent, gain, grads)
+
+
+def last_kernel(
+    size,
+    bits,
+    chunks,
+    dfirst_hbm,
+    outp_hbm,
+    tokens_ref,
+    middle_ref,
+    dmiddle_ref,
+    gain_ref,
+    sums_ref,
+    grads_hbm,
+    output_ref,
+    dtokens_ref,
+    totals_ref,
+    totals_hbm,
+    first_part,
+    first_inbox,
+    out_part,
+    out_inbox,
+    line_box,
+    dp_box,
+    load_sem,
+    line_send,
+    line_recv,
+    dp_send,
+    dp_recv,
+    rs_send,
+    rs_recv,
+    out_send,
+    out_recv,
+    cube_parts,
+    cube_firsts,
+    cube_nexts,
+    cube_load,
+    cube_store,
+    cube_send,
+    cube_recv,
+    cube_free,
+):
+    me = lax.axis_index("tensor")
+    mine = lax.axis_index("dp")
+    own = tokens_ref.shape[0]
+    rows = own // chunks
+    load_first = pltpu.make_async_copy(dfirst_hbm, first_part, load_sem.at[0])
+    load_out = pltpu.make_async_copy(outp_hbm, out_part, load_sem.at[1])
+    load_first.start()
+    cube = CubeSum(
+        bits,
+        mine,
+        grads_hbm,
+        totals_hbm,
+        cube_parts,
+        cube_firsts,
+        cube_nexts,
+        cube_load,
+        cube_store,
+        cube_send,
+        cube_recv,
+        cube_free,
+    )
+    for which in range(len(cube_parts)):
+        cube.load(which)
+    load_out.start()
+    groups = 2**bits
+    peers = [{"dp": (mine + step) % groups} for step in range(1, groups)]
+    others = [{"tensor": (me + step) % size} for step in range(1, size)]
+    enter(peers + others, None)
+    first = LineScatter(size, me, rows, first_part, first_inbox, rs_send, rs_recv)
+    last = LineScatter(size, me, rows, out_part, out_inbox, out_send, out_recv)
+
+    def back(chunk):
+        first.arrive(chunk)
+
+        def body(block):
+            here = pl.ds(chunk * rows + block.start, LINE)
+            values = tokens_ref[here, :].astype(jnp.float32)
+            centered = values - jnp.mean(values, axis=-1, keepdims=True)
+            scale = lax.rsqrt(jnp.mean(centered * centered, axis=-1, keepdims=True) + EPS)
+            normed = centered * scale
+            grad = first.total(here)
+            shaped = grad * gain_ref[...]
+            line_box[me, 2:3, :] += jnp.sum(grad * normed, axis=0, keepdims=True)
+            line_box[me, 3:4, :] += jnp.sum(grad, axis=0, keepdims=True)
+            dtokens_ref[here, :] = dmiddle_ref[here, :] + scale * (
+                shaped
+                - jnp.mean(shaped, axis=-1, keepdims=True)
+                - normed * jnp.mean(shaped * normed, axis=-1, keepdims=True)
+            )
+
+        for_rows(rows, body)
+
+    def finish(chunk):
+        last.arrive(chunk)
+
+        def body(block):
+            here = pl.ds(chunk * rows + block.start, LINE)
+            output_ref[here, :] = (middle_ref[here, :] + last.total(here)).astype(jnp.bfloat16)
+
+        for_rows(rows, body)
+
+    def line_copy(step, slot):
+        return pltpu.make_async_remote_copy(
+            src_ref=line_box.at[me],
+            dst_ref=line_box.at[slot],
+            send_sem=line_send.at[step],
+            recv_sem=line_recv.at[slot],
+            device_id={"tensor": (me + step) % size},
+            device_id_type=MESH,
+        )
+
+    def dp_copy(step, slot):
+        return pltpu.make_async_remote_copy(
+            src_ref=dp_box.at[mine],
+            dst_ref=dp_box.at[slot],
+            send_sem=dp_send.at[step],
+            recv_sem=dp_recv.at[slot],
+            device_id={"dp": (mine + step) % groups},
+            device_id_type=MESH,
+        )
+
+    def sums_on_line():
+        for step in range(1, size):
+            line_copy(step, me).start()
+
+    def sums_on_dp():
+        for step in range(1, size):
+            line_copy(step, (me + step) % size).wait_recv()
+        dp_box[mine] = jnp.sum(line_box[...], axis=0)
+        for step in range(1, groups):
+            dp_copy(step, mine).start()
+
+    def sums_done():
+        for step in range(1, groups):
+            dp_copy(step, (mine + step) % groups).wait_recv()
+        totals_ref[...] = jnp.sum(dp_box[...], axis=0)
+
+    def line_calls():
+        yield functools.partial(first.begin, 0)
+        for chunk in range(chunks):
+            for step in range(size - 1):
+                yield functools.partial(first.put, chunk, step)
+            yield functools.partial((first if chunk < chunks - 1 else last).begin, (chunk + 1) % chunks)
+            yield functools.partial(back, chunk)
+        yield sums_on_line
+        for chunk in range(chunks):
+            for step in range(size - 1):
+                yield functools.partial(last.put, chunk, step)
+            if chunk < chunks - 1:
+                yield functools.partial(last.begin, chunk + 1)
+            yield functools.partial(finish, chunk)
+            if chunk == 0:
+                yield sums_on_dp
+        yield sums_done
+
+    line_box[me] = sums_ref[...]
+    load_first.wait()
+    load_out.wait()
+    interleave(list(cube.calls()), list(line_calls()))
+    for chunk in range(chunks):
+        first.drain(chunk)
+        last.drain(chunk)
+    for step in range(1, size):
+        line_copy(step, me).wait_send()
+    for step in range(1, groups):
+        dp_copy(step, mine).wait_send()
+    cube.drain()
+
+
+def last_sums(size, bits, chunks, dfirst, partial, tokens, middle, dmiddle, gain, sums, grads):
+    own, depth = tokens.shape
+    low, full = jnp.bfloat16, jnp.float32
+    dma = pltpu.SemaphoreType.DMA
+    vmem, anywhere = pl.BlockSpec(memory_space=pltpu.VMEM), pl.BlockSpec(memory_space=pl.ANY)
+    many = [anywhere] * len(grads)
+    return pl.pallas_call(
+        functools.partial(last_kernel, size, bits, chunks),
+        out_shape=(
+            jax.ShapeDtypeStruct((own, depth), low),
+            jax.ShapeDtypeStruct((own, depth), full),
+            jax.ShapeDtypeStruct((8, depth), full),
+            [jax.ShapeDtypeStruct(grad.shape, low) for grad in grads],
+        ),
+        in_specs=[anywhere, anywhere, vmem, vmem, vmem, vmem, vmem, many],
+        out_specs=(vmem, vmem, vmem, many),
+        scratch_shapes=[
+            pltpu.VMEM((size, own, depth), low),
+            pltpu.VMEM((size + 1, own, depth), low),
+            pltpu.VMEM((size, own, depth), low),
+            pltpu.VMEM((size + 1, own, depth), low),
+            pltpu.VMEM((size, 8, depth), full),
+            pltpu.VMEM((2**bits, 8, depth), full),
+            dma((2,)),
+            dma((size,)),
+            dma((size,)),
+            dma((2**bits,)),
+            dma((2**bits,)),
+            dma((size, chunks)),
+            dma((size + 1, chunks)),
+            dma((size, chunks)),
+            dma((size + 1, chunks)),
+        ]
+        + cube_scratch(bits, [grad.shape for grad in grads]),
+        compiler_params=pltpu.CompilerParams(
+            collective_id=2, has_side_effects=True, vmem_limit_bytes=VMEM_BYTES
+        ),
+        cost_estimate=pl.CostEstimate(flops=2**30, bytes_accessed=2**26, transcendentals=0),
+    )(dfirst, partial, tokens, middle, dmiddle, gain, sums, grads)
 
 
 def per_device(
@@ -90,6 +1135,7 @@
     head_local = query_weight.shape[1] // KD
     scale_factor = KD ** (-0.5)
     inputs = tokens.astype(jnp.float32)
+    seed_all = lax.all_gather(cotangent, "tensor", axis=0, tiled=True)
     first_out, first_normed, first_scale = norm_parts(inputs, first_gain, first_bias)
     first_all = lax.all_gather(first_out.astype(jnp.bfloat16), "tensor", axis=0, tiled=True)
     queries = product(first_all, query_weight).astype(jnp.bfloat16)
@@ -120,41 +1166,36 @@
     gate_heads = gates.reshape(seq_count, seq_len, head_local, VD)
     mixed_full, mix_pull = jax.vjp(gated_norm, gate_heads, retained)
     mixed = mixed_full.reshape(group_rows, head_local * VD).astype(jnp.bfloat16)
-    middle = inputs + lax.psum_scatter(
-        product(mixed, out_weight), "tensor", scatter_dimension=0, tiled=True
-    )
-    second_out, second_normed, second_scale = norm_parts(middle, second_gain, second_bias)
-    second_all = lax.all_gather(second_out.astype(jnp.bfloat16), "tensor", axis=0, tiled=True)
-    gate_in = product(second_all, hidden_gate)
-    lin_in = product(second_all, hidden_up)
-    inner_full, inner_pull = jax.vjp(gelu_product, gate_in, lin_in)
-    inner = inner_full.astype(jnp.bfloat16)
-    output = (
-        middle
-        + lax.psum_scatter(product(inner, hidden_down), "tensor", scatter_dimension=0, tiled=True)
-    ).astype(jnp.bfloat16)
-    seed_all = lax.all_gather(cotangent, "tensor", axis=0, tiled=True)
-    grad_inner = product_nt(seed_all, hidden_down)
-    grad_hdown = product_tn(inner, seed_all)
-    grad_gate_in, grad_lin_in = inner_pull(grad_inner)
-    gate_in_low = grad_gate_in.astype(jnp.bfloat16)
-    lin_in_low = grad_lin_in.astype(jnp.bfloat16)
-    grad_hgate = product_tn(second_all, gate_in_low)
-    grad_hup = product_tn(second_all, lin_in_low)
-    grad_second = lax.psum_scatter(
-        product_nt(gate_in_low, hidden_gate) + product_nt(lin_in_low, hidden_up),
-        "tensor",
-        scatter_dimension=0,
-        tiled=True,
-    )
-    grad_sgain = jnp.sum(grad_second * second_normed, axis=0)
-    grad_sbias = jnp.sum(grad_second, axis=0)
-    grad_middle = cotangent.astype(jnp.float32) + norm_back(
-        grad_second, second_gain, second_normed, second_scale
-    )
-    branch_all = lax.all_gather(grad_middle.astype(jnp.bfloat16), "tensor", axis=0, tiled=True)
-    grad_mixed = product_nt(branch_all, out_weight)
-    grad_outw = product_tn(mixed, branch_all)
+    size = lax.axis_size("tensor")
+    bits = lax.axis_size("dp").bit_length() - 1
+    own = tokens.shape[0]
+    second_all, seed_all, inner, gate_in_low, lin_in_low, grad_second, partial, middle = feed_forward(
+        size,
+        CHUNKS,
+        mixed.reshape(size, own, head_local * VD),
+        out_weight,
+        tokens,
+        cotangent,
+        hidden_gate.T,
+        hidden_up.T,
+        hidden_down,
+        second_gain[None],
+        second_bias[None],
+    )
+
+    def flat(item):
+        return item.reshape(group_rows, item.shape[-1])
+
+    second_all, seed_all = flat(second_all), flat(seed_all)
+    feed_grads = [
+        product_tn(flat(inner), seed_all).astype(jnp.bfloat16),
+        product_tn(flat(gate_in_low), second_all).astype(jnp.bfloat16),
+        product_tn(flat(lin_in_low), second_all).astype(jnp.bfloat16),
+    ]
+    branch_all, grad_mixed, grad_middle, second_sums, feed_grads = feed_back(
+        size, bits, CHUNKS, grad_second, out_weight, middle, cotangent, second_gain[None], feed_grads
+    )
+    branch_all = flat(branch_all)
     grad_gates, grad_retained = mix_pull(grad_mixed.reshape(seq_count, seq_len, head_local, VD))
     gates_low = grad_gates.reshape(group_rows, head_local * VD).astype(jnp.bfloat16)
     retained_low = grad_retained.astype(jnp.bfloat16)
@@ -177,34 +1218,37 @@
     )
     queries_low = grad_queries.reshape(group_rows, head_local * KD).astype(jnp.bfloat16)
     keys_back = grad_keys.reshape(group_rows, head_local * KD).astype(jnp.bfloat16)
-    grad_queryw = product_tn(first_all, queries_low)
-    grad_keyw = product_tn(first_all, keys_back)
-    grad_valuew = product_tn(first_all, values_low)
-    grad_gatew = product_tn(first_all, gates_low)
+    grads = [
+        product_tn(mixed, branch_all).astype(jnp.bfloat16),
+        product_tn(values_low, first_all).astype(jnp.bfloat16),
+        product_tn(gates_low, first_all).astype(jnp.bfloat16),
+        product_tn(first_all, queries_low).astype(jnp.bfloat16),
+        product_tn(first_all, keys_back).astype(jnp.bfloat16),
+    ]
     total = product_nt(queries_low, query_weight)
     total = total + product_nt(keys_back, key_weight)
     total = total + product_nt(values_low, value_weight)
-    grad_first = lax.psum_scatter(
-        (total + product_nt(gates_low, gate_weight)).astype(jnp.bfloat16),
-        "tensor",
-        scatter_dimension=0,
-        tiled=True,
-    ).astype(jnp.float32)
-    grad_fgain = jnp.sum(grad_first * first_normed, axis=0)
-    grad_fbias = jnp.sum(grad_first, axis=0)
-    grad_tokens = grad_middle + norm_back(grad_first, first_gain, first_normed, first_scale)
-    grad_queryw, grad_keyw, grad_valuew, grad_gatew, grad_outw, grad_hgate, grad_hup, grad_hdown = (
-        lax.psum(grad_queryw.astype(jnp.bfloat16), "dp").astype(jnp.float32),
-        lax.psum(grad_keyw.astype(jnp.bfloat16), "dp").astype(jnp.float32),
-        lax.psum(grad_valuew.astype(jnp.bfloat16), "dp").astype(jnp.float32),
-        lax.psum(grad_gatew.astype(jnp.bfloat16), "dp").astype(jnp.float32),
-        lax.psum(grad_outw.astype(jnp.bfloat16), "dp").astype(jnp.float32),
-        lax.psum(grad_hgate.astype(jnp.bfloat16), "dp").astype(jnp.float32),
-        lax.psum(grad_hup.astype(jnp.bfloat16), "dp").astype(jnp.float32),
-        lax.psum(grad_hdown.astype(jnp.bfloat16), "dp").astype(jnp.float32),
-    )
-    grad_fgain, grad_fbias, grad_sgain, grad_sbias = lax.psum(
-        (grad_fgain, grad_fbias, grad_sgain, grad_sbias), ("dp", "tensor")
+    total = (total + product_nt(gates_low, gate_weight)).astype(jnp.bfloat16)
+    output, grad_tokens, sums, grads = last_sums(
+        size,
+        bits,
+        CHUNKS,
+        total.reshape(size, own, total.shape[-1]),
+        partial,
+        tokens,
+        middle,
+        grad_middle,
+        first_gain[None],
+        second_sums,
+        grads,
+    )
+    grad_sgain, grad_sbias, grad_fgain, grad_fbias = sums[0], sums[1], sums[2], sums[3]
+    grad_outw, grad_valuew, grad_gatew, grad_queryw, grad_keyw = (
+        item.astype(jnp.float32) for item in grads
+    )
+    grad_hdown, grad_hgate, grad_hup = (item.astype(jnp.float32) for item in feed_grads)
+    grad_valuew, grad_gatew, grad_hgate, grad_hup = (
+        item.T for item in (grad_valuew, grad_gatew, grad_hgate, grad_hup)
     )
     return (
         output,

time: 1350 us -> 874 us (0.65)
  waiting for transfers between devices: 1020 us -> 65.9 us
  Pallas kernels: 0 us -> 568 us
  matrix products: 166 us -> 111 us
  blocking collectives: 42.3 us -> 0 us
  local copies, waits for them, and re-layouts: 20.5 us -> 41.3 us
    pallas_call x0 -> x3, Pallas kernels: none -> 568 us  [the longest x1 213 us: feed_forward(): pl.pallas_call(functools.partial(feed_kernel, size, chunks), out_shape=(b...]
    reduce_scatter x4 -> x0, waiting for transfers between devices: 454 us -> none  [the longest x1 144 us: per_device(): lax.psum_scatter(product(inner, hidden_down), 'tensor', scatter_dimension...]
    psum x1 -> x0, waiting for transfers between devices: 275 us -> none  [per_device(): lax.psum(grad_queryw.astype(jnp.bfloat16), 'dp').astype(jnp.float32)]
    all_gather x3 -> x0, waiting for transfers between devices: 229 us -> none  [the longest x1 81.6 us: per_device(): lax.all_gather(grad_middle.astype(jnp.bfloat16), 'tensor', axis=0, tiled=...]
    psum x1 -> x0, blocking collectives: 42.3 us -> none  [per_device(): lax.psum((grad_fgain, grad_fbias, grad_sgain, grad_sbias), ('dp', 'tensor'))]
    dot_general x8 -> x4, matrix products: 45.3 us -> 15.5 us  [product(): return jnp.dot(left, right, preferred_element_type=jnp.float32)]
    dot_general x8 -> x4, matrix products: 61.4 us -> 32.1 us  [product_nt(): lax.dot_general(left, right, (((1,), (1,)), ((), ())), preferred_element_...]
    convert_element_type x10 -> x4, other arithmetic: 36.9 us -> 14.5 us  [per_device(): item.astype(jnp.float32)]
  transfers between devices with their start and end apart: 9 -> 1, of which waited for: 9 -> 1; matrix products, arithmetic and copies ran while one was open for 7% -> 2% of each run, Pallas kernels for 0% -> 0%
where the time goes in v2:
time: 874 us; the launch traced here: 866 us
  Pallas kernels  568 us (65%)
  matrix products  111 us (13%)
  waiting for transfers between devices  65.9 us (8%)
  other arithmetic  64.2 us (7%)
  local copies, waits for them, and re-layouts  41.3 us (5%)
  between operations  15.1 us (2%)
    pallas_call x1, Pallas kernels, feed_forward(): pl.pallas_call(functools.partial(feed_kernel, size, chunks), out_shape=(b...  213 us
    pallas_call x1, Pallas kernels, last_sums(): pl.pallas_call(functools.partial(last_kernel, size, bits, chunks), out_sh...  186 us
    pallas_call x1, Pallas kernels, feed_back(): pl.pallas_call(functools.partial(back_kernel, size, bits, chunks), out_sh...  168 us
    all_gather x1, waiting for transfers between devices, per_device(): lax.all_gather(first_out.astype(jnp.bfloat16), 'tensor', axis=0, tiled=True)  65.9 us
    dot_general x8, matrix products, product_tn(): lax.dot_general(left, right, (((0,), (0,)), ((), ())), preferred_element_...  45.1 us
    dot_general x4, matrix products, product_nt(): lax.dot_general(left, right, (((1,), (1,)), ((), ())), preferred_element_...  32.1 us
  transfers between devices with their start and end apart: 1, of which 1 were waited for; matrix products, arithmetic and copies ran while one was open for 2% of the time, Pallas kernels for 0%

profile of v2, /device:TPU:0, one launch (start us, length us, event | category | flops | bytes accessed | tf_op | source)
XLA Modules:
  0.0 865.7 jit_solution(15804398788582381745)
XLA Ops:
  21.1 5.5 copy.59
  30.9 65.9 %all-gather.2.cloned.1.call-done = bf16[1024,2048]{1,0:T(8,128)(2,1)} async-done(((bf16[256,2048]{1,0:T(8,128)(2,1)}), bf16[1024,2048]{1,0:T(8,128)(2,1)}) %all-gather.2.cloned.1.call-update) | async-done | bytes 4194320 | tf_op jit(solution)/shard_map/all_gather | solution.py:1140
  96.8 5.4 convolution_convert_fusion.7
  133.7 213.0 %shard_map.254 = (bf16[4,256,2048]{2,1,0:T(8,128)(2,1)}, bf16[4,256,2048]{2,1,0:T(8,128)(2,1)}, bf16[4,256,864]{2,1,0:T(8,128)(2,1)}, bf16[4,256,864]{2,1,0:T(8,...) custom-call(bf16[4,256,864]{2,1,0:T(8,128)(2,1)} %copy.61.mixed_hbm,, ...), custom_call_target="tpu_custom_call" | custom-call | flops 25367150592 | bytes 67108864 | tf_op jit(solution)/shard_map/pallas_call | solution.py:674
  346.7 8.6 bitcast_convert_fusion.1.grads_hbm_1_
  355.3 5.3 bitcast_convert_fusion.grads_hbm_2_
  360.6 5.3 bitcast_convert_fusion.2.grads_hbm_0_
  365.8 168.5 %shard_map.255 = (bf16[4,256,2048]{2,1,0:T(8,128)(2,1)}, f32[4,256,864]{2,1,0:T(8,128)}, f32[256,2048]{1,0:T(8,128)}, f32[8,2048]{1,0:T(8,128)}, bf16[864,2048]{...) custom-call(bf16[4,256,2048]{2,1,0:T(8,128)(2,1)} %get-tuple-element.37.dsecond_hbm, ...), custom_call_target="tpu_custom_call" | custom-call | flops 3623878656 | bytes 67108864 | tf_op jit(solution)/shard_map/pallas_call | solution.py:872
  534.3 7.5 reshape.417
  541.8 7.1 copy.78
  548.9 5.7 multiply_reduce_fusion.1
  554.7 5.5 fusion.20
  563.6 5.9 multiply_reduce_fusion
  577.7 6.8 fusion.26
  584.5 6.8 fusion.25
  595.2 5.7 fusion.24
  600.9 5.4 convolution_convert_fusion.2.grads_hbm_0_
  606.3 12.8 %add_convert_fusion = bf16[1024,2048]{1,0:T(8,128)(2,1)} fusion(f32[1024,2048]{1,0:T(8,128)} %fusion.26, f32[1024,2048]{1,0:T(8,128)} %fusion.25, f32[1024,2048]{1,0:T(8,128)} %fusion.24, bf16[1024,512]{0,1:T(8,128)(2,1)S(1)} %bitcast.126, bf16[2048,512]{1,0:T(8,128)(2,1)S(1)} %copy-done.18), kind=kOutput, calls=%fused_computation | convolution fusion | flops 2155872256 | bytes 32505856 | tf_op jit(solution)/shard_map/dot_general | solution.py:68
  619.1 6.1 convolution_convert_fusion.3.grads_hbm_4_
  628.9 5.3 convolution_convert_fusion.1.grads_hbm_1_
  634.1 5.5 convolution_convert_fusion.grads_hbm_2_
  639.6 186.5 %shard_map.256 = (bf16[256,2048]{1,0:T(8,128)(2,1)}, f32[256,2048]{1,0:T(8,128)}, f32[8,2048]{1,0:T(8,128)}, bf16[864,2048]{1,0:T(8,128)(2,1)}, bf16[864,2048]{1...) custom-call(bf16[4,256,2048]{2,1,0:T(8,128)(2,1)} %bitcast.118, ...), custom_call_target="tpu_custom_call" | custom-call | flops 1073741824 | bytes 67108864 | tf_op jit(solution)/shard_map/pallas_call | solution.py:1081
  839.0 9.1 %convert_bitcast_fusion.2 = (f32[2048,864]{0,1:T(8,128)}, f32[2048,864]{0,1:T(8,128)}) fusion(bf16[864,2048]{1,0:T(8,128)(2,1)} %get-tuple-element.55, bf16[864,2048]{1,0:T(8,128)(2,1)S(1)} %copy-done.16), kind=kLoop, calls=%fused_computation.12 | loop fusion | flops 3538944 | bytes 21233664 | tf_op jit(solution)/shard_map/transpose | solution.py:1251
  848.2 7.0 convert_bitcast_fusion
  (143 shorter events, 84.5 us)
Async XLA Ops:
  7.2 110.0 %copy-start = (bf16[2048,864]{0,1:T(8,128)(2,1)S(1)}, bf16[2048,864]{0,1:T(8,128)(2,1)}, u32[]{:S(2)}) copy-start(bf16[2048,864]{0,1:T(8,128)(2,1)} %param.21) | copy-start | bytes 10616836
  7.2 6.0 copy-start.32
  7.2 89.6 %all-gather.2.cloned.1.call-start = ((), (), s32[]{:S(2)}) async-start(), calls=%async_computation | async-start | bytes 5242880 | tf_op jit(solution)/shard_map/all_gather | solution.py:1140
  26.7 78.0 %copy-start.33 = (f32[2]{0:T(128)}, f32[2]{0:T(128)S(1)}, u32[]{:S(2)}) copy-start(f32[2]{0:T(128)S(1)} %negate_log-plus-one_fusion) | copy-start | bytes 28
  30.9 73.9 %copy-start.28 = (f32[2,1024]{1,0:T(2,128)}, f32[2,1024]{1,0:T(2,128)S(1)}, u32[]{:S(2)}) copy-start(f32[2,1024]{1,0:T(2,128)S(1)} %rsqrt.39) | copy-start | bytes 24580
  346.6 8.6 copy-start.46
  346.7 8.6 copy-start.48
  548.9 5.8 copy-start.25
  548.9 5.8 copy-start.2
  548.9 5.8 copy-start.27
  548.9 11.4 %slice-start = ((s8[8388608]{0:T(1024)(128)(4,1)}), s8[4194304]{0:T(1024)(128)(4,1)S(1)}, s32[]{:S(2)}) async-start(s8[8388608]{0:T(1024)(128)(4,1)} %bitcast.113), calls=%async_computation.1 | async-start | bytes 8388608
  563.6 6.0 copy-start.31
  563.6 6.0 copy-start.5
  563.6 6.0 copy-start.8
  563.6 6.0 copy-start.29
  563.6 6.0 copy-start.34
  577.7 6.8 copy-start.22
  577.7 6.8 copy-start.39
  584.5 6.8 copy-start.12
  619.1 6.1 copy-start.36
  826.1 5.9 copy-start.19
  839.0 9.2 %copy-start.14 = (bf16[864,2048]{1,0:T(8,128)(2,1)S(1)}, bf16[864,2048]{1,0:T(8,128)(2,1)}, u32[]{:S(2)}) copy-start(bf16[864,2048]{1,0:T(8,128)(2,1)} %get-tuple-element.57) | copy-start | bytes 10616836
  839.0 9.2 %copy-start.15 = (bf16[864,2048]{1,0:T(8,128)(2,1)S(1)}, bf16[864,2048]{1,0:T(8,128)(2,1)}, u32[]{:S(2)}) copy-start(bf16[864,2048]{1,0:T(8,128)(2,1)} %get-tuple-element.58) | copy-start | bytes 10616836
  848.2 7.0 copy-start.23
  (28 other events, 107.5 us)
Sparse Core Ops, SparseCore 0:
  13.3 83.4 all-gather.1

commit v3 on v2

--- a/solution.py
+++ b/solution.py
@@ -171,21 +171,25 @@
             for target in range(self.size - 1):
                 self.go_left(chunk, target)
 
-    def put(self, chunk, step):
-        size, me = self.size, self.me
-        right, left = size - 1 - step, step
-
-        @pl.when((me < right) & (me > 0))
+    def right(self, chunk, target):
+        @pl.when((self.me < target) & (self.me > 0))
         def _():
-            self.copy(right, right, chunk, me).wait_recv()
-            self.add(right, chunk)
-            self.go_right(chunk, right)
-
-        @pl.when((me > left) & (me < size - 1))
+            self.copy(target, target, chunk, self.me).wait_recv()
+            self.add(target, chunk)
+            self.go_right(chunk, target)
+
+    def left(self, chunk, target):
+        @pl.when((self.me > target) & (self.me < self.size - 1))
         def _():
-            self.copy(left, left, chunk, me).wait_recv()
-            self.add(left, chunk)
-            self.go_left(chunk, left)
+            self.copy(target, target, chunk, self.me).wait_recv()
+            self.add(target, chunk)
+            self.go_left(chunk, target)
+
+    def calls(self, chunk):
+        for step in range(self.size - 1):
+            if step < self.size - 2:
+                yield functools.partial(self.right, chunk, self.size - 1 - step)
+                yield functools.partial(self.left, chunk, step)
 
     def arrive(self, chunk):
         size, me = self.size, self.me
@@ -229,7 +233,11 @@
             device_id_type=MESH,
         )
 
-    def put(self, chunk, step):
+    def begin(self, chunk):
+        self.right(chunk, 0)
+        self.left(chunk, 0)
+
+    def right(self, chunk, step):
         size, me = self.size, self.me
 
         @pl.when(me >= step)
@@ -241,6 +249,9 @@
             def _():
                 self.copy(me - step, chunk, 0, me + 1).start()
 
+    def left(self, chunk, step):
+        size, me = self.size, self.me
+
         @pl.when(me + step < size)
         def _():
             if step:
@@ -249,6 +260,11 @@
             @pl.when(me > 0)
             def _():
                 self.copy(me + step, chunk, 1, me - 1).start()
+
+    def calls(self, chunk):
+        for step in range(1, self.size):
+            yield functools.partial(self.right, chunk, step)
+            yield functools.partial(self.left, chunk, step)
 
     def drain(self, chunk):
         size, me = self.size, self.me
@@ -272,7 +288,6 @@
         self.free = free
         self.orders = (tuple(range(bits)), (0,) + tuple(range(bits - 1, 0, -1)))
         self.mine = [(me // 2**bit) % 2 for bit in range(bits)]
-        self.steps = 2 * bits + 1
 
     def partner(self, bit):
         return self.me + (1 - 2 * self.mine[bit]) * 2**bit
@@ -359,41 +374,51 @@
         for index, part, whole in self.slices(which, self.sources[which]):
             pltpu.make_async_copy(whole, part, self.load_sem.at[which, index]).start()
 
-    def step(self, which, stage):
-        bits = self.bits
-        if stage == 0:
-            for index, part, whole in self.slices(which, self.sources[which]):
-                pltpu.make_async_copy(whole, part, self.load_sem.at[which, index]).wait()
-            self.halve(which, 2, 0).start()
-        elif stage < bits:
-            if stage == 1:
-                self.land(which, 2, 0)
+    def open(self, which):
+        for index, part, whole in self.slices(which, self.sources[which]):
+            pltpu.make_async_copy(whole, part, self.load_sem.at[which, index]).wait()
+        self.halve(which, 2, 0).start()
+
+    def split(self, which):
+        self.land(which, 2, 0)
+        for color in range(2):
+            self.halve(which, color, 1).start()
+
+    def down(self, which, color, step):
+        self.land(which, color, step - 1)
+        self.halve(which, color, step).start()
+
+    def turn(self, which, color):
+        self.land(which, color, self.bits - 1)
+        self.grow(which, color, self.bits - 1)
+
+    def up(self, which, color, step):
+        self.double(which, color, step + 1).wait_recv()
+        self.grow(which, color, step)
+
+    def join(self, which):
+        for color in range(2):
+            self.double(which, color, 1).wait_recv()
+        self.grow(which, 2, 0)
+
+    def close(self, which):
+        self.double(which, 2, 0).wait_recv()
+        for index, part, whole in self.slices(which, self.results[which]):
+            pltpu.make_async_copy(part, whole, self.store_sem.at[which, index]).start()
+
+    def calls(self, which):
+        yield functools.partial(self.open, which)
+        yield functools.partial(self.split, which)
+        for step in range(2, self.bits):
             for color in range(2):
-                if stage > 1:
-                    self.land(which, color, stage - 1)
-                self.halve(which, color, stage).start()
-        elif stage < 2 * bits - 1:
-            back = 2 * bits - 1 - stage
+                yield functools.partial(self.down, which, color, step)
+        for color in range(2):
+            yield functools.partial(self.turn, which, color)
+        for step in range(self.bits - 2, 0, -1):
             for color in range(2):
-                if back == bits - 1:
-                    self.land(which, color, back)
-                else:
-                    self.double(which, color, back + 1).wait_recv()
-                self.grow(which, color, back)
-        elif stage == 2 * bits - 1:
-            for color in range(2):
-                self.double(which, color, 1).wait_recv()
-            self.grow(which, 2, 0)
-        else:
-            self.double(which, 2, 0).wait_recv()
-            for index, part, whole in self.slices(which, self.results[which]):
-                pltpu.make_async_copy(part, whole, self.store_sem.at[which, index]).start()
-
-    def calls(self):
-        for tick in range(len(self.parts) + self.steps - 1):
-            for stage in range(self.steps - 1, -1, -1):
-                if 0 <= tick - stage < len(self.parts):
-                    yield functools.partial(self.step, tick - stage, stage)
+                yield functools.partial(self.up, which, color, step)
+        yield functools.partial(self.join, which)
+        yield functools.partial(self.close, which)
 
     def drain(self):
         for which in range(len(self.parts)):
@@ -457,11 +482,78 @@
     ]
 
 
-def interleave(first, second):
-    places = [((index + 0.5) / len(first), call) for index, call in enumerate(first)]
-    places += [((index + 0.5) / len(second), call) for index, call in enumerate(second)]
-    for _, call in sorted(places, key=lambda item: item[0]):
-        call()
+ORDERS = {
+    ("feed", 4, 4): (
+        4, 6, 4, 0, 5, 4, 4, 0, 4, 6, 5, 0, 5, 0, 0, 2, 5, 6, 1, 2, 0, 3, 4, 4,
+        6, 1, 6, 7, 5, 0, 6, 1, 1, 5, 2, 0, 0, 1, 3, 2, 0, 1, 7, 3, 3, 0, 5, 1,
+        0, 2, 0, 1, 0, 3, 2, 0, 0, 1, 1, 1, 3, 0, 1, 1, 1, 2, 2, 1, 1, 2, 1, 6,
+        0, 2, 3, 3, 2, 7, 7, 2, 2, 2, 3, 2, 2, 1, 3, 3, 7, 0, 0, 2, 3, 3, 1, 2,
+        7, 1, 7, 0, 3, 1, 3, 3, 3, 3, 2, 2, 0, 3, 2, 3, 3, 2, 1, 3,
+    ),
+    ("back", 4, 4, 3): (
+        0, 8, 9, 4, 10, 1, 5, 2, 8, 9, 4, 3, 10, 8, 8, 6, 0, 1, 9, 9, 4, 0, 1, 0,
+        10, 10, 5, 8, 4, 8, 9, 0, 2, 9, 3, 5, 10, 8, 8, 2, 0, 10, 0, 9, 0, 9, 7, 3,
+        1, 6, 1, 5, 6, 5, 1, 8, 4, 1, 3, 2, 10, 10, 7, 6, 3, 2, 7, 3, 9, 6, 7, 1,
+        2, 3, 8, 10, 5, 4, 2, 6, 7, 2, 9, 3, 10, 7,
+    ),
+    ("last", 4, 4, 3): (
+        7, 0, 4, 7, 4, 6, 0, 6, 4, 5, 2, 4, 3, 0, 6, 6, 8, 1, 0, 0, 7, 4, 5, 7,
+        2, 0, 6, 4, 8, 5, 7, 4, 6, 3, 8, 5, 1, 4, 6, 1, 8, 7, 7, 6, 5, 3, 1, 2,
+        2, 5, 8, 2, 1, 3, 8, 5, 7, 4, 3, 1, 2, 8, 5, 6, 3, 7, 9, 4, 8, 9, 5, 7,
+        9, 8, 6, 5, 8,
+    ),
+    ("feed", 4, 8): (
+        11, 10, 13, 8, 9, 13, 1, 8, 13, 8, 10, 0, 14, 10, 12, 8, 13, 10, 13, 0, 1, 10, 8, 11,
+        9, 12, 2, 14, 0, 0, 1, 1, 11, 8, 1, 3, 0, 9, 11, 9, 5, 12, 2, 1, 3, 10, 12, 11,
+        9, 14, 0, 8, 7, 6, 5, 1, 12, 0, 3, 3, 2, 2, 4, 5, 0, 0, 2, 9, 3, 9, 11, 15,
+        6, 14, 0, 1, 1, 0, 0, 2, 3, 4, 12, 0, 7, 5, 13, 1, 15, 2, 7, 0, 7, 0, 4, 0,
+        4, 6, 6, 10, 4, 2, 0, 2, 1, 12, 5, 1, 1, 1, 4, 1, 3, 1, 1, 2, 11, 3, 6, 2,
+        5, 2, 4, 13, 2, 3, 2, 2, 4, 7, 2, 3, 15, 0, 2, 6, 3, 4, 3, 15, 3, 3, 3, 5,
+        3, 4, 4, 3, 4, 5, 1, 4, 7, 4, 5, 4, 4, 2, 5, 5, 14, 6, 1, 1, 4, 7, 5, 5,
+        2, 5, 14, 5, 14, 0, 6, 1, 6, 4, 5, 6, 7, 5, 3, 6, 6, 6, 6, 7, 6, 5, 7, 2,
+        0, 7, 15, 3, 3, 6, 4, 15, 4, 6, 7, 7, 5, 5, 0, 15, 3, 2, 5, 7, 1, 4, 7, 6,
+        7, 7, 7, 6, 6, 3, 5, 7, 7, 6, 7, 6, 2, 0, 4, 7,
+    ),
+    ("back", 4, 8, 3): (
+        0, 16, 8, 1, 18, 0, 9, 2, 3, 16, 0, 17, 0, 4, 18, 5, 17, 8, 16, 6, 16, 9, 0, 18,
+        0, 3, 2, 18, 4, 1, 10, 9, 8, 6, 5, 17, 3, 6, 17, 11, 9, 6, 16, 12, 4, 3, 16, 18,
+        7, 18, 2, 5, 10, 17, 17, 11, 1, 16, 12, 16, 0, 3, 18, 2, 5, 18, 2, 5, 7, 8, 1, 10,
+        4, 13, 14, 3, 6, 10, 11, 11, 6, 15, 17, 1, 4, 1, 3, 5, 12, 8, 7, 10, 17, 14, 11, 2,
+        16, 1, 8, 12, 0, 2, 7, 9, 1, 2, 12, 7, 5, 6, 13, 3, 18, 15, 13, 4, 13, 10, 12, 14,
+        14, 4, 4, 11, 17, 15, 15, 7, 16, 13, 7, 18, 14, 5, 6, 13, 7, 15, 9, 14, 17, 15,
+    ),
+    ("last", 4, 8, 3): (
+        11, 0, 9, 11, 10, 8, 12, 6, 9, 11, 10, 3, 2, 0, 6, 11, 9, 5, 1, 11, 8, 3, 6, 12,
+        7, 0, 9, 4, 5, 12, 10, 11, 9, 6, 9, 10, 11, 2, 11, 12, 8, 7, 12, 1, 6, 4, 10, 9,
+        4, 2, 12, 8, 5, 2, 10, 2, 8, 9, 3, 4, 7, 1, 0, 8, 10, 3, 4, 11, 1, 8, 1, 10,
+        5, 0, 3, 5, 7, 0, 7, 8, 9, 1, 11, 2, 3, 4, 5, 6, 9, 12, 12, 10, 7, 13, 13, 8,
+        13, 12, 8, 10, 12,
+    ),
+}
+
+
+def run_streams(streams, order, after):
+    streams = [list(stream) for stream in streams]
+    done = [0] * len(streams)
+
+    def ready(stream):
+        place = done[stream]
+        return place < len(streams[stream]) and all(
+            done[other] >= count for other, count in after.get((stream, place), ())
+        )
+
+    def take(stream):
+        streams[stream][done[stream]]()
+        done[stream] += 1
+
+    if order is not None:
+        for stream in order:
+            assert ready(stream)
+            take(stream)
+    while any(done[index] < len(stream) for index, stream in enumerate(streams)):
+        for stream in range(len(streams)):
+            if ready(stream):
+                take(stream)
 
 
 def feed_kernel(
@@ -481,9 +573,11 @@
     inner_hbm,
     dgate_hbm,
     dlin_hbm,
-    dsecond_hbm,
     outp_hbm,
     middle_ref,
+    dmiddle_ref,
+    branch_ref,
+    sums_ref,
     mixed,
     out_weight,
     tokens,
@@ -505,6 +599,8 @@
     store_sem,
     rs_send,
     rs_recv,
+    back_send,
+    back_recv,
     ag_send,
     ag_recv,
     seed_send,
@@ -532,6 +628,7 @@
         load.start()
     enter((), (size, me))
     scatter = LineScatter(size, me, rows, part, inbox, rs_send, rs_recv)
+    scatter_back = LineScatter(size, me, rows, part, inbox, back_send, back_recv)
     gather = LineGather(size, me, rows, second, ag_send, ag_recv)
     gather_seed = LineGather(size, me, rows, seeds, seed_send, seed_recv)
 
@@ -550,12 +647,21 @@
             (inner.at[slot], inner_hbm),
             (dgate.at[slot], dgate_hbm),
             (dlin.at[slot], dlin_hbm),
-            (wide.at[slot, 0], dsecond_hbm),
-            (wide.at[slot, 1], outp_hbm),
+            (wide.at[slot], outp_hbm),
         )[kind]
         return pltpu.make_async_copy(src, dst.at[:, at(chunk)], store_sem.at[kind, chunk])
 
+    waited = set()
+
+    def need(*indices):
+        for index in indices:
+            if index not in waited:
+                waited.add(index)
+                loads[index].wait()
+
     def project(chunk):
+        need(0, 1)
+
         def body(start, width):
             value = dot_nn(flat(mixed, chunk), out_weight[:, pl.ds(start, width)])
             part[:, at(chunk), pl.ds(start, width)] = value.astype(jnp.bfloat16).reshape(
@@ -563,8 +669,10 @@
             )
 
         for_columns(depth, body)
+        scatter.begin(chunk)
 
     def normalize(chunk):
+        need(3)
         scatter.arrive(chunk)
 
         def body(block):
@@ -577,23 +685,36 @@
             second[me, here, :] = value.astype(jnp.bfloat16)
 
         for_rows(rows, body)
-        gather.put(chunk, 0)
-
-    def feed(chunk):
+        gather.begin(chunk)
+
+    def feed_in(chunk):
+        need(4, 5)
+
+        def body(start, width):
+            columns = pl.ds(start, width)
+            gate_in[:, columns] = dot_nt(flat(second, chunk), hidden_gate[columns, :])
+            lin_in[:, columns] = dot_nt(flat(second, chunk), hidden_up[columns, :])
+
+        for_columns(hidden, body)
+        store(0, chunk).start()
+
+    def feed_seed(chunk):
+        need(6)
+
+        def body(start, width):
+            columns = pl.ds(start, width)
+            dinner[:, columns] = dot_nt(flat(seeds, chunk), hidden_down[columns, :])
+
+        for_columns(hidden, body)
+        store(1, chunk).start()
+
+    def feed_act(chunk):
         slot = chunk % 2
         if chunk >= 2:
-            for kind in range(2, 7):
+            for kind in range(2, 5):
                 store(kind, chunk - 2).wait()
-        def body_in(start, width):
-            columns = pl.ds(start, width)
-            left = flat(second, chunk)
-            gate_in[:, columns] = dot_nt(left, hidden_gate[columns, :])
-            lin_in[:, columns] = dot_nt(left, hidden_up[columns, :])
-            dinner[:, columns] = dot_nt(flat(seeds, chunk), hidden_down[columns, :])
-
-        for_columns(hidden, body_in)
-
-        def body_act(block):
+
+        def body(block):
             gate, lin, grad = gate_in[block, :], lin_in[block, :], dinner[block, :]
             cube = GELU_SCALE * (gate + 0.044715 * (gate * gate * gate))
             tanh = jnp.tanh(cube)
@@ -608,55 +729,87 @@
             dlin[slot, owner, inside, :] = (grad * active).astype(jnp.bfloat16)
             dgate[slot, owner, inside, :] = (grad * lin * slope).astype(jnp.bfloat16)
 
-        for_rows(size * rows, body_act)
-        def body_out(start, width):
+        for_rows(size * rows, body)
+        for kind in range(2, 5):
+            store(kind, chunk).start()
+
+    def feed_back(chunk):
+        slot = chunk % 2
+        scatter.drain(chunk)
+
+        def body(start, width):
             columns = pl.ds(start, width)
-            inner_all = inner[slot].reshape(size * rows, hidden)
             dgate_all = dgate[slot].reshape(size * rows, hidden)
             dlin_all = dlin[slot].reshape(size * rows, hidden)
             grad = dot_nn(dgate_all, hidden_gate[:, columns])
             grad = grad + dot_nn(dlin_all, hidden_up[:, columns])
-            wide[slot, 0, :, :, columns] = grad.astype(jnp.bfloat16).reshape(size, rows, width)
+            part[:, at(chunk), columns] = grad.astype(jnp.bfloat16).reshape(size, rows, width)
+
+        for_columns(depth, body)
+        scatter_back.begin(chunk)
+
+    def feed_out(chunk):
+        slot = chunk % 2
+        if chunk >= 2:
+            store(5, chunk - 2).wait()
+
+        def body(start, width):
+            columns = pl.ds(start, width)
+            inner_all = inner[slot].reshape(size * rows, hidden)
             value = dot_nn(inner_all, hidden_down[:, columns])
-            wide[slot, 1, :, :, columns] = value.astype(jnp.bfloat16).reshape(size, rows, width)
-
-        for_columns(depth, body_out)
-        for kind in range(7):
-            store(kind, chunk).start()
-
-    loads[2].wait()
-    gather_seed.put(0, 0)
-    loads[0].wait()
-    loads[1].wait()
-    project(0)
-    scatter.begin(0)
-    for tick in range(chunks + 1):
-        for step in range(size - 1):
-            if tick < chunks:
-                scatter.put(tick, step)
-            if tick:
-                gather.put(tick - 1, step + 1)
-            if tick < chunks and step:
-                gather_seed.put(tick, step)
-        if tick == 0:
-            loads[3].wait()
-        if tick < chunks:
-            normalize(tick)
-            gather_seed.put(tick, size - 1)
-        if tick < chunks - 1:
-            project(tick + 1)
-            scatter.begin(tick + 1)
-            gather_seed.put(tick + 1, 0)
-        if tick == 0:
-            for load in loads[4:]:
-                load.wait()
-        if tick:
-            feed(tick - 1)
+            wide[slot, :, :, columns] = value.astype(jnp.bfloat16).reshape(size, rows, width)
+
+        for_columns(depth, body)
+        store(5, chunk).start()
+
+    def normalize_back(chunk):
+        scatter_back.arrive(chunk)
+
+        def body(block):
+            here = pl.ds(chunk * rows + block.start, LINE)
+            middle = middle_ref[here, :]
+            centered = middle - jnp.mean(middle, axis=-1, keepdims=True)
+            scale = lax.rsqrt(jnp.mean(centered * centered, axis=-1, keepdims=True) + EPS)
+            normed = centered * scale
+            grad = scatter_back.total(here)
+            shaped = grad * gain_ref[...]
+            sums_ref[0:1, :] += jnp.sum(grad * normed, axis=0, keepdims=True)
+            sums_ref[1:2, :] += jnp.sum(grad, axis=0, keepdims=True)
+            dmiddle = seeds[me, here, :].astype(jnp.float32) + scale * (
+                shaped
+                - jnp.mean(shaped, axis=-1, keepdims=True)
+                - normed * jnp.mean(shaped * normed, axis=-1, keepdims=True)
+            )
+            dmiddle_ref[here, :] = dmiddle
+            branch_ref[here, :] = dmiddle.astype(jnp.bfloat16)
+
+        for_rows(rows, body)
+
+    def begin_seed(chunk):
+        need(2)
+        gather_seed.begin(chunk)
+
+    streams, after = [], {}
     for chunk in range(chunks):
-        scatter.drain(chunk)
+        steps = [project, *scatter.calls(chunk), normalize, *gather.calls(chunk)]
+        first_feed = len(steps)
+        steps += [feed_in, feed_seed, feed_act, feed_back, feed_out]
+        steps += [*scatter_back.calls(chunk), normalize_back]
+        streams.append(
+            [step if isinstance(step, functools.partial) else functools.partial(step, chunk) for step in steps]
+        )
+        if chunk:
+            after[chunk, first_feed] = ((chunk - 1, first_feed + 5),)
+        after[chunk, first_feed + 1] = ((chunks + chunk, 2 * size - 1),)
+    for chunk in range(chunks):
+        streams.append([functools.partial(begin_seed, chunk), *gather_seed.calls(chunk)])
+    sums_ref[...] = jnp.zeros_like(sums_ref)
+    run_streams(streams, ORDERS.get(("feed", size, chunks)), after)
+    for chunk in range(chunks):
+        scatter_back.drain(chunk)
         gather.drain(chunk)
         gather_seed.drain(chunk)
-        for kind in range(7 if chunk >= chunks - 2 else 2):
+        for kind in range(6 if chunk >= chunks - 2 else 2):
             store(kind, chunk).wait()
 
 
@@ -680,13 +833,15 @@
             blocks(hidden),
             blocks(hidden),
             blocks(depth),
-            blocks(depth),
             jax.ShapeDtypeStruct((own, depth), full),
+            jax.ShapeDtypeStruct((own, depth), full),
+            jax.ShapeDtypeStruct((own, depth), low),
+            jax.ShapeDtypeStruct((8, depth), full),
         ),
         in_specs=[pl.BlockSpec(memory_space=pl.ANY)] * 7
         + [pl.BlockSpec(memory_space=pltpu.VMEM)] * 2,
-        out_specs=(pl.BlockSpec(memory_space=pl.ANY),) * 7
-        + (pl.BlockSpec(memory_space=pltpu.VMEM),),
+        out_specs=(pl.BlockSpec(memory_space=pl.ANY),) * 6
+        + (pl.BlockSpec(memory_space=pltpu.VMEM),) * 4,
         scratch_shapes=[
             pltpu.VMEM((size, own, mixed.shape[-1]), low),
             pltpu.VMEM(out_weight.shape, low),
@@ -704,9 +859,11 @@
             pltpu.VMEM(thin, low),
             pltpu.VMEM(thin, low),
             pltpu.VMEM(thin, low),
-            pltpu.VMEM((2, 2, size, rows, depth), low),
+            pltpu.VMEM((2, size, rows, depth), low),
             dma((7,)),
-            dma((7, chunks)),
+            dma((6, chunks)),
+            dma((size, chunks)),
+            dma((size + 1, chunks)),
             dma((size, chunks)),
             dma((size + 1, chunks)),
             dma((2, size, chunks)),
@@ -727,16 +884,14 @@
     size,
     bits,
     chunks,
-    dsecond_hbm,
+    outp_hbm,
     out_hbm,
+    own_hbm,
     middle_ref,
-    seed_ref,
-    gain_ref,
     grads_hbm,
     branch_hbm,
     dmixed_hbm,
-    dmiddle_ref,
-    sums_ref,
+    output_ref,
     totals_hbm,
     part,
     out_weight,
@@ -759,10 +914,12 @@
     cube_free,
 ):
     me = lax.axis_index("tensor")
-    own, depth = seed_ref.shape
+    own, depth = middle_ref.shape
     rows = own // chunks
-    load_part = pltpu.make_async_copy(dsecond_hbm, part, load_sem.at[0])
-    load_out = pltpu.make_async_copy(out_hbm, out_weight, load_sem.at[1])
+    load_own = pltpu.make_async_copy(own_hbm, branch.at[me], load_sem.at[0])
+    load_part = pltpu.make_async_copy(outp_hbm, part, load_sem.at[1])
+    load_out = pltpu.make_async_copy(out_hbm, out_weight, load_sem.at[2])
+    load_own.start()
     load_part.start()
     cube = CubeSum(
         bits,
@@ -795,31 +952,18 @@
             src, dst = dmixed.at[chunk % 2], dmixed_hbm
         return pltpu.make_async_copy(src, dst.at[:, at(chunk)], store_sem.at[kind, chunk])
 
-    def normalize(chunk):
+    def finish(chunk):
         scatter.arrive(chunk)
 
         def body(block):
             here = pl.ds(chunk * rows + block.start, LINE)
-            middle = middle_ref[here, :]
-            centered = middle - jnp.mean(middle, axis=-1, keepdims=True)
-            scale = lax.rsqrt(jnp.mean(centered * centered, axis=-1, keepdims=True) + EPS)
-            normed = centered * scale
-            grad = scatter.total(here)
-            shaped = grad * gain_ref[...]
-            sums_ref[0:1, :] += jnp.sum(grad * normed, axis=0, keepdims=True)
-            sums_ref[1:2, :] += jnp.sum(grad, axis=0, keepdims=True)
-            dmiddle = seed_ref[here, :].astype(jnp.float32) + scale * (
-                shaped
-                - jnp.mean(shaped, axis=-1, keepdims=True)
-                - normed * jnp.mean(shaped * normed, axis=-1, keepdims=True)
-            )
-            dmiddle_ref[here, :] = dmiddle
-            branch[me, here, :] = dmiddle.astype(jnp.bfloat16)
+            output_ref[here, :] = (middle_ref[here, :] + scatter.total(here)).astype(jnp.bfloat16)
 
         for_rows(rows, body)
-        gather.put(chunk, 0)
 
     def unproject(chunk):
+        if chunk == 0:
+            load_out.wait()
         if chunk >= 2:
             store(1, chunk - 2).wait()
 
@@ -833,26 +977,31 @@
         for kind in range(2):
             store(kind, chunk).start()
 
-    def line_calls():
-        for tick in range(chunks + 1):
-            for step in range(size - 1):
-                if tick < chunks:
-                    yield functools.partial(scatter.put, tick, step)
-                if tick:
-                    yield functools.partial(gather.put, tick - 1, step + 1)
-            if tick < chunks - 1:
-                yield functools.partial(scatter.begin, tick + 1)
-            if tick < chunks:
-                yield functools.partial(normalize, tick)
-            if tick == 0:
-                yield load_out.wait
-            if tick:
-                yield functools.partial(unproject, tick - 1)
-
-    sums_ref[...] = jnp.zeros_like(sums_ref)
-    load_part.wait()
-    scatter.begin(0)
-    interleave(list(cube.calls()), list(line_calls()))
+    def begin_branch(chunk):
+        if chunk == 0:
+            load_own.wait()
+        gather.begin(chunk)
+
+    def begin_out(chunk):
+        if chunk == 0:
+            load_part.wait()
+        scatter.begin(chunk)
+
+    streams, after = [], {}
+    for chunk in range(chunks):
+        steps = [functools.partial(begin_branch, chunk), *gather.calls(chunk)]
+        if chunk:
+            after[chunk, 0] = ((chunk - 1, 1),)
+            after[chunk, len(steps)] = ((chunk - 1, len(steps) + 1),)
+        streams.append(steps + [functools.partial(unproject, chunk)])
+    for chunk in range(chunks):
+        steps = [functools.partial(begin_out, chunk), *scatter.calls(chunk)]
+        if chunk:
+            after[chunks + chunk, 0] = ((chunks + chunk - 1, 1),)
+        streams.append(steps + [functools.partial(finish, chunk)])
+    for which in range(len(cube_parts)):
+        streams.append(cube.calls(which))
+    run_streams(streams, ORDERS.get(("back", size, chunks, bits)), after)
     for chunk in range(chunks):
         scatter.drain(chunk)
         gather.drain(chunk)
@@ -861,8 +1010,8 @@
     cube.drain()
 
 
-def feed_back(size, bits, chunks, dsecond, out_weight, middle, cotangent, gain, grads):
-    own, depth = cotangent.shape
+def feed_back(size, bits, chunks, partial, out_weight, branch, middle, grads):
+    own, depth = middle.shape
     rows = own // chunks
     width = out_weight.shape[0]
     low, full = jnp.bfloat16, jnp.float32
@@ -874,19 +1023,18 @@
         out_shape=(
             jax.ShapeDtypeStruct((size, own, depth), low),
             jax.ShapeDtypeStruct((size, own, width), full),
-            jax.ShapeDtypeStruct((own, depth), full),
-            jax.ShapeDtypeStruct((8, depth), full),
+            jax.ShapeDtypeStruct((own, depth), low),
             [jax.ShapeDtypeStruct(grad.shape, low) for grad in grads],
         ),
-        in_specs=[anywhere, anywhere, vmem, vmem, vmem, many],
-        out_specs=(anywhere, anywhere, vmem, vmem, many),
+        in_specs=[anywhere, anywhere, anywhere, vmem, many],
+        out_specs=(anywhere, anywhere, vmem, many),
         scratch_shapes=[
             pltpu.VMEM((size, own, depth), low),
             pltpu.VMEM(out_weight.shape, low),
             pltpu.VMEM((size, own, depth), low),
             pltpu.VMEM((size + 1, own, depth), low),
             pltpu.VMEM((2, size, rows, width), full),
-            dma((2,)),
+            dma((3,)),
             dma((2, chunks)),
             dma((size, chunks)),
             dma((size + 1, chunks)),
@@ -900,7 +1048,7 @@
         cost_estimate=pl.CostEstimate(
             flops=2 * size * own * depth * width, bytes_accessed=2**26, transcendentals=0
         ),
-    )(dsecond, out_weight, middle, cotangent, gain, grads)
+    )(partial, out_weight, branch, middle, grads)
 
 
 def last_kernel(
@@ -908,21 +1056,16 @@
     bits,
     chunks,
     dfirst_hbm,
-    outp_hbm,
     tokens_ref,
-    middle_ref,
     dmiddle_ref,
     gain_ref,
     sums_ref,
     grads_hbm,
-    output_ref,
     dtokens_ref,
     totals_ref,
     totals_hbm,
     first_part,
     first_inbox,
-    out_part,
-    out_inbox,
     line_box,
     dp_box,
     load_sem,
@@ -932,8 +1075,6 @@
     dp_recv,
     rs_send,
     rs_recv,
-    out_send,
-    out_recv,
     cube_parts,
     cube_firsts,
     cube_nexts,
@@ -948,7 +1089,6 @@
     own = tokens_ref.shape[0]
     rows = own // chunks
     load_first = pltpu.make_async_copy(dfirst_hbm, first_part, load_sem.at[0])
-    load_out = pltpu.make_async_copy(outp_hbm, out_part, load_sem.at[1])
     load_first.start()
     cube = CubeSum(
         bits,
@@ -966,13 +1106,11 @@
     )
     for which in range(len(cube_parts)):
         cube.load(which)
-    load_out.start()
     groups = 2**bits
     peers = [{"dp": (mine + step) % groups} for step in range(1, groups)]
     others = [{"tensor": (me + step) % size} for step in range(1, size)]
     enter(peers + others, None)
     first = LineScatter(size, me, rows, first_part, first_inbox, rs_send, rs_recv)
-    last = LineScatter(size, me, rows, out_part, out_inbox, out_send, out_recv)
 
     def back(chunk):
         first.arrive(chunk)
@@ -995,15 +1133,6 @@
 
         for_rows(rows, body)
 
-    def finish(chunk):
-        last.arrive(chunk)
-
-        def body(block):
-            here = pl.ds(chunk * rows + block.start, LINE)
-            output_ref[here, :] = (middle_ref[here, :] + last.total(here)).astype(jnp.bfloat16)
-
-        for_rows(rows, body)
-
     def line_copy(step, slot):
         return pltpu.make_async_remote_copy(
             src_ref=line_box.at[me],
@@ -1040,31 +1169,24 @@
             dp_copy(step, (mine + step) % groups).wait_recv()
         totals_ref[...] = jnp.sum(dp_box[...], axis=0)
 
-    def line_calls():
-        yield functools.partial(first.begin, 0)
-        for chunk in range(chunks):
-            for step in range(size - 1):
-                yield functools.partial(first.put, chunk, step)
-            yield functools.partial((first if chunk < chunks - 1 else last).begin, (chunk + 1) % chunks)
-            yield functools.partial(back, chunk)
-        yield sums_on_line
-        for chunk in range(chunks):
-            for step in range(size - 1):
-                yield functools.partial(last.put, chunk, step)
-            if chunk < chunks - 1:
-                yield functools.partial(last.begin, chunk + 1)
-            yield functools.partial(finish, chunk)
-            if chunk == 0:
-                yield sums_on_dp
-        yield sums_done
-
     line_box[me] = sums_ref[...]
     load_first.wait()
-    load_out.wait()
-    interleave(list(cube.calls()), list(line_calls()))
+    streams = []
+    for chunk in range(chunks):
+        streams.append(
+            [
+                functools.partial(first.begin, chunk),
+                *first.calls(chunk),
+                functools.partial(back, chunk),
+            ]
+        )
+    after = {(chunks + len(cube_parts), 0): [(chunk, 2 * size - 2) for chunk in range(chunks)]}
+    for which in range(len(cube_parts)):
+        streams.append(cube.calls(which))
+    streams.append([sums_on_line, sums_on_dp, sums_done])
+    run_streams(streams, ORDERS.get(("last", size, chunks, bits)), after)
     for chunk in range(chunks):
         first.drain(chunk)
-        last.drain(chunk)
     for step in range(1, size):
         line_copy(step, me).wait_send()
     for step in range(1, groups):
@@ -1072,7 +1194,7 @@
     cube.drain()
 
 
-def last_sums(size, bits, chunks, dfirst, partial, tokens, middle, dmiddle, gain, sums, grads):
+def last_sums(size, bits, chunks, dfirst, tokens, dmiddle, gain, sums, grads):
     own, depth = tokens.shape
     low, full = jnp.bfloat16, jnp.float32
     dma = pltpu.SemaphoreType.DMA
@@ -1081,27 +1203,22 @@
     return pl.pallas_call(
         functools.partial(last_kernel, size, bits, chunks),
         out_shape=(
-            jax.ShapeDtypeStruct((own, depth), low),
             jax.ShapeDtypeStruct((own, depth), full),
             jax.ShapeDtypeStruct((8, depth), full),
             [jax.ShapeDtypeStruct(grad.shape, low) for grad in grads],
         ),
-        in_specs=[anywhere, anywhere, vmem, vmem, vmem, vmem, vmem, many],
-        out_specs=(vmem, vmem, vmem, many),
+        in_specs=[anywhere, vmem, vmem, vmem, vmem, many],
+        out_specs=(vmem, vmem, many),
         scratch_shapes=[
-            pltpu.VMEM((size, own, depth), low),
-            pltpu.VMEM((size + 1, own, depth), low),
             pltpu.VMEM((size, own, depth), low),
             pltpu.VMEM((size + 1, own, depth), low),
             pltpu.VMEM((size, 8, depth), full),
             pltpu.VMEM((2**bits, 8, depth), full),
-            dma((2,)),
+            dma((1,)),
             dma((size,)),
             dma((size,)),
             dma((2**bits,)),
             dma((2**bits,)),
-            dma((size, chunks)),
-            dma((size + 1, chunks)),
             dma((size, chunks)),
             dma((size + 1, chunks)),
         ]
@@ -1110,7 +1227,7 @@
             collective_id=2, has_side_effects=True, vmem_limit_bytes=VMEM_BYTES
         ),
         cost_estimate=pl.CostEstimate(flops=2**30, bytes_accessed=2**26, transcendentals=0),
-    )(dfirst, partial, tokens, middle, dmiddle, gain, sums, grads)
+    )(dfirst, tokens, dmiddle, gain, sums, grads)
 
 
 def per_device(
@@ -1169,7 +1286,18 @@
     size = lax.axis_size("tensor")
     bits = lax.axis_size("dp").bit_length() - 1
     own = tokens.shape[0]
-    second_all, seed_all, inner, gate_in_low, lin_in_low, grad_second, partial, middle = feed_forward(
+    (
+        second_all,
+        seed_all,
+        inner,
+        gate_in_low,
+        lin_in_low,
+        partial,
+        middle,
+        grad_middle,
+        branch,
+        second_sums,
+    ) = feed_forward(
         size,
         CHUNKS,
         mixed.reshape(size, own, head_local * VD),
@@ -1192,8 +1320,8 @@
         product_tn(flat(gate_in_low), second_all).astype(jnp.bfloat16),
         product_tn(flat(lin_in_low), second_all).astype(jnp.bfloat16),
     ]
-    branch_all, grad_mixed, grad_middle, second_sums, feed_grads = feed_back(
-        size, bits, CHUNKS, grad_second, out_weight, middle, cotangent, second_gain[None], feed_grads
+    branch_all, grad_mixed, output, feed_grads = feed_back(
+        size, bits, CHUNKS, partial, out_weight, branch, middle, feed_grads
     )
     branch_all = flat(branch_all)
     grad_gates, grad_retained = mix_pull(grad_mixed.reshape(seq_count, seq_len, head_local, VD))
@@ -1229,14 +1357,12 @@
     total = total + product_nt(keys_back, key_weight)
     total = total + product_nt(values_low, value_weight)
     total = (total + product_nt(gates_low, gate_weight)).astype(jnp.bfloat16)
-    output, grad_tokens, sums, grads = last_sums(
+    grad_tokens, sums, grads = last_sums(
         size,
         bits,
         CHUNKS,
         total.reshape(size, own, total.shape[-1]),
-        partial,
         tokens,
-        middle,
         grad_middle,
         first_gain[None],
         second_sums,

time: 874 us -> 784 us (0.90)
  Pallas kernels: 568 us -> 478 us
    pallas_call x1, Pallas kernels: 168 us -> 115 us  [feed_back(): pl.pallas_call(functools.partial(back_kernel, size, bits, chunks), out_sh...]
    pallas_call x1, Pallas kernels: 186 us -> 146 us  [last_sums(): pl.pallas_call(functools.partial(last_kernel, size, bits, chunks), out_sh...]
where the time goes in v3:
time: 784 us; the launch traced here: 776 us
  Pallas kernels  478 us (61%)
  matrix products  111 us (14%)
  waiting for transfers between devices  66 us (8%)
  other arithmetic  64.2 us (8%)
  local copies, waits for them, and re-layouts  41.4 us (5%)
  between operations  15.1 us (2%)
    pallas_call x1, Pallas kernels, feed_forward(): pl.pallas_call(functools.partial(feed_kernel, size, chunks), out_shape=(b...  217 us
    pallas_call x1, Pallas kernels, last_sums(): pl.pallas_call(functools.partial(last_kernel, size, bits, chunks), out_sh...  146 us
    pallas_call x1, Pallas kernels, feed_back(): pl.pallas_call(functools.partial(back_kernel, size, bits, chunks), out_sh...  115 us
    all_gather x1, waiting for transfers between devices, per_device(): lax.all_gather(first_out.astype(jnp.bfloat16), 'tensor', axis=0, tiled=True)  66 us
    dot_general x8, matrix products, product_tn(): lax.dot_general(left, right, (((0,), (0,)), ((), ())), preferred_element_...  45.1 us
    dot_general x4, matrix products, product_nt(): lax.dot_general(left, right, (((1,), (1,)), ((), ())), preferred_element_...  32.1 us
    transpose x2, other arithmetic, per_device(): grad_valuew, grad_gatew, grad_hgate, grad_hup = (item.T for item in (grad...  16.1 us
  transfers between devices with their start and end apart: 1, of which 1 were waited for; matrix products, arithmetic and copies ran while one was open for 2% of the time, Pallas kernels for 0%

profile of v3, /device:TPU:0, one launch (start us, length us, event | category | flops | bytes accessed | tf_op | source)
XLA Modules:
  0.0 776.2 jit_solution(13611543611328917563)
XLA Ops:
  21.1 5.5 copy.59
  30.9 66.0 %all-gather.2.cloned.1.call-done = bf16[1024,2048]{1,0:T(8,128)(2,1)} async-done(((bf16[256,2048]{1,0:T(8,128)(2,1)}), bf16[1024,2048]{1,0:T(8,128)(2,1)}) %all-gather.2.cloned.1.call-update) | async-done | bytes 4194320 | tf_op jit(solution)/shard_map/all_gather | solution.py:1257
  96.8 5.4 convolution_convert_fusion.7
  133.9 217.1 %shard_map.254 = (bf16[4,256,2048]{2,1,0:T(8,128)(2,1)}, bf16[4,256,2048]{2,1,0:T(8,128)(2,1)}, bf16[4,256,864]{2,1,0:T(8,128)(2,1)}, bf16[4,256,864]{2,1,0:T(8,...) custom-call(bf16[4,256,864]{2,1,0:T(8,128)(2,1)} %copy.61.mixed_hbm,, ...), custom_call_target="tpu_custom_call" | custom-call | flops 25367150592 | bytes 67108864 | tf_op jit(solution)/shard_map/pallas_call | solution.py:827
  351.0 8.6 %bitcast_convert_fusion.1.grads_hbm_1_ = bf16[864,2048]{1,0:T(8,128)(2,1)} fusion(bf16[4,256,864]{2,1,0:T(8,128)(2,1)} %get-tuple-element.42, bf16[4,256,2048]{2,1,0:T(8,128)(2,1)} %get-tuple-element.43), kind=kOutput, calls=%fused_computation.8 | convolution fusion | flops 3625648128 | bytes 9502720 | tf_op jit(solution)/shard_map/dot_general | solution.py:74
  359.6 5.3 bitcast_convert_fusion.grads_hbm_2_
  364.9 5.3 bitcast_convert_fusion.2.grads_hbm_0_
  370.2 115.1 %shard_map.255 = (bf16[4,256,2048]{2,1,0:T(8,128)(2,1)}, f32[4,256,864]{2,1,0:T(8,128)}, bf16[256,2048]{1,0:T(8,128)(2,1)}, bf16[864,2048]{1,0:T(8,128)(2,1)}, b...) custom-call(bf16[4,256,2048]{2,1,0:T(8,128)(2,1)} %get-tuple-element.37.outp_hbm, bf16[864,2048]{1,0:T(8,128)(2,1)} %out_hbm.3, ...), custom_call_target="tpu_custom_call" | custom-call | flops 3623878656 | bytes 67108864 | tf_op jit(solution)/shard_map/pallas_call | solution.py:1021
  485.3 7.5 reshape.417
  492.8 7.1 copy.78
  499.8 5.7 multiply_reduce_fusion.1
  505.7 5.5 fusion.20
  514.5 5.9 multiply_reduce_fusion
  528.6 6.8 fusion.26
  535.4 6.8 fusion.25
  546.1 5.7 fusion.24
  551.8 5.4 convolution_convert_fusion.2.grads_hbm_0_
  557.2 12.8 %add_convert_fusion = bf16[1024,2048]{1,0:T(8,128)(2,1)} fusion(f32[1024,2048]{1,0:T(8,128)} %fusion.26, f32[1024,2048]{1,0:T(8,128)} %fusion.25, f32[1024,2048]{1,0:T(8,128)} %fusion.24, bf16[1024,512]{0,1:T(8,128)(2,1)S(1)} %bitcast.126, bf16[2048,512]{1,0:T(8,128)(2,1)S(1)} %copy-done.17), kind=kOutput, calls=%fused_computation | convolution fusion | flops 2155872256 | bytes 32505856 | tf_op jit(solution)/shard_map/dot_general | solution.py:68
  570.0 6.1 convolution_convert_fusion.3.grads_hbm_4_
  579.8 5.3 convolution_convert_fusion.1.grads_hbm_1_
  585.1 5.5 convolution_convert_fusion.grads_hbm_2_
  590.6 146.0 %shard_map.256 = (f32[256,2048]{1,0:T(8,128)}, f32[8,2048]{1,0:T(8,128)}, bf16[864,2048]{1,0:T(8,128)(2,1)}, bf16[864,2048]{1,0:T(8,128)(2,1)}, bf16[864,2048]{1...) custom-call(bf16[4,256,2048]{2,1,0:T(8,128)(2,1)} %bitcast.118, bf16[256,2048]{1,0:T(8,128)(2,1)} %tokens_ref.1, ...), custom_call_target="tpu_custom_call" | custom-call | flops 1073741824 | bytes 67108864 | tf_op jit(solution)/shard_map/pallas_call | solution.py:1203
  749.5 9.1 %convert_bitcast_fusion.2 = (f32[2048,864]{0,1:T(8,128)}, f32[2048,864]{0,1:T(8,128)}) fusion(bf16[864,2048]{1,0:T(8,128)(2,1)} %get-tuple-element.55, bf16[864,2048]{1,0:T(8,128)(2,1)S(1)} %copy-done.16), kind=kLoop, calls=%fused_computation.12 | loop fusion | flops 3538944 | bytes 21233664 | tf_op jit(solution)/shard_map/transpose | solution.py:1377
  758.7 7.0 convert_bitcast_fusion
  (143 shorter events, 84.7 us)
Async XLA Ops:
  7.2 110.2 %copy-start = (bf16[2048,864]{0,1:T(8,128)(2,1)S(1)}, bf16[2048,864]{0,1:T(8,128)(2,1)}, u32[]{:S(2)}) copy-start(bf16[2048,864]{0,1:T(8,128)(2,1)} %param.21) | copy-start | bytes 10616836
  7.2 6.0 copy-start.31
  7.2 89.6 %all-gather.2.cloned.1.call-start = ((), (), s32[]{:S(2)}) async-start(), calls=%async_computation | async-start | bytes 5242880 | tf_op jit(solution)/shard_map/all_gather | solution.py:1257
  26.7 78.0 %copy-start.32 = (f32[2]{0:T(128)}, f32[2]{0:T(128)S(1)}, u32[]{:S(2)}) copy-start(f32[2]{0:T(128)S(1)} %negate_log-plus-one_fusion) | copy-start | bytes 28
  30.8 73.9 %copy-start.27 = (f32[2,1024]{1,0:T(2,128)}, f32[2,1024]{1,0:T(2,128)S(1)}, u32[]{:S(2)}) copy-start(f32[2,1024]{1,0:T(2,128)S(1)} %rsqrt.39) | copy-start | bytes 24580
  351.0 8.6 %copy-start.46 = (bf16[4,256,2048]{2,1,0:T(8,128)(2,1)S(1)}, bf16[4,256,2048]{2,1,0:T(8,128)(2,1)}, u32[]{:S(2)}) copy-start(bf16[4,256,2048]{2,1,0:T(8,128)(2,1)} %get-tuple-element.43) | copy-start | bytes 12582916
  351.0 8.6 %copy-start.48 = (bf16[4,256,864]{2,1,0:T(8,128)(2,1)S(1)}, bf16[4,256,864]{2,1,0:T(8,128)(2,1)}, u32[]{:S(2)}) copy-start(bf16[4,256,864]{2,1,0:T(8,128)(2,1)} %get-tuple-element.44) | copy-start | bytes 5308420
  499.8 5.8 copy-start.24
  499.8 5.8 copy-start.2
  499.8 5.8 copy-start.26
  499.8 11.4 %slice-start = ((s8[8388608]{0:T(1024)(128)(4,1)}), s8[4194304]{0:T(1024)(128)(4,1)S(1)}, s32[]{:S(2)}) async-start(s8[8388608]{0:T(1024)(128)(4,1)} %bitcast.113), calls=%async_computation.1 | async-start | bytes 8388608
  514.5 6.0 copy-start.30
  514.5 6.0 copy-start.5
  514.5 6.0 copy-start.8
  514.5 6.0 copy-start.28
  514.5 6.0 copy-start.33
  528.6 6.8 copy-start.21
  528.6 6.8 copy-start.38
  535.4 6.8 copy-start.12
  570.0 6.1 copy-start.35
  736.6 5.9 copy-start.18
  749.5 9.2 %copy-start.14 = (bf16[864,2048]{1,0:T(8,128)(2,1)S(1)}, bf16[864,2048]{1,0:T(8,128)(2,1)}, u32[]{:S(2)}) copy-start(bf16[864,2048]{1,0:T(8,128)(2,1)} %get-tuple-element.57) | copy-start | bytes 10616836
  749.5 9.2 %copy-start.15 = (bf16[864,2048]{1,0:T(8,128)(2,1)S(1)}, bf16[864,2048]{1,0:T(8,128)(2,1)}, u32[]{:S(2)}) copy-start(bf16[864,2048]{1,0:T(8,128)(2,1)} %get-tuple-element.58) | copy-start | bytes 10616836
  758.7 7.0 copy-start.22
  (28 other events, 107.9 us)
Sparse Core Ops, SparseCore 0:
  13.3 83.4 all-gather.1

commit v4 on v3

--- a/solution.py
+++ b/solution.py
@@ -21,53 +21,7 @@
 VMEM_BYTES = 60 * 2**20
 TILE = 256
 LINE = 16
-
-
-def norm_parts(rows, gain, bias):
-    centered = rows - jnp.mean(rows, axis=-1, keepdims=True)
-    scale = lax.rsqrt(jnp.mean(centered * centered, axis=-1, keepdims=True) + EPS)
-    normed = centered * scale
-    return (normed * gain + bias, normed, scale)
-
-
-def norm_back(grad_out, gain, normed, scale):
-    shaped = grad_out * gain
-    return scale * (
-        shaped
-        - jnp.mean(shaped, axis=-1, keepdims=True)
-        - normed * jnp.mean(shaped * normed, axis=-1, keepdims=True)
-    )
-
-
-def decay_table(segments, rates):
-    place = jnp.arange(segments.shape[-1], dtype=jnp.int32)
-    offset = place[:, None] - place[None, :]
-    same_doc = (segments[..., :, None] == segments[..., None, :]) & (offset >= 0)
-    distance = jnp.maximum(offset, 0).astype(jnp.float32)
-    decay = jnp.where(same_doc[..., None, :, :], jnp.exp(-rates[:, None, None] * distance), 0.0)
-    return decay * lax.rsqrt(jnp.sum(decay, axis=-1, keepdims=True))
-
-
-def normalize_scores(scores, table):
-    weighted = scores * table
-    total = jnp.sum(weighted, axis=-1, keepdims=True)
-    return weighted * lax.rsqrt(total * total + 1.0)
-
-
-def gated_norm(gates, retained):
-    centered = retained - jnp.mean(retained, axis=-1, keepdims=True)
-    normed = centered * lax.rsqrt(jnp.mean(centered * centered, axis=-1, keepdims=True) + GROUP_EPS)
-    return jax.nn.silu(gates) * normed
-
-
-def product(left, right):
-    return jnp.dot(left, right, preferred_element_type=jnp.float32)
-
-
-def product_nt(left, right):
-    return lax.dot_general(
-        left, right, (((1,), (1,)), ((), ())), preferred_element_type=jnp.float32
-    )
+BAND = 64
 
 
 def product_tn(left, right):
@@ -89,12 +43,12 @@
         body(full * TILE, width % TILE)
 
 
-def for_rows(count, body):
+def for_rows(count, body, size=LINE):
     def step(index, carry):
-        body(pl.ds(pl.multiple_of(index * LINE, LINE), LINE))
+        body(pl.ds(pl.multiple_of(index * size, LINE), size))
         return carry
 
-    lax.fori_loop(0, count // LINE, step, 0)
+    lax.fori_loop(0, count // size, step, 0)
 
 
 def dot_nn(left, right):
@@ -103,6 +57,10 @@
 
 def dot_nt(left, right):
     return lax.dot_general(left, right, (((1,), (1,)), ((), ())), preferred_element_type=jnp.float32)
+
+
+def dot_tn(left, right):
+    return lax.dot_general(left, right, (((0,), (0,)), ((), ())), preferred_element_type=jnp.float32)
 
 
 def enter(peers, line):
@@ -949,7 +907,9 @@
         if kind == 0:
             src, dst = branch.at[:, at(chunk)], branch_hbm
         else:
-            src, dst = dmixed.at[chunk % 2], dmixed_hbm
+            return pltpu.make_async_copy(
+                dmixed.at[chunk % 2], dmixed_hbm.at[:, :, at(chunk)], store_sem.at[kind, chunk]
+            )
         return pltpu.make_async_copy(src, dst.at[:, at(chunk)], store_sem.at[kind, chunk])
 
     def finish(chunk):
@@ -970,10 +930,11 @@
         def body(start, width):
             columns = pl.ds(start, width)
             left = branch[:, at(chunk), :].reshape(size * rows, depth)
-            value = dot_nt(left, out_weight[columns, :])
-            dmixed[chunk % 2, :, :, columns] = value.reshape(size, rows, width)
-
-        for_columns(out_weight.shape[0], body)
+            for head in range(dmixed.shape[1]):
+                value = dot_nt(left, out_weight[pl.ds(head * VD + start, width), :])
+                dmixed[chunk % 2, head, :, :, columns] = value.reshape(size, rows, width)
+
+        for_columns(VD, body)
         for kind in range(2):
             store(kind, chunk).start()
 
@@ -1022,7 +983,7 @@
         functools.partial(back_kernel, size, bits, chunks),
         out_shape=(
             jax.ShapeDtypeStruct((size, own, depth), low),
-            jax.ShapeDtypeStruct((size, own, width), full),
+            jax.ShapeDtypeStruct((width // VD, size, own, VD), full),
             jax.ShapeDtypeStruct((own, depth), low),
             [jax.ShapeDtypeStruct(grad.shape, low) for grad in grads],
         ),
@@ -1033,7 +994,7 @@
             pltpu.VMEM(out_weight.shape, low),
             pltpu.VMEM((size, own, depth), low),
             pltpu.VMEM((size + 1, own, depth), low),
-            pltpu.VMEM((2, size, rows, width), full),
+            pltpu.VMEM((2, width // VD, size, rows, VD), full),
             dma((3,)),
             dma((2, chunks)),
             dma((size, chunks)),
@@ -1230,6 +1191,501 @@
     )(dfirst, tokens, dmiddle, gain, sums, grads)
 
 
+def decay_rows(rate, column, row, first):
+    shape = (column.shape[0], row.shape[1])
+    here = first + lax.broadcasted_iota(jnp.int32, shape, 0)
+    offset = here - lax.broadcasted_iota(jnp.int32, shape, 1)
+    inside = (column == row) & (offset >= 0)
+    distance = jnp.maximum(offset, 0).astype(jnp.float32)
+    decay = jnp.where(inside, jnp.exp(-rate * distance), 0.0)
+    return decay * lax.rsqrt(jnp.sum(decay, axis=-1, keepdims=True))
+
+
+def group_parts(values):
+    centered = values - jnp.mean(values, axis=-1, keepdims=True)
+    scale = lax.rsqrt(jnp.mean(centered * centered, axis=-1, keepdims=True) + GROUP_EPS)
+    return centered * scale, scale
+
+
+def sigmoid(values):
+    return 1.0 / (1.0 + jnp.exp(-values))
+
+
+def first_kernel(
+    size,
+    chunks,
+    heads,
+    tokens_ref,
+    gain_ref,
+    bias_ref,
+    column_ref,
+    row_ref,
+    rates_ref,
+    query_hbm,
+    key_hbm,
+    value_hbm,
+    gate_hbm,
+    first_hbm,
+    queries_hbm,
+    keys_hbm,
+    values_hbm,
+    gates_hbm,
+    retained_hbm,
+    mixed_hbm,
+    table_hbm,
+    query_weight,
+    key_weight,
+    value_weight,
+    gate_weight,
+    first,
+    queries,
+    keys,
+    values,
+    gates,
+    retained,
+    mixed,
+    table,
+    raw,
+    retain,
+    load_sem,
+    store_sem,
+    done_sem,
+    ag_send,
+    ag_recv,
+):
+    me = lax.axis_index("tensor")
+    own, depth = tokens_ref.shape
+    rows = own // chunks
+    pairs = (
+        (query_hbm, query_weight),
+        (key_hbm, key_weight),
+        (value_hbm, value_weight),
+        (gate_hbm, gate_weight),
+    )
+    loads = [
+        pltpu.make_async_copy(src, dst, load_sem.at[index])
+        for index, (src, dst) in enumerate(pairs)
+    ]
+    for load in loads:
+        load.start()
+    enter((), (size, me))
+    gather = LineGather(size, me, rows, first, ag_send, ag_recv)
+    waited = set()
+
+    def need(index):
+        if index not in waited:
+            waited.add(index)
+            loads[index].wait()
+
+    def at(chunk):
+        return pl.ds(chunk * rows, rows)
+
+    def flat(chunk):
+        return first[:, at(chunk), :].reshape(size * rows, depth)
+
+    def store(kind, block):
+        src, dst = (
+            (queries, queries_hbm),
+            (keys, keys_hbm),
+            (first, first_hbm),
+            (mixed, mixed_hbm),
+        )[kind]
+        return pltpu.make_async_copy(src.at[block], dst.at[block], store_sem.at[kind, block])
+
+    def store_head(kind, head, block):
+        src, dst = (
+            (values, values_hbm),
+            (gates, gates_hbm),
+            (retained, retained_hbm),
+            (table, table_hbm),
+        )[kind]
+        return pltpu.make_async_copy(
+            src.at[head, block], dst.at[head, block], done_sem.at[kind, head, block]
+        )
+
+    def normalize(chunk):
+        def body(block):
+            here = pl.ds(chunk * rows + block.start, LINE)
+            tokens = tokens_ref[here, :].astype(jnp.float32)
+            centered = tokens - jnp.mean(tokens, axis=-1, keepdims=True)
+            scale = lax.rsqrt(jnp.mean(centered * centered, axis=-1, keepdims=True) + EPS)
+            value = centered * scale * gain_ref[...] + bias_ref[...]
+            first[me, here, :] = value.astype(jnp.bfloat16)
+
+        for_rows(rows, body)
+        gather.begin(chunk)
+
+    def project_pair(chunk):
+        need(0)
+        need(1)
+
+        def body(start, width):
+            columns = pl.ds(start, width)
+            value = dot_nn(flat(chunk), query_weight[:, columns])
+            queries[:, at(chunk), columns] = value.astype(jnp.bfloat16).reshape(size, rows, width)
+            value = dot_nn(flat(chunk), key_weight[:, columns])
+            keys[:, at(chunk), columns] = value.astype(jnp.bfloat16).reshape(size, rows, width)
+
+        for_columns(heads * KD, body)
+
+    def project_value(chunk, head):
+        need(2)
+
+        def body(start, width):
+            weight = value_weight[pl.ds(head * VD + start, width), :]
+            value = dot_nt(flat(chunk), weight).astype(jnp.bfloat16)
+            values[head, :, at(chunk), pl.ds(start, width)] = value.reshape(size, rows, width)
+
+        for_columns(VD, body)
+
+    def project_gate(chunk, head):
+        need(3)
+
+        def body(start, width):
+            weight = gate_weight[pl.ds(head * VD + start, width), :]
+            value = dot_nt(flat(chunk), weight)
+            gates[head, :, at(chunk), pl.ds(start, width)] = value.reshape(size, rows, width)
+
+        for_columns(VD, body)
+
+    def tabulate(head, block):
+        seen = (block + 1) * own
+
+        def body(part):
+            there = pl.ds(block * own + part.start, part.size)
+            table[head, block, part, :seen] = decay_rows(
+                rates_ref[head], column_ref[there, :], row_ref[:, :seen], block * own + part.start
+            )
+
+        for_rows(own, body, BAND)
+        store_head(3, head, block).start()
+
+    def attend(head, block):
+        seen = (block + 1) * own
+        lanes = pl.ds(head * KD, KD)
+        query = queries[block, :, lanes]
+        raw[:, :seen] = dot_nt(query, keys[: block + 1, :, lanes].reshape(seen, KD))
+
+        def body(part):
+            weighted = raw[part, :seen] * (KD**-0.5) * table[head, block, part, :seen]
+            total = jnp.sum(weighted, axis=-1, keepdims=True)
+            retain[part, :seen] = (weighted * lax.rsqrt(total * total + 1.0)).astype(jnp.bfloat16)
+
+        for_rows(own, body, BAND)
+        value = values[head, : block + 1].reshape(seen, VD)
+        retained[head, block] = dot_nn(retain[:, :seen], value)
+
+        def body_mix(part):
+            normed, _ = group_parts(retained[head, block, part, :])
+            gate = gates[head, block, part, :]
+            value = (gate * sigmoid(gate) * normed).astype(jnp.bfloat16)
+            mixed[block, part, pl.ds(head * VD, VD)] = value
+
+        for_rows(own, body_mix, BAND)
+        store_head(2, head, block).start()
+        if head == heads - 1:
+            store(3, block).start()
+
+    streams, after = [], {}
+    for chunk in range(chunks):
+        steps = [functools.partial(normalize, chunk), *gather.calls(chunk)]
+        if chunk:
+            after[chunk, 0] = ((chunk - 1, 1),)
+        steps.append(functools.partial(project_pair, chunk))
+        for head in range(heads):
+            steps.append(functools.partial(project_value, chunk, head))
+            steps.append(functools.partial(project_gate, chunk, head))
+        streams.append(steps)
+    streams.append(
+        [functools.partial(tabulate, head, block) for head in range(heads) for block in range(size)]
+    )
+    run_streams(streams, ORDERS.get(("first", size, chunks, heads)), after)
+    for block in range(size):
+        for kind in range(3):
+            store(kind, block).start()
+        for head in range(heads):
+            for kind in range(2):
+                store_head(kind, head, block).start()
+    for head in range(heads):
+        for block in range(size):
+            attend(head, block)
+    for chunk in range(chunks):
+        gather.drain(chunk)
+    for block in range(size):
+        for kind in range(4):
+            store(kind, block).wait()
+        for head in range(heads):
+            for kind in range(4):
+                store_head(kind, head, block).wait()
+
+
+def first_part(size, chunks, tokens, gain, bias, segments, rates, query, key, value, gate):
+    own, depth = tokens.shape
+    heads = query.shape[1] // KD
+    rows = size * own
+    low, full = jnp.bfloat16, jnp.float32
+    dma = pltpu.SemaphoreType.DMA
+    vmem, anywhere = pl.BlockSpec(memory_space=pltpu.VMEM), pl.BlockSpec(memory_space=pl.ANY)
+    shapes = (
+        ((size, own, depth), low),
+        ((size, own, heads * KD), low),
+        ((size, own, heads * KD), low),
+        ((heads, size, own, VD), low),
+        ((heads, size, own, VD), full),
+        ((heads, size, own, VD), full),
+        ((size, own, heads * VD), low),
+        ((heads, size, own, rows), full),
+    )
+    return pl.pallas_call(
+        functools.partial(first_kernel, size, chunks, heads),
+        out_shape=tuple(jax.ShapeDtypeStruct(*item) for item in shapes),
+        in_specs=[vmem] * 5 + [pl.BlockSpec(memory_space=pltpu.SMEM)] + [anywhere] * 4,
+        out_specs=(anywhere,) * 8,
+        scratch_shapes=[pltpu.VMEM(item.shape, low) for item in (query, key, value, gate)]
+        + [pltpu.VMEM(*item) for item in shapes]
+        + [
+            pltpu.VMEM((own, rows), full),
+            pltpu.VMEM((own, rows), low),
+            dma((4,)),
+            dma((4, size)),
+            dma((4, heads, size)),
+            dma((2, size, chunks)),
+            dma((size, chunks)),
+        ],
+        compiler_params=pltpu.CompilerParams(
+            collective_id=3, has_side_effects=True, vmem_limit_bytes=VMEM_BYTES
+        ),
+        cost_estimate=pl.CostEstimate(flops=2**33, bytes_accessed=2**26, transcendentals=0),
+    )(
+        tokens,
+        gain,
+        bias,
+        segments.reshape(rows, 1),
+        segments.reshape(1, rows),
+        rates,
+        query,
+        key,
+        value,
+        gate,
+    )
+
+
+def retain_kernel(
+    size,
+    heads,
+    queries_hbm,
+    keys_hbm,
+    values_hbm,
+    gates_hbm,
+    retained_hbm,
+    dmixed_hbm,
+    table_hbm,
+    query_hbm,
+    key_hbm,
+    value_hbm,
+    gate_hbm,
+    dqueries_hbm,
+    dkeys_hbm,
+    dvalues_hbm,
+    dgates_hbm,
+    dfirst_hbm,
+    queries,
+    keys,
+    values,
+    gates,
+    retained,
+    dmixed,
+    table,
+    query_weight,
+    key_weight,
+    value_weight,
+    gate_weight,
+    dqueries,
+    dkeys,
+    dvalues,
+    dgates,
+    dfirst,
+    raw,
+    grad,
+    retain,
+    dscores,
+    dretained,
+    dkey_sum,
+    dvalue_sum,
+    load_sem,
+    block_sem,
+    store_sem,
+):
+    own = queries.shape[1]
+    depth = query_weight.shape[0]
+
+    def load_whole(kind):
+        src, dst = (
+            (queries_hbm, queries),
+            (keys_hbm, keys),
+            (query_hbm, query_weight),
+            (key_hbm, key_weight),
+            (value_hbm, value_weight),
+            (gate_hbm, gate_weight),
+        )[kind]
+        return pltpu.make_async_copy(src, dst, load_sem.at[kind])
+
+    def load_block(kind, head, block):
+        src, dst = (
+            (values_hbm, values),
+            (gates_hbm, gates),
+            (retained_hbm, retained),
+            (dmixed_hbm, dmixed),
+            (table_hbm, table),
+        )[kind]
+        return pltpu.make_async_copy(
+            src.at[head, block], dst.at[head, block], block_sem.at[kind, head, block]
+        )
+
+    def store(kind, block):
+        src, dst = (
+            (dqueries, dqueries_hbm),
+            (dkeys, dkeys_hbm),
+            (dvalues, dvalues_hbm),
+            (dgates, dgates_hbm),
+            (dfirst, dfirst_hbm),
+        )[kind]
+        return pltpu.make_async_copy(src.at[block], dst.at[block], store_sem.at[kind, block])
+
+    for kind in range(2):
+        load_whole(kind).start()
+    for head in range(heads):
+        for block in range(size):
+            for kind in range(5):
+                load_block(kind, head, block).start()
+    for kind in range(2, 6):
+        load_whole(kind).start()
+    for kind in range(2):
+        load_whole(kind).wait()
+
+    def attend(head, block):
+        seen = (block + 1) * own
+        lanes = pl.ds(head * KD, KD)
+
+        for kind in range(5):
+            load_block(kind, head, block).wait()
+
+        def body_mix(part):
+            normed, scale = group_parts(retained[head, block, part, :])
+            gate = gates[head, block, part, :]
+            dmix = dmixed[head, block, part, :]
+            half = sigmoid(gate)
+            dgate = dmix * normed * (half * (1.0 + gate * (1.0 - half)))
+            dgates[block, part, pl.ds(head * VD, VD)] = dgate.astype(jnp.bfloat16)
+            dnormed = dmix * (gate * half)
+            value = scale * (
+                dnormed
+                - jnp.mean(dnormed, axis=-1, keepdims=True)
+                - normed * jnp.mean(dnormed * normed, axis=-1, keepdims=True)
+            )
+            dretained[part, :] = value.astype(jnp.bfloat16)
+
+        for_rows(own, body_mix, BAND)
+        query = queries[block, :, lanes]
+        key = keys[: block + 1, :, lanes].reshape(seen, KD)
+        raw[:, :seen] = dot_nt(query, key)
+        value = values[head, : block + 1].reshape(seen, VD)
+        grad[:, :seen] = dot_nt(dretained[...], value)
+
+        def body(part):
+            decay = table[head, block, part, :seen]
+            weighted = raw[part, :seen] * (KD**-0.5) * decay
+            dretain = grad[part, :seen]
+            total = jnp.sum(weighted, axis=-1, keepdims=True)
+            along = jnp.sum(dretain * weighted, axis=-1, keepdims=True)
+            inverse = lax.rsqrt(total * total + 1.0)
+            retain[part, :seen] = (weighted * inverse).astype(jnp.bfloat16)
+            along = along * total * inverse * inverse
+            dscores[part, :seen] = (decay * inverse * (dretain - along)).astype(jnp.bfloat16)
+
+        for_rows(own, body, BAND)
+        dquery = dot_nn(dscores[:, :seen], key) * (KD**-0.5)
+        dqueries[block, :, lanes] = dquery.astype(jnp.bfloat16)
+        for other in range(block + 1):
+            there = pl.ds(other * own, own)
+            dkey = dot_tn(dscores[:, there], query)
+            dvalue = dot_tn(retain[:, there], dretained[...])
+            if other == block:
+                dkey_sum[other] = dkey
+                dvalue_sum[other] = dvalue
+            else:
+                dkey_sum[other] += dkey
+                dvalue_sum[other] += dvalue
+
+    for head in range(heads):
+        for block in range(size):
+            attend(head, block)
+
+        lanes = pl.ds(head * KD, KD)
+        for block in range(size):
+            dkeys[block, :, lanes] = (dkey_sum[block] * (KD**-0.5)).astype(jnp.bfloat16)
+            dvalues[block, :, pl.ds(head * VD, VD)] = dvalue_sum[block].astype(jnp.bfloat16)
+
+    for kind in range(2, 6):
+        load_whole(kind).wait()
+    for block in range(size):
+        for kind in range(4):
+            store(kind, block).start()
+
+        def body(start, width):
+            columns = pl.ds(start, width)
+            total = dot_nt(dqueries[block], query_weight[columns, :])
+            total = total + dot_nt(dkeys[block], key_weight[columns, :])
+            total = total + dot_nn(dvalues[block], value_weight[:, columns])
+            total = total + dot_nn(dgates[block], gate_weight[:, columns])
+            dfirst[block, :, columns] = total.astype(jnp.bfloat16)
+
+        for_columns(depth, body)
+        store(4, block).start()
+    for block in range(size):
+        for kind in range(5):
+            store(kind, block).wait()
+
+
+def retain_back(size, queries, keys, values, gates, retained, dmixed, table, query, key, value, gate):
+    own = queries.shape[1]
+    heads = values.shape[0]
+    rows, depth = size * own, query.shape[0]
+    low, full = jnp.bfloat16, jnp.float32
+    dma = pltpu.SemaphoreType.DMA
+    anywhere = pl.BlockSpec(memory_space=pl.ANY)
+    inputs = (queries, keys, values, gates, retained, dmixed, table, query, key, value, gate)
+    shapes = (
+        queries.shape,
+        keys.shape,
+        (size, own, heads * VD),
+        (size, own, heads * VD),
+        (size, own, depth),
+    )
+    return pl.pallas_call(
+        functools.partial(retain_kernel, size, heads),
+        out_shape=tuple(jax.ShapeDtypeStruct(shape, low) for shape in shapes),
+        in_specs=[anywhere] * len(inputs),
+        out_specs=(anywhere,) * 5,
+        scratch_shapes=[pltpu.VMEM(item.shape, item.dtype) for item in inputs]
+        + [pltpu.VMEM(shape, low) for shape in shapes]
+        + [
+            pltpu.VMEM((own, rows), full),
+            pltpu.VMEM((own, rows), full),
+            pltpu.VMEM((own, rows), low),
+            pltpu.VMEM((own, rows), low),
+            pltpu.VMEM((own, VD), low),
+            pltpu.VMEM((size, own, KD), full),
+            pltpu.VMEM((size, own, VD), full),
+            dma((6,)),
+            dma((5, heads, size)),
+            dma((5, size)),
+        ],
+        compiler_params=pltpu.CompilerParams(vmem_limit_bytes=VMEM_BYTES),
+        cost_estimate=pl.CostEstimate(flops=2**34, bytes_accessed=2**26, transcendentals=0),
+    )(*inputs)
+
+
 def per_device(
     tokens,
     first_gain,
@@ -1247,43 +1703,26 @@
     segments,
     cotangent,
 ):
-    seq_count, seq_len = segments.shape
-    group_rows = seq_count * seq_len
+    size = lax.axis_size("tensor")
+    group_rows = segments.size
     head_local = query_weight.shape[1] // KD
-    scale_factor = KD ** (-0.5)
-    inputs = tokens.astype(jnp.float32)
-    seed_all = lax.all_gather(cotangent, "tensor", axis=0, tiled=True)
-    first_out, first_normed, first_scale = norm_parts(inputs, first_gain, first_bias)
-    first_all = lax.all_gather(first_out.astype(jnp.bfloat16), "tensor", axis=0, tiled=True)
-    queries = product(first_all, query_weight).astype(jnp.bfloat16)
-    keys_low = product(first_all, key_weight).astype(jnp.bfloat16)
-    values = product(first_all, value_weight).astype(jnp.bfloat16)
-    gates = product(first_all, gate_weight)
     head_index = (lax.axis_index("tensor") * head_local + jnp.arange(head_local)).astype(
         jnp.float32
     )
     rates = -jnp.log1p(-jnp.exp2(-5.0 - head_index))
-    table = decay_table(segments, rates)
-    query_heads = queries.reshape(seq_count, seq_len, head_local, KD)
-    key_heads = keys_low.reshape(seq_count, seq_len, head_local, KD)
-    value_heads = values.reshape(seq_count, seq_len, head_local, VD)
-    scores = (
-        jnp.einsum("bnhk,bmhk->bhnm", query_heads, key_heads, preferred_element_type=jnp.float32)
-        * scale_factor
+    first_all, queries, keys, values, gates, retained, mixed, table = first_part(
+        size,
+        CHUNKS,
+        tokens,
+        first_gain[None],
+        first_bias[None],
+        segments,
+        rates,
+        query_weight,
+        key_weight,
+        value_weight.T,
+        gate_weight.T,
     )
-
-    def score_step(raw):
-        return normalize_scores(raw, table)
-
-    retain_full, score_pull = jax.vjp(score_step, scores)
-    retain = retain_full.astype(jnp.bfloat16)
-    retained = jnp.einsum(
-        "bhnm,bmhv->bnhv", retain, value_heads, preferred_element_type=jnp.float32
-    )
-    gate_heads = gates.reshape(seq_count, seq_len, head_local, VD)
-    mixed_full, mix_pull = jax.vjp(gated_norm, gate_heads, retained)
-    mixed = mixed_full.reshape(group_rows, head_local * VD).astype(jnp.bfloat16)
-    size = lax.axis_size("tensor")
     bits = lax.axis_size("dp").bit_length() - 1
     own = tokens.shape[0]
     (
@@ -1300,7 +1739,7 @@
     ) = feed_forward(
         size,
         CHUNKS,
-        mixed.reshape(size, own, head_local * VD),
+        mixed,
         out_weight,
         tokens,
         cotangent,
@@ -1324,44 +1763,34 @@
         size, bits, CHUNKS, partial, out_weight, branch, middle, feed_grads
     )
     branch_all = flat(branch_all)
-    grad_gates, grad_retained = mix_pull(grad_mixed.reshape(seq_count, seq_len, head_local, VD))
-    gates_low = grad_gates.reshape(group_rows, head_local * VD).astype(jnp.bfloat16)
-    retained_low = grad_retained.astype(jnp.bfloat16)
-    grad_retain = jnp.einsum(
-        "bnhv,bmhv->bhnm", retained_low, value_heads, preferred_element_type=jnp.float32
+    grad_queries, grad_keys, grad_values, grad_gates, grad_first = retain_back(
+        size,
+        queries,
+        keys,
+        values,
+        gates,
+        retained,
+        grad_mixed,
+        table,
+        query_weight,
+        key_weight,
+        value_weight.T,
+        gate_weight.T,
     )
-    grad_values = jnp.einsum(
-        "bhnm,bnhv->bmhv", retain, retained_low, preferred_element_type=jnp.float32
-    )
-    values_low = grad_values.reshape(group_rows, head_local * VD).astype(jnp.bfloat16)
-    (grad_scores,) = score_pull(grad_retain)
-    scores_low = grad_scores.astype(jnp.bfloat16)
-    grad_queries = (
-        jnp.einsum("bhnm,bmhk->bnhk", scores_low, key_heads, preferred_element_type=jnp.float32)
-        * scale_factor
-    )
-    grad_keys = (
-        jnp.einsum("bhnm,bnhk->bmhk", scores_low, query_heads, preferred_element_type=jnp.float32)
-        * scale_factor
-    )
-    queries_low = grad_queries.reshape(group_rows, head_local * KD).astype(jnp.bfloat16)
-    keys_back = grad_keys.reshape(group_rows, head_local * KD).astype(jnp.bfloat16)
+    first_all = flat(first_all)
+
     grads = [
-        product_tn(mixed, branch_all).astype(jnp.bfloat16),
-        product_tn(values_low, first_all).astype(jnp.bfloat16),
-        product_tn(gates_low, first_all).astype(jnp.bfloat16),
-        product_tn(first_all, queries_low).astype(jnp.bfloat16),
-        product_tn(first_all, keys_back).astype(jnp.bfloat16),
+        product_tn(flat(mixed), branch_all).astype(jnp.bfloat16),
+        product_tn(flat(grad_values), first_all).astype(jnp.bfloat16),
+        product_tn(flat(grad_gates), first_all).astype(jnp.bfloat16),
+        product_tn(first_all, flat(grad_queries)).astype(jnp.bfloat16),
+        product_tn(first_all, flat(grad_keys)).astype(jnp.bfloat16),
     ]
-    total = product_nt(queries_low, query_weight)
-    total = total + product_nt(keys_back, key_weight)
-    total = total + product_nt(values_low, value_weight)
-    total = (total + product_nt(gates_low, gate_weight)).astype(jnp.bfloat16)
     grad_tokens, sums, grads = last_sums(
         size,
         bits,
         CHUNKS,
-        total.reshape(size, own, total.shape[-1]),
+        grad_first,
         tokens,
         grad_middle,
         first_gain[None],

time: 784 us -> 726 us (0.926)
  Pallas kernels: 478 us -> 633 us
  waiting for transfers between devices: 66 us -> 0 us
  matrix products: 111 us -> 45.1 us
  other arithmetic: 64.2 us -> 29.7 us
  local copies, waits for them, and re-layouts: 41.4 us -> 8.41 us
  between operations: 15.1 us -> 1.21 us
    pallas_call x0 -> x2, Pallas kernels: none -> 159 us  [the longest x1 109 us: first_part(): pl.pallas_call(functools.partial(first_kernel, size, chunks, heads), out_...]
    dot_general x14 -> x0, matrix products: 66.2 us -> none  [the longest x4 32.1 us: product_nt(): lax.dot_general(left, right, (((1,), (1,)), ((), ())), preferred_element_...]
    all_gather x1 -> x0, waiting for transfers between devices: 66 us -> none  [per_device(): lax.all_gather(first_out.astype(jnp.bfloat16), 'tensor', axis=0, tiled=True)]
    reduce_sum x6 -> x0, other arithmetic: 19.1 us -> none  [the longest x1 5.75 us: gated_norm(): centered * lax.rsqrt(jnp.mean(centered * centered, axis=-1, keepdims=True...]
    convert_element_type x3 -> x0, local copies, waits for them, and re-layouts: 14.1 us -> none  [the longest x2 8.51 us: per_device(): mixed = mixed_full.reshape(group_rows, head_local * VD).astype(jnp.bfloat16)]
    reshape x2 -> x1, local copies, waits for them, and re-layouts: 14.6 us -> 1.71 us  [first_part(): segments.reshape(rows, 1)]
    convert_element_type x4 -> x0, other arithmetic: 12.7 us -> none  [the longest x1 5.24 us: per_device(): scores_low = grad_scores.astype(jnp.bfloat16)]
  transfers between devices with their start and end apart: 1 -> 0, of which waited for: 1 -> 0; matrix products, arithmetic and copies ran while one was open for 2% -> 0% of each run, Pallas kernels for 0% -> 0%
where the time goes in v4:
time: 726 us; the launch traced here: 718 us
  Pallas kernels  633 us (87%)
  matrix products  45.1 us (6%)
  other arithmetic  29.7 us (4%)
  local copies, waits for them, and re-layouts  8.41 us (1%)
    pallas_call x1, Pallas kernels, feed_forward(): pl.pallas_call(functools.partial(feed_kernel, size, chunks), out_shape=(b...  213 us
    pallas_call x1, Pallas kernels, last_sums(): pl.pallas_call(functools.partial(last_kernel, size, bits, chunks), out_sh...  146 us
    pallas_call x1, Pallas kernels, feed_back(): pl.pallas_call(functools.partial(back_kernel, size, bits, chunks), out_sh...  115 us
    pallas_call x1, Pallas kernels, first_part(): pl.pallas_call(functools.partial(first_kernel, size, chunks, heads), out_...  109 us
    pallas_call x1, Pallas kernels, retain_back(): pl.pallas_call(functools.partial(retain_kernel, size, heads), out_shape=t...  49.9 us
    dot_general x8, matrix products, product_tn(): lax.dot_general(left, right, (((0,), (0,)), ((), ())), preferred_element_...  45.1 us
    convert_element_type x4, other arithmetic, per_device(): item.astype(jnp.float32)  15.2 us

profile of v4, /device:TPU:0, one launch (start us, length us, event | category | flops | bytes accessed | tf_op | source)
XLA Modules:
  0.0 717.5 jit_solution(10055145623546669375)
XLA Ops:
  1.2 1.7 copy.37.column_ref
  2.9 109.1 %shard_map.254 = (bf16[4,256,2048]{2,1,0:T(8,128)(2,1)}, bf16[4,256,512]{2,1,0:T(8,128)(2,1)}, bf16[4,256,512]{2,1,0:T(8,128)(2,1)}, bf16[2,4,256,432]{3,2,1,0:T...) custom-call(bf16[256,2048]{1,0:T(8,128)(2,1)} %tokens_ref.3, ...), custom_call_target="tpu_custom_call" | custom-call | flops 8589934592 | bytes 67108864 | tf_op jit(solution)/shard_map/pallas_call | solution.py:1439
  112.0 213.4 %shard_map.255 = (bf16[4,256,2048]{2,1,0:T(8,128)(2,1)}, bf16[4,256,2048]{2,1,0:T(8,128)(2,1)}, bf16[4,256,864]{2,1,0:T(8,128)(2,1)}, bf16[4,256,864]{2,1,0:T(8,...) custom-call(bf16[4,256,864]{2,1,0:T(8,128)(2,1)} %get-tuple-element., ...), custom_call_target="tpu_custom_call" | custom-call | flops 25367150592 | bytes 67108864 | tf_op jit(solution)/shard_map/pallas_call | solution.py:785
  325.4 8.6 %bitcast_convert_fusion.5.grads_hbm_0_ = bf16[864,2048]{1,0:T(8,128)(2,1)} fusion(bf16[4,256,864]{2,1,0:T(8,128)(2,1)} %get-tuple-element.54, bf16[4,256,2048]{2,1,0:T(8,128)(2,1)} %get-tuple-element.55), kind=kOutput, calls=%fused_computation.5 | convolution fusion | flops 3625648128 | bytes 9502720 | tf_op jit(solution)/shard_map/dot_general | solution.py:28
  334.0 5.3 bitcast_convert_fusion.4.grads_hbm_1_
  339.3 5.3 bitcast_convert_fusion.3.grads_hbm_2_
  344.5 114.8 %shard_map.256 = (bf16[4,256,2048]{2,1,0:T(8,128)(2,1)}, f32[2,4,256,432]{3,2,1,0:T(8,128)}, bf16[256,2048]{1,0:T(8,128)(2,1)}, bf16[864,2048]{1,0:T(8,128)(2,1)...) custom-call(bf16[4,256,2048]{2,1,0:T(8,128)(2,1)} %get-tuple-element.51.outp_hbm, bf16[864,2048]{1,0:T(8,128)(2,1)} %out_hbm.3, ...), custom_call_target="tpu_custom_call" | custom-call | flops 3623878656 | bytes 67108864 | tf_op jit(solution)/shard_map/pallas_call | solution.py:982
  459.3 49.9 %shard_map.257 = (bf16[4,256,512]{2,1,0:T(8,128)(2,1)}, bf16[4,256,512]{2,1,0:T(8,128)(2,1)}, bf16[4,256,864]{2,1,0:T(8,128)(2,1)}, bf16[4,256,864]{2,1,0:T(8,128)(2,1)}, bf16[4,256,2048]{2,1,0:T(8,128)(2,1)}) custom-call(bf16[4,256,512]{2,1,0:T(8,128)(2,1)} %get-tuple-element.60.queries_hbm, bf16[4,256,512]{2,1,0:T(8,128)(2,1)} %get-tuple-element.61.keys_hbm, ...), custom_call_target="tpu_custom_call" | custom-call | flops 17179869184 | bytes 67108864 | tf_op jit(solution)/shard_map/pallas_call | solution.py:1665
  509.3 8.0 %bitcast_convert_fusion.2.grads_hbm_0_ = bf16[864,2048]{1,0:T(8,128)(2,1)} fusion(bf16[4,256,864]{2,1,0:T(8,128)(2,1)S(1)} %copy-done.11, bf16[4,256,2048]{2,1,0:T(8,128)(2,1)} %get-tuple-element.70), kind=kOutput, calls=%fused_computation.2 | convolution fusion | flops 3625648128 | bytes 9502720 | tf_op jit(solution)/shard_map/dot_general | solution.py:28
  517.3 3.7 bitcast_convert_fusion.7.grads_hbm_3_
  521.0 3.7 bitcast_convert_fusion.6.grads_hbm_4_
  524.7 5.3 bitcast_convert_fusion.1.grads_hbm_1_
  530.0 5.3 bitcast_convert_fusion.grads_hbm_2_
  535.3 146.0 %shard_map.258 = (f32[256,2048]{1,0:T(8,128)}, f32[8,2048]{1,0:T(8,128)}, bf16[864,2048]{1,0:T(8,128)(2,1)}, bf16[864,2048]{1,0:T(8,128)(2,1)}, bf16[864,2048]{1...) custom-call(bf16[4,256,2048]{2,1,0:T(8,128)(2,1)} %get-tuple-element.67.dfirst_hbm, ...), custom_call_target="tpu_custom_call" | custom-call | flops 1073741824 | bytes 67108864 | tf_op jit(solution)/shard_map/pallas_call | solution.py:1164
  681.3 1.7 fusion
  683.0 4.2 convert_element_type.52
  687.2 2.6 convert_element_type.53
  690.3 3.9 convert_element_type.54
  694.2 4.5 convert_element_type.55
  698.7 1.1 copy-done.5
  699.8 7.0 convert_bitcast_fusion.2
  706.8 7.0 convert_bitcast_fusion
  714.8 1.0 copy-done.7
  715.8 1.3 copy.57
  (36 shorter events, 2.1 us)
Async XLA Ops:
  325.4 8.6 %copy-start.10 = (bf16[4,256,2048]{2,1,0:T(8,128)(2,1)S(1)}, bf16[4,256,2048]{2,1,0:T(8,128)(2,1)}, u32[]{:S(2)}) copy-start(bf16[4,256,2048]{2,1,0:T(8,128)(2,1)} %get-tuple-element.57) | copy-start | bytes 12582916
  325.4 8.6 %copy-start.15 = (bf16[4,256,864]{2,1,0:T(8,128)(2,1)S(1)}, bf16[4,256,864]{2,1,0:T(8,128)(2,1)}, u32[]{:S(2)}) copy-start(bf16[4,256,864]{2,1,0:T(8,128)(2,1)} %get-tuple-element.56) | copy-start | bytes 5308420
  334.0 5.3 copy-start.14
  459.3 50.0 %copy-start.11 = (bf16[4,256,864]{2,1,0:T(8,128)(2,1)S(1)}, bf16[4,256,864]{2,1,0:T(8,128)(2,1)}, u32[]{:S(2)}) copy-start(bf16[4,256,864]{2,1,0:T(8,128)(2,1)} %get-tuple-element.50.mixed_hbm) | copy-start | bytes 5308420
  509.3 8.0 %copy-start.9 = (bf16[4,256,2048]{2,1,0:T(8,128)(2,1)S(1)}, bf16[4,256,2048]{2,1,0:T(8,128)(2,1)}, u32[]{:S(2)}) copy-start(bf16[4,256,2048]{2,1,0:T(8,128)(2,1)} %get-tuple-element.72) | copy-start | bytes 12582916
  509.3 8.0 %copy-start.17 = (bf16[4,256,512]{2,1,0:T(8,128)(2,1)S(1)}, bf16[4,256,512]{2,1,0:T(8,128)(2,1)}, u32[]{:S(2)}) copy-start(bf16[4,256,512]{2,1,0:T(8,128)(2,1)} %get-tuple-element.74) | copy-start | bytes 3145732
  517.3 3.7 copy-start.16
  521.0 3.7 copy-start.13
  524.7 5.3 copy-start.12
  681.3 5.9 copy-start.6
  687.2 3.1 copy-start.1
  690.3 3.9 copy-start
  694.2 4.5 copy-start.4
  694.2 5.6 copy-start.5
  699.8 7.0 copy-start.2
  699.8 7.0 copy-start.3
  706.8 7.0 copy-start.8
  713.8 2.0 copy-start.7

commit v5 on v4

--- a/solution.py
+++ b/solution.py
@@ -22,12 +22,6 @@
 TILE = 256
 LINE = 16
 BAND = 64
-
-
-def product_tn(left, right):
-    return lax.dot_general(
-        left, right, (((0,), (0,)), ((), ())), preferred_element_type=jnp.float32
-    )
 
 
 def for_columns(width, body):
@@ -238,11 +232,11 @@
 
 
 class CubeSum:
-    def __init__(self, bits, me, sources, results, parts, firsts, nexts, load, store, send, recv, free):
+    def __init__(self, bits, me, results, parts, firsts, nexts, store, send, recv, free):
         self.bits, self.me = bits, me
-        self.sources, self.results, self.parts = sources, results, parts
+        self.results, self.parts = results, parts
         self.firsts, self.nexts = firsts, nexts
-        self.load_sem, self.store_sem, self.send, self.recv = load, store, send, recv
+        self.store_sem, self.send, self.recv = store, send, recv
         self.free = free
         self.orders = (tuple(range(bits)), (0,) + tuple(range(bits - 1, 0, -1)))
         self.mine = [(me // 2**bit) % 2 for bit in range(bits)]
@@ -328,13 +322,19 @@
                 whole = ref.at[pl.ds(index * rows, rows), :]
             yield index, self.parts[which].at[lead], whole
 
-    def load(self, which):
-        for index, part, whole in self.slices(which, self.sources[which]):
-            pltpu.make_async_copy(whole, part, self.load_sem.at[which, index]).start()
+    def make_wide(self, which, left, right):
+        columns = self.parts[which].shape[-1]
+        half = 2 ** (self.bits - 1)
+
+        def some(start):
+            for index in range(start, start + half):
+                lead = tuple((index >> bit) & 1 for bit in range(self.bits - 1, -1, -1))
+                value = dot_nn(left[...], right(pl.ds(index * columns, columns)))
+                self.parts[which][lead] = value.astype(jnp.bfloat16)
+
+        return [functools.partial(some, 0), functools.partial(some, half)]
 
     def open(self, which):
-        for index, part, whole in self.slices(which, self.sources[which]):
-            pltpu.make_async_copy(whole, part, self.load_sem.at[which, index]).wait()
         self.halve(which, 2, 0).start()
 
     def split(self, which):
@@ -433,7 +433,6 @@
         firsts,
         nexts,
         dma((len(shapes), 2**bits)),
-        dma((len(shapes), 2**bits)),
         dma((len(shapes), 2, 2 * bits)),
         dma((len(shapes), 2, 2 * bits)),
         pltpu.SemaphoreType.REGULAR((len(shapes), 2, bits)),
@@ -441,6 +440,11 @@
 
 
 ORDERS = {
+    ("first", 4, 4, 2): (
+        0, 1, 2, 4, 4, 0, 0, 4, 4, 2, 2, 4, 0, 1, 4, 3, 4, 0, 2, 2, 0, 4, 1, 0,
+        2, 2, 2, 0, 0, 2, 2, 1, 0, 0, 2, 3, 3, 2, 1, 1, 1, 1, 1, 0, 1, 1, 1, 3,
+        3, 3, 3, 3, 3, 3, 3, 3,
+    ),
     ("feed", 4, 4): (
         4, 6, 4, 0, 5, 4, 4, 0, 4, 6, 5, 0, 5, 0, 0, 2, 5, 6, 1, 2, 0, 3, 4, 4,
         6, 1, 6, 7, 5, 0, 6, 1, 1, 5, 2, 0, 0, 1, 3, 2, 0, 1, 7, 3, 3, 0, 5, 1,
@@ -449,43 +453,20 @@
         7, 1, 7, 0, 3, 1, 3, 3, 3, 3, 2, 2, 0, 3, 2, 3, 3, 2, 1, 3,
     ),
     ("back", 4, 4, 3): (
-        0, 8, 9, 4, 10, 1, 5, 2, 8, 9, 4, 3, 10, 8, 8, 6, 0, 1, 9, 9, 4, 0, 1, 0,
-        10, 10, 5, 8, 4, 8, 9, 0, 2, 9, 3, 5, 10, 8, 8, 2, 0, 10, 0, 9, 0, 9, 7, 3,
-        1, 6, 1, 5, 6, 5, 1, 8, 4, 1, 3, 2, 10, 10, 7, 6, 3, 2, 7, 3, 9, 6, 7, 1,
-        2, 3, 8, 10, 5, 4, 2, 6, 7, 2, 9, 3, 10, 7,
+        0, 1, 8, 8, 8, 8, 4, 5, 2, 0, 9, 9, 3, 8, 9, 1, 9, 1, 10, 10, 0, 10, 9, 10,
+        0, 10, 8, 4, 9, 6, 0, 0, 9, 8, 5, 10, 2, 10, 7, 4, 0, 8, 3, 8, 4, 5, 10, 2,
+        10, 9, 3, 5, 1, 9, 2, 10, 1, 10, 8, 2, 8, 3, 1, 4, 1, 5, 6, 9, 9, 7, 3, 7,
+        7, 10, 0, 1, 2, 2, 6, 8, 3, 6, 5, 7, 6, 3, 2, 9, 3, 4, 10, 8, 7, 9, 6,
+    ),
+    ("retain", 4, 3, 2): (
+        0, 0, 0, 0, 1, 1, 0, 1, 1, 1, 0, 0, 1, 1, 0, 0, 1, 0, 0, 1, 1, 1, 0, 1,
+        0,
     ),
     ("last", 4, 4, 3): (
-        7, 0, 4, 7, 4, 6, 0, 6, 4, 5, 2, 4, 3, 0, 6, 6, 8, 1, 0, 0, 7, 4, 5, 7,
-        2, 0, 6, 4, 8, 5, 7, 4, 6, 3, 8, 5, 1, 4, 6, 1, 8, 7, 7, 6, 5, 3, 1, 2,
-        2, 5, 8, 2, 1, 3, 8, 5, 7, 4, 3, 1, 2, 8, 5, 6, 3, 7, 9, 4, 8, 9, 5, 7,
-        9, 8, 6, 5, 8,
-    ),
-    ("feed", 4, 8): (
-        11, 10, 13, 8, 9, 13, 1, 8, 13, 8, 10, 0, 14, 10, 12, 8, 13, 10, 13, 0, 1, 10, 8, 11,
-        9, 12, 2, 14, 0, 0, 1, 1, 11, 8, 1, 3, 0, 9, 11, 9, 5, 12, 2, 1, 3, 10, 12, 11,
-        9, 14, 0, 8, 7, 6, 5, 1, 12, 0, 3, 3, 2, 2, 4, 5, 0, 0, 2, 9, 3, 9, 11, 15,
-        6, 14, 0, 1, 1, 0, 0, 2, 3, 4, 12, 0, 7, 5, 13, 1, 15, 2, 7, 0, 7, 0, 4, 0,
-        4, 6, 6, 10, 4, 2, 0, 2, 1, 12, 5, 1, 1, 1, 4, 1, 3, 1, 1, 2, 11, 3, 6, 2,
-        5, 2, 4, 13, 2, 3, 2, 2, 4, 7, 2, 3, 15, 0, 2, 6, 3, 4, 3, 15, 3, 3, 3, 5,
-        3, 4, 4, 3, 4, 5, 1, 4, 7, 4, 5, 4, 4, 2, 5, 5, 14, 6, 1, 1, 4, 7, 5, 5,
-        2, 5, 14, 5, 14, 0, 6, 1, 6, 4, 5, 6, 7, 5, 3, 6, 6, 6, 6, 7, 6, 5, 7, 2,
-        0, 7, 15, 3, 3, 6, 4, 15, 4, 6, 7, 7, 5, 5, 0, 15, 3, 2, 5, 7, 1, 4, 7, 6,
-        7, 7, 7, 6, 6, 3, 5, 7, 7, 6, 7, 6, 2, 0, 4, 7,
-    ),
-    ("back", 4, 8, 3): (
-        0, 16, 8, 1, 18, 0, 9, 2, 3, 16, 0, 17, 0, 4, 18, 5, 17, 8, 16, 6, 16, 9, 0, 18,
-        0, 3, 2, 18, 4, 1, 10, 9, 8, 6, 5, 17, 3, 6, 17, 11, 9, 6, 16, 12, 4, 3, 16, 18,
-        7, 18, 2, 5, 10, 17, 17, 11, 1, 16, 12, 16, 0, 3, 18, 2, 5, 18, 2, 5, 7, 8, 1, 10,
-        4, 13, 14, 3, 6, 10, 11, 11, 6, 15, 17, 1, 4, 1, 3, 5, 12, 8, 7, 10, 17, 14, 11, 2,
-        16, 1, 8, 12, 0, 2, 7, 9, 1, 2, 12, 7, 5, 6, 13, 3, 18, 15, 13, 4, 13, 10, 12, 14,
-        14, 4, 4, 11, 17, 15, 15, 7, 16, 13, 7, 18, 14, 5, 6, 13, 7, 15, 9, 14, 17, 15,
-    ),
-    ("last", 4, 8, 3): (
-        11, 0, 9, 11, 10, 8, 12, 6, 9, 11, 10, 3, 2, 0, 6, 11, 9, 5, 1, 11, 8, 3, 6, 12,
-        7, 0, 9, 4, 5, 12, 10, 11, 9, 6, 9, 10, 11, 2, 11, 12, 8, 7, 12, 1, 6, 4, 10, 9,
-        4, 2, 12, 8, 5, 2, 10, 2, 8, 9, 3, 4, 7, 1, 0, 8, 10, 3, 4, 11, 1, 8, 1, 10,
-        5, 0, 3, 5, 7, 0, 7, 8, 9, 1, 11, 2, 3, 4, 5, 6, 9, 12, 12, 10, 7, 13, 13, 8,
-        13, 12, 8, 10, 12,
+        0, 4, 4, 4, 4, 5, 5, 2, 4, 5, 5, 6, 6, 6, 5, 6, 3, 6, 4, 4, 1, 0, 6, 7,
+        2, 5, 5, 7, 4, 4, 3, 2, 5, 5, 6, 2, 7, 6, 3, 7, 4, 4, 3, 0, 2, 3, 6, 5,
+        6, 5, 1, 0, 4, 1, 0, 1, 7, 7, 4, 6, 1, 6, 5, 2, 7, 3, 7, 0, 5, 1, 8, 6,
+        8, 7, 8, 6, 7,
     ),
 }
 
@@ -846,7 +827,11 @@
     out_hbm,
     own_hbm,
     middle_ref,
-    grads_hbm,
+    seeds_hbm,
+    second_hbm,
+    inner_hbm,
+    dgate_hbm,
+    dlin_hbm,
     branch_hbm,
     dmixed_hbm,
     output_ref,
@@ -856,7 +841,12 @@
     branch,
     inbox,
     dmixed,
+    seeds,
+    second,
+    thin,
+    turned,
     load_sem,
+    grad_sem,
     store_sem,
     rs_send,
     rs_recv,
@@ -865,7 +855,6 @@
     cube_parts,
     cube_firsts,
     cube_nexts,
-    cube_load,
     cube_store,
     cube_send,
     cube_recv,
@@ -882,19 +871,29 @@
     cube = CubeSum(
         bits,
         lax.axis_index("dp"),
-        grads_hbm,
         totals_hbm,
         cube_parts,
         cube_firsts,
         cube_nexts,
-        cube_load,
         cube_store,
         cube_send,
         cube_recv,
         cube_free,
     )
-    for which in range(len(cube_parts)):
-        cube.load(which)
+    grad_loads = [
+        pltpu.make_async_copy(src, dst, grad_sem.at[index])
+        for index, (src, dst) in enumerate(
+            (
+                (inner_hbm, thin.at[0]),
+                (seeds_hbm, seeds),
+                (dgate_hbm, thin.at[1]),
+                (second_hbm, second),
+                (dlin_hbm, thin.at[0]),
+            )
+        )
+    ]
+    for load in grad_loads[:4]:
+        load.start()
     load_out.start()
     enter([{"dp": cube.partner(bit)} for bit in range(bits)], (size, me))
     scatter = LineScatter(size, me, rows, part, inbox, rs_send, rs_recv)
@@ -947,6 +946,19 @@
         if chunk == 0:
             load_part.wait()
         scatter.begin(chunk)
+
+    def turn(which):
+        needs = ((0, 1), (2, 3), (4,))[which]
+        for index in needs:
+            grad_loads[index].wait()
+        for owner in range(size):
+            turned[:, pl.ds(owner * own, own)] = thin[which % 2, owner].T
+        if which == 0:
+            grad_loads[4].start()
+
+    def wide_columns(which):
+        ref = (seeds, second, second)[which]
+        return lambda columns: ref[:, :, columns].reshape(size * own, columns.size)
 
     streams, after = [], {}
     for chunk in range(chunks):
@@ -961,7 +973,15 @@
             after[chunks + chunk, 0] = ((chunks + chunk - 1, 1),)
         streams.append(steps + [functools.partial(finish, chunk)])
     for which in range(len(cube_parts)):
-        streams.append(cube.calls(which))
+        if which:
+            after[2 * chunks + which, 0] = ((2 * chunks + which - 1, 3),)
+        streams.append(
+            [
+                functools.partial(turn, which),
+                *cube.make_wide(which, turned, wide_columns(which)),
+                *cube.calls(which),
+            ]
+        )
     run_streams(streams, ORDERS.get(("back", size, chunks, bits)), after)
     for chunk in range(chunks):
         scatter.drain(chunk)
@@ -971,13 +991,14 @@
     cube.drain()
 
 
-def feed_back(size, bits, chunks, partial, out_weight, branch, middle, grads):
+def feed_back(size, bits, chunks, partial, out_weight, branch, middle, seeds, second, thins):
     own, depth = middle.shape
     rows = own // chunks
     width = out_weight.shape[0]
     low, full = jnp.bfloat16, jnp.float32
     dma = pltpu.SemaphoreType.DMA
     vmem, anywhere = pl.BlockSpec(memory_space=pltpu.VMEM), pl.BlockSpec(memory_space=pl.ANY)
+    grads = [jax.ShapeDtypeStruct((thin.shape[-1], depth), low) for thin in thins]
     many = [anywhere] * len(grads)
     return pl.pallas_call(
         functools.partial(back_kernel, size, bits, chunks),
@@ -985,9 +1006,9 @@
             jax.ShapeDtypeStruct((size, own, depth), low),
             jax.ShapeDtypeStruct((width // VD, size, own, VD), full),
             jax.ShapeDtypeStruct((own, depth), low),
-            [jax.ShapeDtypeStruct(grad.shape, low) for grad in grads],
+            grads,
         ),
-        in_specs=[anywhere, anywhere, anywhere, vmem, many],
+        in_specs=[anywhere, anywhere, anywhere, vmem] + [anywhere] * 5,
         out_specs=(anywhere, anywhere, vmem, many),
         scratch_shapes=[
             pltpu.VMEM((size, own, depth), low),
@@ -995,7 +1016,12 @@
             pltpu.VMEM((size, own, depth), low),
             pltpu.VMEM((size + 1, own, depth), low),
             pltpu.VMEM((2, width // VD, size, rows, VD), full),
+            pltpu.VMEM((size, own, depth), low),
+            pltpu.VMEM((size, own, depth), low),
+            pltpu.VMEM((2,) + thins[0].shape, low),
+            pltpu.VMEM((thins[0].shape[-1], size * own), low),
             dma((3,)),
+            dma((5,)),
             dma((2, chunks)),
             dma((size, chunks)),
             dma((size + 1, chunks)),
@@ -1009,7 +1035,7 @@
         cost_estimate=pl.CostEstimate(
             flops=2 * size * own * depth * width, bytes_accessed=2**26, transcendentals=0
         ),
-    )(partial, out_weight, branch, middle, grads)
+    )(partial, out_weight, branch, middle, seeds, second, *thins)
 
 
 def last_kernel(
@@ -1021,7 +1047,11 @@
     dmiddle_ref,
     gain_ref,
     sums_ref,
-    grads_hbm,
+    firsts_hbm,
+    dvalues_hbm,
+    dgates_hbm,
+    dqueries_hbm,
+    dkeys_hbm,
     dtokens_ref,
     totals_ref,
     totals_hbm,
@@ -1029,6 +1059,13 @@
     first_inbox,
     line_box,
     dp_box,
+    firsts,
+    dvalues,
+    dgates,
+    dqueries,
+    dkeys,
+    turned,
+    slice_turned,
     load_sem,
     line_send,
     line_recv,
@@ -1039,7 +1076,6 @@
     cube_parts,
     cube_firsts,
     cube_nexts,
-    cube_load,
     cube_store,
     cube_send,
     cube_recv,
@@ -1054,19 +1090,29 @@
     cube = CubeSum(
         bits,
         mine,
-        grads_hbm,
         totals_hbm,
         cube_parts,
         cube_firsts,
         cube_nexts,
-        cube_load,
         cube_store,
         cube_send,
         cube_recv,
         cube_free,
     )
-    for which in range(len(cube_parts)):
-        cube.load(which)
+    loads = [
+        pltpu.make_async_copy(src, dst, load_sem.at[1 + index])
+        for index, (src, dst) in enumerate(
+            (
+                (dvalues_hbm, dvalues),
+                (firsts_hbm, firsts),
+                (dgates_hbm, dgates),
+                (dqueries_hbm, dqueries),
+                (dkeys_hbm, dkeys),
+            )
+        )
+    ]
+    for load in loads:
+        load.start()
     groups = 2**bits
     peers = [{"dp": (mine + step) % groups} for step in range(1, groups)]
     others = [{"tensor": (me + step) % size} for step in range(1, size)]
@@ -1132,6 +1178,30 @@
 
     line_box[me] = sums_ref[...]
     load_first.wait()
+    def turn(which):
+        for index in ((0, 1), (2,))[which]:
+            loads[index].wait()
+        ref = (dvalues, dgates)[which]
+        for owner in range(size):
+            turned[:, pl.ds(owner * own, own)] = ref[owner].T
+
+    def first_columns(columns):
+        return firsts[:, :, columns].reshape(size * own, columns.size)
+
+    def make_tall(start):
+        if start == 0:
+            loads[3].wait()
+            loads[4].wait()
+        lines = cube_parts[2].shape[-2]
+        for index in range(start, start + groups // 4):
+            lead = tuple((index >> bit) & 1 for bit in range(bits - 1, -1, -1))
+            for owner in range(size):
+                piece = firsts[owner, :, pl.ds(index * lines, lines)]
+                slice_turned[:, pl.ds(owner * own, own)] = piece.T
+            for which, ref in ((2, dqueries), (3, dkeys)):
+                value = dot_nn(slice_turned[...], ref[...].reshape(size * own, ref.shape[-1]))
+                cube_parts[which][lead] = value.astype(jnp.bfloat16)
+
     streams = []
     for chunk in range(chunks):
         streams.append(
@@ -1141,9 +1211,22 @@
                 functools.partial(back, chunk),
             ]
         )
-    after = {(chunks + len(cube_parts), 0): [(chunk, 2 * size - 2) for chunk in range(chunks)]}
-    for which in range(len(cube_parts)):
-        streams.append(cube.calls(which))
+    after = {(chunks + 4, 0): [(chunk, 2 * size - 2) for chunk in range(chunks)]}
+    for which in range(2):
+        if which:
+            after[chunks + which, 0] = ((chunks + which - 1, 3),)
+        streams.append(
+            [
+                functools.partial(turn, which),
+                *cube.make_wide(which, turned, first_columns),
+                *cube.calls(which),
+            ]
+        )
+    quarters = [functools.partial(make_tall, quarter * (groups // 4)) for quarter in range(4)]
+    after[chunks + 2, 0] = ((chunks, 1),)
+    after[chunks + 3, 0] = ((chunks + 2, 4),)
+    streams.append([*quarters, *cube.calls(2)])
+    streams.append(cube.calls(3))
     streams.append([sums_on_line, sums_on_dp, sums_done])
     run_streams(streams, ORDERS.get(("last", size, chunks, bits)), after)
     for chunk in range(chunks):
@@ -1155,27 +1238,36 @@
     cube.drain()
 
 
-def last_sums(size, bits, chunks, dfirst, tokens, dmiddle, gain, sums, grads):
+def last_sums(size, bits, chunks, dfirst, tokens, dmiddle, gain, sums, firsts, parts):
     own, depth = tokens.shape
     low, full = jnp.bfloat16, jnp.float32
     dma = pltpu.SemaphoreType.DMA
     vmem, anywhere = pl.BlockSpec(memory_space=pltpu.VMEM), pl.BlockSpec(memory_space=pl.ANY)
+    grads = [
+        jax.ShapeDtypeStruct((part.shape[-1], depth) if place < 2 else (depth, part.shape[-1]), low)
+        for place, part in enumerate(parts)
+    ]
     many = [anywhere] * len(grads)
+    group = size * own
     return pl.pallas_call(
         functools.partial(last_kernel, size, bits, chunks),
         out_shape=(
             jax.ShapeDtypeStruct((own, depth), full),
             jax.ShapeDtypeStruct((8, depth), full),
-            [jax.ShapeDtypeStruct(grad.shape, low) for grad in grads],
+            grads,
         ),
-        in_specs=[anywhere, vmem, vmem, vmem, vmem, many],
+        in_specs=[anywhere, vmem, vmem, vmem, vmem] + [anywhere] * 5,
         out_specs=(vmem, vmem, many),
         scratch_shapes=[
             pltpu.VMEM((size, own, depth), low),
             pltpu.VMEM((size + 1, own, depth), low),
             pltpu.VMEM((size, 8, depth), full),
             pltpu.VMEM((2**bits, 8, depth), full),
-            dma((1,)),
+            pltpu.VMEM(firsts.shape, low),
+            *[pltpu.VMEM(part.shape, low) for part in parts],
+            pltpu.VMEM((parts[0].shape[-1], group), low),
+            pltpu.VMEM((depth // 2**bits, group), low),
+            dma((6,)),
             dma((size,)),
             dma((size,)),
             dma((2**bits,)),
@@ -1188,7 +1280,7 @@
             collective_id=2, has_side_effects=True, vmem_limit_bytes=VMEM_BYTES
         ),
         cost_estimate=pl.CostEstimate(flops=2**30, bytes_accessed=2**26, transcendentals=0),
-    )(dfirst, tokens, dmiddle, gain, sums, grads)
+    )(dfirst, tokens, dmiddle, gain, sums, firsts, *parts)
 
 
 def decay_rows(rate, column, row, first):
@@ -1472,6 +1564,7 @@
 
 def retain_kernel(
     size,
+    bits,
     heads,
     queries_hbm,
     keys_hbm,
@@ -1484,11 +1577,14 @@
     key_hbm,
     value_hbm,
     gate_hbm,
+    mixed_hbm,
+    branch_hbm,
     dqueries_hbm,
     dkeys_hbm,
     dvalues_hbm,
     dgates_hbm,
     dfirst_hbm,
+    totals_hbm,
     queries,
     keys,
     values,
@@ -1500,11 +1596,14 @@
     key_weight,
     value_weight,
     gate_weight,
+    mixed,
+    branch,
     dqueries,
     dkeys,
     dvalues,
     dgates,
     dfirst,
+    turned,
     raw,
     grad,
     retain,
@@ -1515,6 +1614,13 @@
     load_sem,
     block_sem,
     store_sem,
+    cube_parts,
+    cube_firsts,
+    cube_nexts,
+    cube_store,
+    cube_send,
+    cube_recv,
+    cube_free,
 ):
     own = queries.shape[1]
     depth = query_weight.shape[0]
@@ -1523,6 +1629,8 @@
         src, dst = (
             (queries_hbm, queries),
             (keys_hbm, keys),
+            (mixed_hbm, mixed),
+            (branch_hbm, branch),
             (query_hbm, query_weight),
             (key_hbm, key_weight),
             (value_hbm, value_weight),
@@ -1531,16 +1639,20 @@
         return pltpu.make_async_copy(src, dst, load_sem.at[kind])
 
     def load_block(kind, head, block):
+        slot = (head * size + block) % 2
         src, dst = (
-            (values_hbm, values),
-            (gates_hbm, gates),
-            (retained_hbm, retained),
-            (dmixed_hbm, dmixed),
-            (table_hbm, table),
+            (values_hbm, values.at[head, block]),
+            (gates_hbm, gates.at[slot]),
+            (retained_hbm, retained.at[slot]),
+            (dmixed_hbm, dmixed.at[slot]),
+            (table_hbm, table.at[slot]),
         )[kind]
-        return pltpu.make_async_copy(
-            src.at[head, block], dst.at[head, block], block_sem.at[kind, head, block]
-        )
+        return pltpu.make_async_copy(src.at[head, block], dst, block_sem.at[kind, head, block])
+
+    def load_blocks(place):
+        if place < heads * size:
+            for kind in range(5):
+                load_block(kind, place // size, place % size).start()
 
     def store(kind, block):
         src, dst = (
@@ -1554,26 +1666,41 @@
 
     for kind in range(2):
         load_whole(kind).start()
-    for head in range(heads):
-        for block in range(size):
-            for kind in range(5):
-                load_block(kind, head, block).start()
-    for kind in range(2, 6):
+    load_blocks(0)
+    for kind in range(2, 4):
         load_whole(kind).start()
-    for kind in range(2):
-        load_whole(kind).wait()
+    load_blocks(1)
+    for kind in range(4, 8):
+        load_whole(kind).start()
+    cube = CubeSum(
+        bits,
+        lax.axis_index("dp"),
+        totals_hbm,
+        cube_parts,
+        cube_firsts,
+        cube_nexts,
+        cube_store,
+        cube_send,
+        cube_recv,
+        cube_free,
+    )
+    enter([{"dp": cube.partner(bit)} for bit in range(bits)], None)
 
     def attend(head, block):
         seen = (block + 1) * own
+        slot = (head * size + block) % 2
+        if head == 0 and block == 0:
+            for kind in range(2):
+                load_whole(kind).wait()
         lanes = pl.ds(head * KD, KD)
 
         for kind in range(5):
             load_block(kind, head, block).wait()
 
         def body_mix(part):
-            normed, scale = group_parts(retained[head, block, part, :])
-            gate = gates[head, block, part, :]
-            dmix = dmixed[head, block, part, :]
+            normed, scale = group_parts(retained[slot, part, :])
+            gate = gates[slot, part, :]
+            dmix = dmixed[slot, part, :]
             half = sigmoid(gate)
             dgate = dmix * normed * (half * (1.0 + gate * (1.0 - half)))
             dgates[block, part, pl.ds(head * VD, VD)] = dgate.astype(jnp.bfloat16)
@@ -1593,7 +1720,7 @@
         grad[:, :seen] = dot_nt(dretained[...], value)
 
         def body(part):
-            decay = table[head, block, part, :seen]
+            decay = table[slot, part, :seen]
             weighted = raw[part, :seen] * (KD**-0.5) * decay
             dretain = grad[part, :seen]
             total = jnp.sum(weighted, axis=-1, keepdims=True)
@@ -1617,18 +1744,17 @@
                 dkey_sum[other] += dkey
                 dvalue_sum[other] += dvalue
 
-    for head in range(heads):
-        for block in range(size):
-            attend(head, block)
-
-        lanes = pl.ds(head * KD, KD)
-        for block in range(size):
-            dkeys[block, :, lanes] = (dkey_sum[block] * (KD**-0.5)).astype(jnp.bfloat16)
-            dvalues[block, :, pl.ds(head * VD, VD)] = dvalue_sum[block].astype(jnp.bfloat16)
-
-    for kind in range(2, 6):
-        load_whole(kind).wait()
-    for block in range(size):
+        load_blocks(head * size + block + 2)
+        if block == size - 1:
+            for other in range(size):
+                dkeys[other, :, lanes] = (dkey_sum[other] * (KD**-0.5)).astype(jnp.bfloat16)
+                there = pl.ds(head * VD, VD)
+                dvalues[other, :, there] = dvalue_sum[other].astype(jnp.bfloat16)
+
+    def combine(block):
+        if block == 0:
+            for kind in range(4, 8):
+                load_whole(kind).wait()
         for kind in range(4):
             store(kind, block).start()
 
@@ -1642,12 +1768,31 @@
 
         for_columns(depth, body)
         store(4, block).start()
+
+    def turn():
+        for kind in range(2, 4):
+            load_whole(kind).wait()
+        for owner in range(size):
+            turned[:, pl.ds(owner * own, own)] = mixed[owner].T
+
+    def branch_columns(columns):
+        return branch[:, :, columns].reshape(size * own, columns.size)
+
+    steps = [
+        functools.partial(attend, head, block) for head in range(heads) for block in range(size)
+    ]
+    steps += [functools.partial(combine, block) for block in range(size)]
+    sums = [turn, *cube.make_wide(0, turned, branch_columns), *cube.calls(0)]
+    run_streams([sums, steps], ORDERS.get(("retain", size, bits, heads)), {})
     for block in range(size):
         for kind in range(5):
             store(kind, block).wait()
-
-
-def retain_back(size, queries, keys, values, gates, retained, dmixed, table, query, key, value, gate):
+    cube.drain()
+
+
+def retain_back(
+    size, bits, queries, keys, values, gates, retained, dmixed, table, query, key, value, gate, mixed, branch
+):
     own = queries.shape[1]
     heads = values.shape[0]
     rows, depth = size * own, query.shape[0]
@@ -1655,6 +1800,12 @@
     dma = pltpu.SemaphoreType.DMA
     anywhere = pl.BlockSpec(memory_space=pl.ANY)
     inputs = (queries, keys, values, gates, retained, dmixed, table, query, key, value, gate)
+    inputs = inputs + (mixed, branch)
+    slots = [
+        jax.ShapeDtypeStruct((2,) + item.shape[2:], item.dtype) if 3 <= place < 7 else item
+        for place, item in enumerate(inputs)
+    ]
+    total = jax.ShapeDtypeStruct((heads * VD, depth), low)
     shapes = (
         queries.shape,
         keys.shape,
@@ -1663,13 +1814,14 @@
         (size, own, depth),
     )
     return pl.pallas_call(
-        functools.partial(retain_kernel, size, heads),
-        out_shape=tuple(jax.ShapeDtypeStruct(shape, low) for shape in shapes),
+        functools.partial(retain_kernel, size, bits, heads),
+        out_shape=tuple(jax.ShapeDtypeStruct(shape, low) for shape in shapes) + ([total],),
         in_specs=[anywhere] * len(inputs),
-        out_specs=(anywhere,) * 5,
-        scratch_shapes=[pltpu.VMEM(item.shape, item.dtype) for item in inputs]
+        out_specs=(anywhere,) * 5 + ([anywhere],),
+        scratch_shapes=[pltpu.VMEM(item.shape, item.dtype) for item in slots]
         + [pltpu.VMEM(shape, low) for shape in shapes]
         + [
+            pltpu.VMEM((heads * VD, rows), low),
             pltpu.VMEM((own, rows), full),
             pltpu.VMEM((own, rows), full),
             pltpu.VMEM((own, rows), low),
@@ -1677,11 +1829,14 @@
             pltpu.VMEM((own, VD), low),
             pltpu.VMEM((size, own, KD), full),
             pltpu.VMEM((size, own, VD), full),
-            dma((6,)),
+            dma((8,)),
             dma((5, heads, size)),
             dma((5, size)),
-        ],
-        compiler_params=pltpu.CompilerParams(vmem_limit_bytes=VMEM_BYTES),
+        ]
+        + cube_scratch(bits, [total.shape]),
+        compiler_params=pltpu.CompilerParams(
+            collective_id=4, has_side_effects=True, vmem_limit_bytes=VMEM_BYTES
+        ),
         cost_estimate=pl.CostEstimate(flops=2**34, bytes_accessed=2**26, transcendentals=0),
     )(*inputs)
 
@@ -1750,21 +1905,21 @@
         second_bias[None],
     )
 
-    def flat(item):
-        return item.reshape(group_rows, item.shape[-1])
-
-    second_all, seed_all = flat(second_all), flat(seed_all)
-    feed_grads = [
-        product_tn(flat(inner), seed_all).astype(jnp.bfloat16),
-        product_tn(flat(gate_in_low), second_all).astype(jnp.bfloat16),
-        product_tn(flat(lin_in_low), second_all).astype(jnp.bfloat16),
-    ]
     branch_all, grad_mixed, output, feed_grads = feed_back(
-        size, bits, CHUNKS, partial, out_weight, branch, middle, feed_grads
+        size,
+        bits,
+        CHUNKS,
+        partial,
+        out_weight,
+        branch,
+        middle,
+        seed_all,
+        second_all,
+        (inner, gate_in_low, lin_in_low),
     )
-    branch_all = flat(branch_all)
-    grad_queries, grad_keys, grad_values, grad_gates, grad_first = retain_back(
+    grad_queries, grad_keys, grad_values, grad_gates, grad_first, (grad_outw,) = retain_back(
         size,
+        bits,
         queries,
         keys,
         values,
@@ -1776,16 +1931,9 @@
         key_weight,
         value_weight.T,
         gate_weight.T,
+        mixed,
+        branch_all,
     )
-    first_all = flat(first_all)
-
-    grads = [
-        product_tn(flat(mixed), branch_all).astype(jnp.bfloat16),
-        product_tn(flat(grad_values), first_all).astype(jnp.bfloat16),
-        product_tn(flat(grad_gates), first_all).astype(jnp.bfloat16),
-        product_tn(first_all, flat(grad_queries)).astype(jnp.bfloat16),
-        product_tn(first_all, flat(grad_keys)).astype(jnp.bfloat16),
-    ]
     grad_tokens, sums, grads = last_sums(
         size,
         bits,
@@ -1795,11 +1943,12 @@
         grad_middle,
         first_gain[None],
         second_sums,
-        grads,
+        first_all,
+        (grad_values, grad_gates, grad_queries, grad_keys),
     )
     grad_sgain, grad_sbias, grad_fgain, grad_fbias = sums[0], sums[1], sums[2], sums[3]
     grad_outw, grad_valuew, grad_gatew, grad_queryw, grad_keyw = (
-        item.astype(jnp.float32) for item in grads
+        item.astype(jnp.float32) for item in (grad_outw, *grads)
     )
     grad_hdown, grad_hgate, grad_hup = (item.astype(jnp.float32) for item in feed_grads)
     grad_valuew, grad_gatew, grad_hgate, grad_hup = (

time: 726 us -> 656 us (0.904)
  matrix products: 45.1 us -> 0 us
  Pallas kernels: 633 us -> 607 us
    dot_general x8 -> x0, matrix products: 45.1 us -> none  [product_tn(): lax.dot_general(left, right, (((0,), (0,)), ((), ())), preferred_element_...]
    pallas_call x1, Pallas kernels: 146 us -> 118 us  [last_sums(): pl.pallas_call(functools.partial(last_kernel, size, bits, chunks), out_sh...]
    pallas_call x1, Pallas kernels: 109 us -> 95.6 us  [first_part(): pl.pallas_call(functools.partial(first_kernel, size, chunks, heads), out_...]
    pallas_call x1, Pallas kernels: 49.9 us -> 61.8 us  [retain_back(): pl.pallas_call(functools.partial(retain_kernel, size, bits, heads), out_s...]
where the time goes in v5:
time: 656 us; the launch traced here: 646 us
  Pallas kernels  607 us (93%)
  other arithmetic  29.7 us (5%)
  local copies, waits for them, and re-layouts  8.37 us (1%)
    pallas_call x1, Pallas kernels, feed_forward(): pl.pallas_call(functools.partial(feed_kernel, size, chunks), out_shape=(b...  218 us
    pallas_call x1, Pallas kernels, last_sums(): pl.pallas_call(functools.partial(last_kernel, size, bits, chunks), out_sh...  118 us
    pallas_call x1, Pallas kernels, feed_back(): pl.pallas_call(functools.partial(back_kernel, size, bits, chunks), out_sh...  114 us
    pallas_call x1, Pallas kernels, first_part(): pl.pallas_call(functools.partial(first_kernel, size, chunks, heads), out_...  95.6 us
    pallas_call x1, Pallas kernels, retain_back(): pl.pallas_call(functools.partial(retain_kernel, size, bits, heads), out_s...  61.8 us
    convert_element_type x4, other arithmetic, per_device(): item.astype(jnp.float32)  15.2 us
    transpose x2, other arithmetic, per_device(): grad_valuew, grad_gatew, grad_hgate, grad_hup = (item.T for item in (grad...  14 us

profile of v5, /device:TPU:0, one launch (start us, length us, event | category | flops | bytes accessed | tf_op | source)
XLA Modules:
  0.0 646.5 jit_solution(6012052840105460314)
XLA Ops:
  0.6 0.5 log-plus-one_negate_fusion.rates_ref
  1.2 1.7 copy.29.column_ref
  2.9 95.6 %shard_map.254 = (bf16[4,256,2048]{2,1,0:T(8,128)(2,1)}, bf16[4,256,512]{2,1,0:T(8,128)(2,1)}, bf16[4,256,512]{2,1,0:T(8,128)(2,1)}, bf16[2,4,256,432]{3,2,1,0:T...) custom-call(bf16[256,2048]{1,0:T(8,128)(2,1)} %tokens_ref.3, ...), custom_call_target="tpu_custom_call" | custom-call | flops 8589934592 | bytes 67108864 | tf_op jit(solution)/shard_map/pallas_call | solution.py:1531
  98.5 217.6 %shard_map.255 = (bf16[4,256,2048]{2,1,0:T(8,128)(2,1)}, bf16[4,256,2048]{2,1,0:T(8,128)(2,1)}, bf16[4,256,864]{2,1,0:T(8,128)(2,1)}, bf16[4,256,864]{2,1,0:T(8,...) custom-call(bf16[4,256,864]{2,1,0:T(8,128)(2,1)} %get-tuple-element., ...), custom_call_target="tpu_custom_call" | custom-call | flops 25367150592 | bytes 67108864 | tf_op jit(solution)/shard_map/pallas_call | solution.py:766
  316.1 114.0 %shard_map.256 = (bf16[4,256,2048]{2,1,0:T(8,128)(2,1)}, f32[2,4,256,432]{3,2,1,0:T(8,128)}, bf16[256,2048]{1,0:T(8,128)(2,1)}, bf16[864,2048]{1,0:T(8,128)(2,1)...) custom-call(bf16[4,256,2048]{2,1,0:T(8,128)(2,1)} %get-tuple-element.51.outp_hbm, bf16[864,2048]{1,0:T(8,128)(2,1)} %out_hbm.3, ...), custom_call_target="tpu_custom_call" | custom-call | flops 3623878656 | bytes 67108864 | tf_op jit(solution)/shard_map/pallas_call | solution.py:1003
  430.1 61.8 %shard_map.257 = (bf16[4,256,512]{2,1,0:T(8,128)(2,1)}, bf16[4,256,512]{2,1,0:T(8,128)(2,1)}, bf16[4,256,864]{2,1,0:T(8,128)(2,1)}, bf16[4,256,864]{2,1,0:T(8,12...) custom-call(bf16[4,256,512]{2,1,0:T(8,128)(2,1)} %get-tuple-element.60.queries_hbm, ...), custom_call_target="tpu_custom_call" | custom-call | flops 17179869184 | bytes 67108864 | tf_op jit(solution)/shard_map/pallas_call | solution.py:1816
  491.9 118.3 %shard_map.258 = (f32[256,2048]{1,0:T(8,128)}, f32[8,2048]{1,0:T(8,128)}, bf16[864,2048]{1,0:T(8,128)(2,1)}, bf16[864,2048]{1,0:T(8,128)(2,1)}, bf16[2048,512]{1,0:T(8,128)(2,1)}, /*index=5*/bf16[2048,512]{1,0:T(8,128)(2,1)}) custom-call(bf16[4,256,2048]{2,1,0:T(8,128)(2,1)} %get-tuple-element.68.dfirst_hbm, bf16[256,2048]{1,0:T(8,128)(2,1)} %tokens_ref.3, ...), custom_call_target="tpu_custom_call" | custom-call | flops 1073741824 | bytes 67108864 | tf_op jit(solution)/shard_map/pallas_call | solution.py:1252
  610.2 0.0 copy-start.6
  610.2 1.7 fusion
  611.9 4.2 convert_element_type.20
  616.1 0.0 copy-done.6
  616.1 2.6 convert_element_type.21
  618.8 0.5 copy-done.1
  619.3 3.9 convert_element_type.22
  623.1 0.0 copy-done
  623.1 4.5 convert_element_type.23
  627.6 0.0 copy-done.4
  627.6 1.1 copy-done.5
  628.8 7.0 %convert_bitcast_fusion.2 = (f32[2048,864]{0,1:T(8,128)}, f32[2048,864]{0,1:T(8,128)}) fusion(bf16[864,2048]{1,0:T(8,128)(2,1)S(1)} %copy-done.5, bf16[864,2048]{1,0:T(8,128)(2,1)S(1)} %copy-done.4), kind=kLoop, calls=%fused_computation.2 | loop fusion | flops 3538944 | bytes 21233664 | tf_op jit(solution)/shard_map/transpose | solution.py:1955
  635.8 7.0 %convert_bitcast_fusion = (f32[2048,864]{0,1:T(8,128)}, f32[2048,864]{0,1:T(8,128)}) fusion(bf16[864,2048]{1,0:T(8,128)(2,1)S(1)} %copy-done.3, bf16[864,2048]{1,0:T(8,128)(2,1)S(1)} %copy-done.2), kind=kLoop, calls=%fused_computation | loop fusion | flops 3538944 | bytes 21233664 | tf_op jit(solution)/shard_map/transpose | solution.py:1955
  642.8 0.0 copy-done.8
  642.8 1.0 copy.32
  643.7 1.0 copy-done.7
  644.7 1.3 copy.33
  (10 shorter events, 0.0 us)
Async XLA Ops:
  610.2 5.9 copy-start.6
  616.1 3.1 copy-start.1
  619.3 3.9 copy-start
  623.1 4.5 copy-start.4
  623.1 5.6 copy-start.5
  628.8 7.0 %copy-start.2 = (bf16[864,2048]{1,0:T(8,128)(2,1)S(1)}, bf16[864,2048]{1,0:T(8,128)(2,1)}, u32[]{:S(2)}) copy-start(bf16[864,2048]{1,0:T(8,128)(2,1)} %get-tuple-element.83) | copy-start | bytes 10616836
  628.8 7.0 %copy-start.3 = (bf16[864,2048]{1,0:T(8,128)(2,1)S(1)}, bf16[864,2048]{1,0:T(8,128)(2,1)}, u32[]{:S(2)}) copy-start(bf16[864,2048]{1,0:T(8,128)(2,1)} %get-tuple-element.84) | copy-start | bytes 10616836
  635.8 7.0 %copy-start.8 = (bf16[256,2048]{1,0:T(8,128)(2,1)S(1)}, bf16[256,2048]{1,0:T(8,128)(2,1)}, u32[]{:S(2)}) copy-start(bf16[256,2048]{1,0:T(8,128)(2,1)} %get-tuple-element.108) | copy-start | bytes 3145732
  642.8 2.0 copy-start.7

commit v6 on v5

--- a/solution.py
+++ b/solution.py
@@ -19,9 +19,11 @@
 
 MESH = pl.DeviceIdType.MESH
 VMEM_BYTES = 60 * 2**20
-TILE = 256
+TILE = 1024
 LINE = 16
 BAND = 64
+ACT = 64
+WHOLE = 256
 
 
 def for_columns(width, body):
@@ -37,7 +39,9 @@
         body(full * TILE, width % TILE)
 
 
-def for_rows(count, body, size=LINE):
+def for_rows(count, body, size=None):
+    size = min(count, size or BAND)
+
     def step(index, carry):
         body(pl.ds(pl.multiple_of(index * size, LINE), size))
         return carry
@@ -98,7 +102,7 @@
 
     def add(self, target, chunk):
         def body(rows):
-            at = pl.ds(chunk * self.rows + rows.start, LINE)
+            at = pl.ds(chunk * self.rows + rows.start, rows.size)
             total = self.part[target, at, :].astype(jnp.float32)
             total = total + self.inbox[target, at, :].astype(jnp.float32)
             self.part[target, at, :] = total.astype(jnp.bfloat16)
@@ -441,32 +445,31 @@
 
 ORDERS = {
     ("first", 4, 4, 2): (
-        0, 1, 2, 4, 4, 0, 0, 4, 4, 2, 2, 4, 0, 1, 4, 3, 4, 0, 2, 2, 0, 4, 1, 0,
-        2, 2, 2, 0, 0, 2, 2, 1, 0, 0, 2, 3, 3, 2, 1, 1, 1, 1, 1, 0, 1, 1, 1, 3,
-        3, 3, 3, 3, 3, 3, 3, 3,
+        0, 1, 0, 2, 1, 3, 4, 0, 1, 2, 0, 2, 0, 0, 4, 4, 4, 3, 0, 3, 0, 4, 0, 4,
+        4, 2, 1, 2, 3, 1, 3, 6, 2, 1, 4, 1, 2, 0, 2, 2, 0, 1, 2, 1, 0, 1, 3, 3,
+        3, 3, 3, 1, 3, 2, 3, 1, 2, 5, 5, 5, 6, 6, 5, 5, 5, 5, 5, 5, 6, 6, 6, 6,
     ),
     ("feed", 4, 4): (
-        4, 6, 4, 0, 5, 4, 4, 0, 4, 6, 5, 0, 5, 0, 0, 2, 5, 6, 1, 2, 0, 3, 4, 4,
-        6, 1, 6, 7, 5, 0, 6, 1, 1, 5, 2, 0, 0, 1, 3, 2, 0, 1, 7, 3, 3, 0, 5, 1,
-        0, 2, 0, 1, 0, 3, 2, 0, 0, 1, 1, 1, 3, 0, 1, 1, 1, 2, 2, 1, 1, 2, 1, 6,
-        0, 2, 3, 3, 2, 7, 7, 2, 2, 2, 3, 2, 2, 1, 3, 3, 7, 0, 0, 2, 3, 3, 1, 2,
-        7, 1, 7, 0, 3, 1, 3, 3, 3, 3, 2, 2, 0, 3, 2, 3, 3, 2, 1, 3,
+        4, 0, 5, 1, 6, 0, 4, 5, 0, 5, 0, 0, 4, 4, 5, 1, 0, 2, 3, 5, 6, 4, 0, 1,
+        6, 0, 0, 2, 0, 4, 4, 5, 0, 1, 0, 2, 1, 5, 6, 2, 2, 0, 1, 2, 3, 1, 1, 0,
+        0, 0, 1, 2, 1, 1, 3, 1, 3, 3, 2, 0, 1, 1, 3, 1, 1, 1, 2, 2, 2, 2, 0, 2,
+        2, 3, 2, 3, 2, 3, 2, 1, 6, 3, 3, 1, 1, 0, 2, 3, 0, 6, 0, 6, 1, 3, 3, 3,
+        3, 3, 3, 2, 2, 1, 3, 3, 0, 2, 3, 2, 3,
     ),
     ("back", 4, 4, 3): (
-        0, 1, 8, 8, 8, 8, 4, 5, 2, 0, 9, 9, 3, 8, 9, 1, 9, 1, 10, 10, 0, 10, 9, 10,
-        0, 10, 8, 4, 9, 6, 0, 0, 9, 8, 5, 10, 2, 10, 7, 4, 0, 8, 3, 8, 4, 5, 10, 2,
-        10, 9, 3, 5, 1, 9, 2, 10, 1, 10, 8, 2, 8, 3, 1, 4, 1, 5, 6, 9, 9, 7, 3, 7,
-        7, 10, 0, 1, 2, 2, 6, 8, 3, 6, 5, 7, 6, 3, 2, 9, 3, 4, 10, 8, 7, 9, 6,
+        0, 8, 8, 8, 8, 1, 4, 9, 9, 9, 9, 0, 8, 10, 10, 5, 10, 1, 0, 2, 0, 9, 10, 10,
+        1, 4, 8, 1, 8, 9, 3, 9, 5, 10, 0, 10, 2, 8, 8, 1, 3, 5, 9, 5, 9, 4, 3, 2,
+        6, 1, 10, 10, 0, 8, 2, 7, 8, 9, 9, 0, 3, 6, 4, 2, 5, 0, 10, 3, 10, 1, 2, 1,
+        3, 3, 4, 7, 7, 8, 7, 2, 9, 4, 6, 6, 7, 5, 8, 6, 2, 10, 7, 3, 9, 10, 6,
     ),
     ("retain", 4, 3, 2): (
-        0, 0, 0, 0, 1, 1, 0, 1, 1, 1, 0, 0, 1, 1, 0, 0, 1, 0, 0, 1, 1, 1, 0, 1,
-        0,
+        0, 0, 0, 0, 0, 1, 1, 0, 0, 1, 0, 0, 0, 0, 1, 1, 1, 1, 0, 1, 0,
     ),
     ("last", 4, 4, 3): (
-        0, 4, 4, 4, 4, 5, 5, 2, 4, 5, 5, 6, 6, 6, 5, 6, 3, 6, 4, 4, 1, 0, 6, 7,
-        2, 5, 5, 7, 4, 4, 3, 2, 5, 5, 6, 2, 7, 6, 3, 7, 4, 4, 3, 0, 2, 3, 6, 5,
-        6, 5, 1, 0, 4, 1, 0, 1, 7, 7, 4, 6, 1, 6, 5, 2, 7, 3, 7, 0, 5, 1, 8, 6,
-        8, 7, 8, 6, 7,
+        4, 4, 4, 4, 0, 6, 6, 4, 6, 6, 7, 5, 6, 2, 7, 5, 5, 5, 4, 4, 6, 0, 7, 7,
+        5, 2, 0, 0, 4, 4, 3, 6, 2, 2, 6, 5, 5, 1, 4, 2, 4, 0, 3, 7, 7, 6, 6, 5,
+        5, 1, 1, 7, 7, 1, 0, 3, 5, 1, 5, 3, 7, 6, 4, 3, 7, 1, 6, 2, 3, 8, 5, 8,
+        4, 6, 8, 5, 6,
     ),
 }
 
@@ -502,6 +505,7 @@
     out_hbm,
     tokens_hbm,
     seed_hbm,
+    seed_first_hbm,
     gate_hbm,
     up_hbm,
     down_hbm,
@@ -555,11 +559,12 @@
             (
                 (mixed_hbm, mixed),
                 (out_hbm, out_weight),
-                (seed_hbm, seeds.at[me]),
+                (seed_hbm.at[pl.ds(rows, own - rows)], seeds.at[me, pl.ds(rows, own - rows)]),
                 (tokens_hbm, tokens),
                 (gate_hbm, hidden_gate),
                 (up_hbm, hidden_up),
                 (down_hbm, hidden_down),
+                (seed_first_hbm, seeds.at[:, pl.ds(0, rows)]),
             )
         )
     ]
@@ -615,7 +620,7 @@
         scatter.arrive(chunk)
 
         def body(block):
-            here = pl.ds(chunk * rows + block.start, LINE)
+            here = pl.ds(chunk * rows + block.start, block.size)
             middle = tokens[here, :].astype(jnp.float32) + scatter.total(here)
             middle_ref[here, :] = middle
             centered = middle - jnp.mean(middle, axis=-1, keepdims=True)
@@ -638,7 +643,7 @@
         store(0, chunk).start()
 
     def feed_seed(chunk):
-        need(6)
+        need(6, 7)
 
         def body(start, width):
             columns = pl.ds(start, width)
@@ -663,12 +668,12 @@
                 GELU_SCALE * (1.0 + 3.0 * 0.044715 * (gate * gate))
             )
             owner = block.start // rows
-            inside = pl.ds(block.start - owner * rows, LINE)
+            inside = pl.ds(block.start - owner * rows, block.size)
             inner[slot, owner, inside, :] = (active * lin).astype(jnp.bfloat16)
             dlin[slot, owner, inside, :] = (grad * active).astype(jnp.bfloat16)
             dgate[slot, owner, inside, :] = (grad * lin * slope).astype(jnp.bfloat16)
 
-        for_rows(size * rows, body)
+        for_rows(size * rows, body, min(ACT, rows))
         for kind in range(2, 5):
             store(kind, chunk).start()
 
@@ -705,7 +710,7 @@
         scatter_back.arrive(chunk)
 
         def body(block):
-            here = pl.ds(chunk * rows + block.start, LINE)
+            here = pl.ds(chunk * rows + block.start, block.size)
             middle = middle_ref[here, :]
             centered = middle - jnp.mean(middle, axis=-1, keepdims=True)
             scale = lax.rsqrt(jnp.mean(centered * centered, axis=-1, keepdims=True) + EPS)
@@ -739,20 +744,21 @@
         )
         if chunk:
             after[chunk, first_feed] = ((chunk - 1, first_feed + 5),)
-        after[chunk, first_feed + 1] = ((chunks + chunk, 2 * size - 1),)
-    for chunk in range(chunks):
+            after[chunk, first_feed + 1] = ((chunks + chunk - 1, 2 * size - 1),)
+    for chunk in range(1, chunks):
         streams.append([functools.partial(begin_seed, chunk), *gather_seed.calls(chunk)])
     sums_ref[...] = jnp.zeros_like(sums_ref)
     run_streams(streams, ORDERS.get(("feed", size, chunks)), after)
     for chunk in range(chunks):
         scatter_back.drain(chunk)
         gather.drain(chunk)
-        gather_seed.drain(chunk)
+        if chunk:
+            gather_seed.drain(chunk)
         for kind in range(6 if chunk >= chunks - 2 else 2):
             store(kind, chunk).wait()
 
 
-def feed_forward(size, chunks, mixed, out_weight, tokens, cotangent, hidden_gate, hidden_up, hidden_down, gain, bias):
+def feed_forward(size, chunks, mixed, out_weight, tokens, cotangent, seed_first, hidden_gate, hidden_up, hidden_down, gain, bias):
     own, depth = tokens.shape
     hidden = hidden_gate.shape[0]
     rows = own // chunks
@@ -777,7 +783,7 @@
             jax.ShapeDtypeStruct((own, depth), low),
             jax.ShapeDtypeStruct((8, depth), full),
         ),
-        in_specs=[pl.BlockSpec(memory_space=pl.ANY)] * 7
+        in_specs=[pl.BlockSpec(memory_space=pl.ANY)] * 8
         + [pl.BlockSpec(memory_space=pltpu.VMEM)] * 2,
         out_specs=(pl.BlockSpec(memory_space=pl.ANY),) * 6
         + (pl.BlockSpec(memory_space=pltpu.VMEM),) * 4,
@@ -799,7 +805,7 @@
             pltpu.VMEM(thin, low),
             pltpu.VMEM(thin, low),
             pltpu.VMEM((2, size, rows, depth), low),
-            dma((7,)),
+            dma((8,)),
             dma((6, chunks)),
             dma((size, chunks)),
             dma((size + 1, chunks)),
@@ -816,7 +822,7 @@
         cost_estimate=pl.CostEstimate(
             flops=14 * size * own * depth * hidden, bytes_accessed=2**26, transcendentals=0
         ),
-    )(mixed, out_weight, tokens, cotangent, hidden_gate, hidden_up, hidden_down, gain, bias)
+    )(mixed, out_weight, tokens, cotangent, seed_first, hidden_gate, hidden_up, hidden_down, gain, bias)
 
 
 def back_kernel(
@@ -915,7 +921,7 @@
         scatter.arrive(chunk)
 
         def body(block):
-            here = pl.ds(chunk * rows + block.start, LINE)
+            here = pl.ds(chunk * rows + block.start, block.size)
             output_ref[here, :] = (middle_ref[here, :] + scatter.total(here)).astype(jnp.bfloat16)
 
         for_rows(rows, body)
@@ -1042,7 +1048,10 @@
     size,
     bits,
     chunks,
-    dfirst_hbm,
+    query_hbm,
+    key_hbm,
+    value_hbm,
+    gate_hbm,
     tokens_ref,
     dmiddle_ref,
     gain_ref,
@@ -1066,6 +1075,10 @@
     dkeys,
     turned,
     slice_turned,
+    query_weight,
+    key_weight,
+    value_weight,
+    gate_weight,
     load_sem,
     line_send,
     line_recv,
@@ -1085,8 +1098,6 @@
     mine = lax.axis_index("dp")
     own = tokens_ref.shape[0]
     rows = own // chunks
-    load_first = pltpu.make_async_copy(dfirst_hbm, first_part, load_sem.at[0])
-    load_first.start()
     cube = CubeSum(
         bits,
         mine,
@@ -1100,7 +1111,7 @@
         cube_free,
     )
     loads = [
-        pltpu.make_async_copy(src, dst, load_sem.at[1 + index])
+        pltpu.make_async_copy(src, dst, load_sem.at[index])
         for index, (src, dst) in enumerate(
             (
                 (dvalues_hbm, dvalues),
@@ -1108,6 +1119,10 @@
                 (dgates_hbm, dgates),
                 (dqueries_hbm, dqueries),
                 (dkeys_hbm, dkeys),
+                (query_hbm, query_weight),
+                (key_hbm, key_weight),
+                (value_hbm, value_weight),
+                (gate_hbm, gate_weight),
             )
         )
     ]
@@ -1123,7 +1138,7 @@
         first.arrive(chunk)
 
         def body(block):
-            here = pl.ds(chunk * rows + block.start, LINE)
+            here = pl.ds(chunk * rows + block.start, block.size)
             values = tokens_ref[here, :].astype(jnp.float32)
             centered = values - jnp.mean(values, axis=-1, keepdims=True)
             scale = lax.rsqrt(jnp.mean(centered * centered, axis=-1, keepdims=True) + EPS)
@@ -1177,10 +1192,34 @@
         totals_ref[...] = jnp.sum(dp_box[...], axis=0)
 
     line_box[me] = sums_ref[...]
-    load_first.wait()
+    waited = set()
+
+    def need(*indices):
+        for index in indices:
+            if index not in waited:
+                waited.add(index)
+                loads[index].wait()
+
+    def combine(chunk):
+        need(0, 2, 3, 4, 5, 6, 7, 8)
+        at = pl.ds(chunk * rows, rows)
+
+        def flat(ref):
+            return ref[:, at, :].reshape(size * rows, ref.shape[-1])
+
+        def body(start, width):
+            columns = pl.ds(start, width)
+            total = dot_nt(flat(dqueries), query_weight[columns, :])
+            total = total + dot_nt(flat(dkeys), key_weight[columns, :])
+            total = total + dot_nn(flat(dvalues), value_weight[:, columns])
+            total = total + dot_nn(flat(dgates), gate_weight[:, columns])
+            first_part[:, at, columns] = total.astype(jnp.bfloat16).reshape(size, rows, width)
+
+        for_columns(first_part.shape[-1], body)
+        first.begin(chunk)
+
     def turn(which):
-        for index in ((0, 1), (2,))[which]:
-            loads[index].wait()
+        need(*((0, 1), (2,))[which])
         ref = (dvalues, dgates)[which]
         for owner in range(size):
             turned[:, pl.ds(owner * own, own)] = ref[owner].T
@@ -1189,9 +1228,7 @@
         return firsts[:, :, columns].reshape(size * own, columns.size)
 
     def make_tall(start):
-        if start == 0:
-            loads[3].wait()
-            loads[4].wait()
+        need(1, 3, 4)
         lines = cube_parts[2].shape[-2]
         for index in range(start, start + groups // 4):
             lead = tuple((index >> bit) & 1 for bit in range(bits - 1, -1, -1))
@@ -1206,7 +1243,7 @@
     for chunk in range(chunks):
         streams.append(
             [
-                functools.partial(first.begin, chunk),
+                functools.partial(combine, chunk),
                 *first.calls(chunk),
                 functools.partial(back, chunk),
             ]
@@ -1238,7 +1275,7 @@
     cube.drain()
 
 
-def last_sums(size, bits, chunks, dfirst, tokens, dmiddle, gain, sums, firsts, parts):
+def last_sums(size, bits, chunks, weights, tokens, dmiddle, gain, sums, firsts, parts):
     own, depth = tokens.shape
     low, full = jnp.bfloat16, jnp.float32
     dma = pltpu.SemaphoreType.DMA
@@ -1256,7 +1293,7 @@
             jax.ShapeDtypeStruct((8, depth), full),
             grads,
         ),
-        in_specs=[anywhere, vmem, vmem, vmem, vmem] + [anywhere] * 5,
+        in_specs=[anywhere] * 4 + [vmem] * 4 + [anywhere] * 5,
         out_specs=(vmem, vmem, many),
         scratch_shapes=[
             pltpu.VMEM((size, own, depth), low),
@@ -1267,7 +1304,8 @@
             *[pltpu.VMEM(part.shape, low) for part in parts],
             pltpu.VMEM((parts[0].shape[-1], group), low),
             pltpu.VMEM((depth // 2**bits, group), low),
-            dma((6,)),
+            *[pltpu.VMEM(weight.shape, low) for weight in weights],
+            dma((9,)),
             dma((size,)),
             dma((size,)),
             dma((2**bits,)),
@@ -1280,7 +1318,7 @@
             collective_id=2, has_side_effects=True, vmem_limit_bytes=VMEM_BYTES
         ),
         cost_estimate=pl.CostEstimate(flops=2**30, bytes_accessed=2**26, transcendentals=0),
-    )(dfirst, tokens, dmiddle, gain, sums, firsts, *parts)
+    )(*weights, tokens, dmiddle, gain, sums, firsts, *parts)
 
 
 def decay_rows(rate, column, row, first):
@@ -1308,6 +1346,7 @@
     chunks,
     heads,
     tokens_ref,
+    seed_hbm,
     gain_ref,
     bias_ref,
     column_ref,
@@ -1325,6 +1364,7 @@
     retained_hbm,
     mixed_hbm,
     table_hbm,
+    seeds_hbm,
     query_weight,
     key_weight,
     value_weight,
@@ -1337,6 +1377,7 @@
     retained,
     mixed,
     table,
+    seeds,
     raw,
     retain,
     load_sem,
@@ -1344,6 +1385,8 @@
     done_sem,
     ag_send,
     ag_recv,
+    seed_send,
+    seed_recv,
 ):
     me = lax.axis_index("tensor")
     own, depth = tokens_ref.shape
@@ -1353,6 +1396,7 @@
         (key_hbm, key_weight),
         (value_hbm, value_weight),
         (gate_hbm, gate_weight),
+        (seed_hbm.at[pl.ds(0, rows)], seeds.at[me]),
     )
     loads = [
         pltpu.make_async_copy(src, dst, load_sem.at[index])
@@ -1362,6 +1406,7 @@
         load.start()
     enter((), (size, me))
     gather = LineGather(size, me, rows, first, ag_send, ag_recv)
+    gather_seed = LineGather(size, me, rows, seeds, seed_send, seed_recv)
     waited = set()
 
     def need(index):
@@ -1397,7 +1442,7 @@
 
     def normalize(chunk):
         def body(block):
-            here = pl.ds(chunk * rows + block.start, LINE)
+            here = pl.ds(chunk * rows + block.start, block.size)
             tokens = tokens_ref[here, :].astype(jnp.float32)
             centered = tokens - jnp.mean(tokens, axis=-1, keepdims=True)
             scale = lax.rsqrt(jnp.mean(centered * centered, axis=-1, keepdims=True) + EPS)
@@ -1449,7 +1494,7 @@
                 rates_ref[head], column_ref[there, :], row_ref[:, :seen], block * own + part.start
             )
 
-        for_rows(own, body, BAND)
+        for_rows(own, body, WHOLE)
         store_head(3, head, block).start()
 
     def attend(head, block):
@@ -1463,7 +1508,7 @@
             total = jnp.sum(weighted, axis=-1, keepdims=True)
             retain[part, :seen] = (weighted * lax.rsqrt(total * total + 1.0)).astype(jnp.bfloat16)
 
-        for_rows(own, body, BAND)
+        for_rows(own, body, WHOLE)
         value = values[head, : block + 1].reshape(seen, VD)
         retained[head, block] = dot_nn(retain[:, :seen], value)
 
@@ -1473,11 +1518,24 @@
             value = (gate * sigmoid(gate) * normed).astype(jnp.bfloat16)
             mixed[block, part, pl.ds(head * VD, VD)] = value
 
-        for_rows(own, body_mix, BAND)
+        for_rows(own, body_mix, WHOLE)
         store_head(2, head, block).start()
         if head == heads - 1:
             store(3, block).start()
 
+    def flush():
+        for block in range(size):
+            for kind in range(3):
+                store(kind, block).start()
+            for head in range(heads):
+                for kind in range(2):
+                    store_head(kind, head, block).start()
+
+    def begin_seed():
+        need(4)
+        gather_seed.begin(0)
+
+    places = [(head, block) for head in range(heads) for block in range(size)]
     streams, after = [], {}
     for chunk in range(chunks):
         steps = [functools.partial(normalize, chunk), *gather.calls(chunk)]
@@ -1488,19 +1546,17 @@
             steps.append(functools.partial(project_value, chunk, head))
             steps.append(functools.partial(project_gate, chunk, head))
         streams.append(steps)
-    streams.append(
-        [functools.partial(tabulate, head, block) for head in range(heads) for block in range(size)]
-    )
+    streams.append([functools.partial(tabulate, *place) for place in places])
+    streams.append([flush] + [functools.partial(attend, *place) for place in places])
+    after[chunks + 1, 0] = [(chunk, len(streams[chunk])) for chunk in range(chunks)]
+    for index in range(len(places)):
+        after[chunks + 1, index + 1] = ((chunks, index + 1),)
+    streams.append([begin_seed, *gather_seed.calls(0)])
     run_streams(streams, ORDERS.get(("first", size, chunks, heads)), after)
-    for block in range(size):
-        for kind in range(3):
-            store(kind, block).start()
-        for head in range(heads):
-            for kind in range(2):
-                store_head(kind, head, block).start()
-    for head in range(heads):
-        for block in range(size):
-            attend(head, block)
+    store_seeds = pltpu.make_async_copy(seeds, seeds_hbm, load_sem.at[5])
+    store_seeds.start()
+    gather_seed.drain(0)
+    store_seeds.wait()
     for chunk in range(chunks):
         gather.drain(chunk)
     for block in range(size):
@@ -1511,7 +1567,7 @@
                 store_head(kind, head, block).wait()
 
 
-def first_part(size, chunks, tokens, gain, bias, segments, rates, query, key, value, gate):
+def first_part(size, chunks, tokens, seed, gain, bias, segments, rates, query, key, value, gate):
     own, depth = tokens.shape
     heads = query.shape[1] // KD
     rows = size * own
@@ -1527,22 +1583,25 @@
         ((heads, size, own, VD), full),
         ((size, own, heads * VD), low),
         ((heads, size, own, rows), full),
+        ((size, own // chunks, depth), low),
     )
     return pl.pallas_call(
         functools.partial(first_kernel, size, chunks, heads),
         out_shape=tuple(jax.ShapeDtypeStruct(*item) for item in shapes),
-        in_specs=[vmem] * 5 + [pl.BlockSpec(memory_space=pltpu.SMEM)] + [anywhere] * 4,
-        out_specs=(anywhere,) * 8,
+        in_specs=[vmem, anywhere] + [vmem] * 4 + [pl.BlockSpec(memory_space=pltpu.SMEM)] + [anywhere] * 4,
+        out_specs=(anywhere,) * 9,
         scratch_shapes=[pltpu.VMEM(item.shape, low) for item in (query, key, value, gate)]
         + [pltpu.VMEM(*item) for item in shapes]
         + [
             pltpu.VMEM((own, rows), full),
             pltpu.VMEM((own, rows), low),
-            dma((4,)),
+            dma((6,)),
             dma((4, size)),
             dma((4, heads, size)),
             dma((2, size, chunks)),
             dma((size, chunks)),
+            dma((2, size, 1)),
+            dma((size, 1)),
         ],
         compiler_params=pltpu.CompilerParams(
             collective_id=3, has_side_effects=True, vmem_limit_bytes=VMEM_BYTES
@@ -1550,6 +1609,7 @@
         cost_estimate=pl.CostEstimate(flops=2**33, bytes_accessed=2**26, transcendentals=0),
     )(
         tokens,
+        seed,
         gain,
         bias,
         segments.reshape(rows, 1),
@@ -1573,17 +1633,12 @@
     retained_hbm,
     dmixed_hbm,
     table_hbm,
-    query_hbm,
-    key_hbm,
-    value_hbm,
-    gate_hbm,
     mixed_hbm,
     branch_hbm,
     dqueries_hbm,
     dkeys_hbm,
     dvalues_hbm,
     dgates_hbm,
-    dfirst_hbm,
     totals_hbm,
     queries,
     keys,
@@ -1592,17 +1647,12 @@
     retained,
     dmixed,
     table,
-    query_weight,
-    key_weight,
-    value_weight,
-    gate_weight,
     mixed,
     branch,
     dqueries,
     dkeys,
     dvalues,
     dgates,
-    dfirst,
     turned,
     raw,
     grad,
@@ -1623,7 +1673,6 @@
     cube_free,
 ):
     own = queries.shape[1]
-    depth = query_weight.shape[0]
 
     def load_whole(kind):
         src, dst = (
@@ -1631,10 +1680,6 @@
             (keys_hbm, keys),
             (mixed_hbm, mixed),
             (branch_hbm, branch),
-            (query_hbm, query_weight),
-            (key_hbm, key_weight),
-            (value_hbm, value_weight),
-            (gate_hbm, gate_weight),
         )[kind]
         return pltpu.make_async_copy(src, dst, load_sem.at[kind])
 
@@ -1660,7 +1705,6 @@
             (dkeys, dkeys_hbm),
             (dvalues, dvalues_hbm),
             (dgates, dgates_hbm),
-            (dfirst, dfirst_hbm),
         )[kind]
         return pltpu.make_async_copy(src.at[block], dst.at[block], store_sem.at[kind, block])
 
@@ -1670,8 +1714,6 @@
     for kind in range(2, 4):
         load_whole(kind).start()
     load_blocks(1)
-    for kind in range(4, 8):
-        load_whole(kind).start()
     cube = CubeSum(
         bits,
         lax.axis_index("dp"),
@@ -1712,7 +1754,7 @@
             )
             dretained[part, :] = value.astype(jnp.bfloat16)
 
-        for_rows(own, body_mix, BAND)
+        for_rows(own, body_mix, WHOLE)
         query = queries[block, :, lanes]
         key = keys[: block + 1, :, lanes].reshape(seen, KD)
         raw[:, :seen] = dot_nt(query, key)
@@ -1730,7 +1772,7 @@
             along = along * total * inverse * inverse
             dscores[part, :seen] = (decay * inverse * (dretain - along)).astype(jnp.bfloat16)
 
-        for_rows(own, body, BAND)
+        for_rows(own, body, WHOLE)
         dquery = dot_nn(dscores[:, :seen], key) * (KD**-0.5)
         dqueries[block, :, lanes] = dquery.astype(jnp.bfloat16)
         for other in range(block + 1):
@@ -1750,24 +1792,9 @@
                 dkeys[other, :, lanes] = (dkey_sum[other] * (KD**-0.5)).astype(jnp.bfloat16)
                 there = pl.ds(head * VD, VD)
                 dvalues[other, :, there] = dvalue_sum[other].astype(jnp.bfloat16)
-
-    def combine(block):
-        if block == 0:
-            for kind in range(4, 8):
-                load_whole(kind).wait()
-        for kind in range(4):
-            store(kind, block).start()
-
-        def body(start, width):
-            columns = pl.ds(start, width)
-            total = dot_nt(dqueries[block], query_weight[columns, :])
-            total = total + dot_nt(dkeys[block], key_weight[columns, :])
-            total = total + dot_nn(dvalues[block], value_weight[:, columns])
-            total = total + dot_nn(dgates[block], gate_weight[:, columns])
-            dfirst[block, :, columns] = total.astype(jnp.bfloat16)
-
-        for_columns(depth, body)
-        store(4, block).start()
+                if head == heads - 1:
+                    for kind in range(4):
+                        store(kind, other).start()
 
     def turn():
         for kind in range(2, 4):
@@ -1781,26 +1808,24 @@
     steps = [
         functools.partial(attend, head, block) for head in range(heads) for block in range(size)
     ]
-    steps += [functools.partial(combine, block) for block in range(size)]
     sums = [turn, *cube.make_wide(0, turned, branch_columns), *cube.calls(0)]
     run_streams([sums, steps], ORDERS.get(("retain", size, bits, heads)), {})
     for block in range(size):
-        for kind in range(5):
+        for kind in range(4):
             store(kind, block).wait()
     cube.drain()
 
 
 def retain_back(
-    size, bits, queries, keys, values, gates, retained, dmixed, table, query, key, value, gate, mixed, branch
+    size, bits, queries, keys, values, gates, retained, dmixed, table, mixed, branch
 ):
     own = queries.shape[1]
     heads = values.shape[0]
-    rows, depth = size * own, query.shape[0]
+    rows, depth = size * own, branch.shape[-1]
     low, full = jnp.bfloat16, jnp.float32
     dma = pltpu.SemaphoreType.DMA
     anywhere = pl.BlockSpec(memory_space=pl.ANY)
-    inputs = (queries, keys, values, gates, retained, dmixed, table, query, key, value, gate)
-    inputs = inputs + (mixed, branch)
+    inputs = (queries, keys, values, gates, retained, dmixed, table, mixed, branch)
     slots = [
         jax.ShapeDtypeStruct((2,) + item.shape[2:], item.dtype) if 3 <= place < 7 else item
         for place, item in enumerate(inputs)
@@ -1811,13 +1836,12 @@
         keys.shape,
         (size, own, heads * VD),
         (size, own, heads * VD),
-        (size, own, depth),
     )
     return pl.pallas_call(
         functools.partial(retain_kernel, size, bits, heads),
         out_shape=tuple(jax.ShapeDtypeStruct(shape, low) for shape in shapes) + ([total],),
         in_specs=[anywhere] * len(inputs),
-        out_specs=(anywhere,) * 5 + ([anywhere],),
+        out_specs=(anywhere,) * 4 + ([anywhere],),
         scratch_shapes=[pltpu.VMEM(item.shape, item.dtype) for item in slots]
         + [pltpu.VMEM(shape, low) for shape in shapes]
         + [
@@ -1829,9 +1853,9 @@
             pltpu.VMEM((own, VD), low),
             pltpu.VMEM((size, own, KD), full),
             pltpu.VMEM((size, own, VD), full),
-            dma((8,)),
+            dma((4,)),
             dma((5, heads, size)),
-            dma((5, size)),
+            dma((4, size)),
         ]
         + cube_scratch(bits, [total.shape]),
         compiler_params=pltpu.CompilerParams(
@@ -1839,6 +1863,31 @@
         ),
         cost_estimate=pl.CostEstimate(flops=2**34, bytes_accessed=2**26, transcendentals=0),
     )(*inputs)
+
+
+def cast_kernel(count, *refs):
+    for src, dst in zip(refs[:count], refs[count:]):
+        dst[...] = src[...].astype(jnp.float32)
+
+
+def cast_all(items):
+    specs = []
+    for item in items:
+        blocks = 9 if item.shape[0] % (9 * LINE) == 0 else 8
+        specs.append(
+            pl.BlockSpec(
+                (item.shape[0] // blocks, item.shape[1]),
+                lambda step, last=blocks - 1: (jnp.minimum(step, last), 0),
+            )
+        )
+    return pl.pallas_call(
+        functools.partial(cast_kernel, len(items)),
+        out_shape=[jax.ShapeDtypeStruct(item.shape, jnp.float32) for item in items],
+        grid=(9,),
+        in_specs=specs,
+        out_specs=specs,
+        compiler_params=pltpu.CompilerParams(vmem_limit_bytes=VMEM_BYTES),
+    )(*items)
 
 
 def per_device(
@@ -1865,10 +1914,11 @@
         jnp.float32
     )
     rates = -jnp.log1p(-jnp.exp2(-5.0 - head_index))
-    first_all, queries, keys, values, gates, retained, mixed, table = first_part(
+    first_all, queries, keys, values, gates, retained, mixed, table, seed_first = first_part(
         size,
         CHUNKS,
         tokens,
+        cotangent,
         first_gain[None],
         first_bias[None],
         segments,
@@ -1898,6 +1948,7 @@
         out_weight,
         tokens,
         cotangent,
+        seed_first,
         hidden_gate.T,
         hidden_up.T,
         hidden_down,
@@ -1917,7 +1968,7 @@
         second_all,
         (inner, gate_in_low, lin_in_low),
     )
-    grad_queries, grad_keys, grad_values, grad_gates, grad_first, (grad_outw,) = retain_back(
+    grad_queries, grad_keys, grad_values, grad_gates, (grad_outw,) = retain_back(
         size,
         bits,
         queries,
@@ -1927,10 +1978,6 @@
         retained,
         grad_mixed,
         table,
-        query_weight,
-        key_weight,
-        value_weight.T,
-        gate_weight.T,
         mixed,
         branch_all,
     )
@@ -1938,7 +1985,7 @@
         size,
         bits,
         CHUNKS,
-        grad_first,
+        (query_weight, key_weight, value_weight.T, gate_weight.T),
         tokens,
         grad_middle,
         first_gain[None],
@@ -1947,10 +1994,16 @@
         (grad_values, grad_gates, grad_queries, grad_keys),
     )
     grad_sgain, grad_sbias, grad_fgain, grad_fbias = sums[0], sums[1], sums[2], sums[3]
-    grad_outw, grad_valuew, grad_gatew, grad_queryw, grad_keyw = (
-        item.astype(jnp.float32) for item in (grad_outw, *grads)
-    )
-    grad_hdown, grad_hgate, grad_hup = (item.astype(jnp.float32) for item in feed_grads)
+    (
+        grad_outw,
+        grad_valuew,
+        grad_gatew,
+        grad_queryw,
+        grad_keyw,
+        grad_hdown,
+        grad_hgate,
+        grad_hup,
+    ) = cast_all([grad_outw, *grads, *feed_grads])
     grad_valuew, grad_gatew, grad_hgate, grad_hup = (
         item.T for item in (grad_valuew, grad_gatew, grad_hgate, grad_hup)
     )

time: 656 us -> 631 us (0.962)
  other arithmetic: 29.7 us -> 0.53 us
    pallas_call x0 -> x1, Pallas kernels: none -> 25.8 us  [cast_all(): pl.pallas_call(functools.partial(cast_kernel, len(items)), out_shape=[jax...]
    convert_element_type x4 -> x0, other arithmetic: 15.2 us -> none  [per_device(): item.astype(jnp.float32)]
    transpose x2 -> x0, other arithmetic: 14 us -> none  [per_device(): grad_valuew, grad_gatew, grad_hgate, grad_hup = (item.T for item in (grad...]
    pallas_call x1, Pallas kernels: 218 us -> 204 us  [feed_forward(): pl.pallas_call(functools.partial(feed_kernel, size, chunks), out_shape=(b...]
    pallas_call x1, Pallas kernels: 61.8 us -> 54.3 us  [retain_back(): pl.pallas_call(functools.partial(retain_kernel, size, bits, heads), out_s...]
where the time goes in v6:
time: 631 us; the launch traced here: 621 us
  Pallas kernels  613 us (97%)
  local copies, waits for them, and re-layouts  6.6 us (1%)
    pallas_call x1, Pallas kernels, feed_forward(): pl.pallas_call(functools.partial(feed_kernel, size, chunks), out_shape=(b...  204 us
    pallas_call x1, Pallas kernels, last_sums(): pl.pallas_call(functools.partial(last_kernel, size, bits, chunks), out_sh...  122 us
    pallas_call x1, Pallas kernels, feed_back(): pl.pallas_call(functools.partial(back_kernel, size, bits, chunks), out_sh...  114 us
    pallas_call x1, Pallas kernels, first_part(): pl.pallas_call(functools.partial(first_kernel, size, chunks, heads), out_...  93.1 us
    pallas_call x1, Pallas kernels, retain_back(): pl.pallas_call(functools.partial(retain_kernel, size, bits, heads), out_s...  54.3 us
    pallas_call x1, Pallas kernels, cast_all(): pl.pallas_call(functools.partial(cast_kernel, len(items)), out_shape=[jax...  25.8 us

profile of v6, /device:TPU:0, one launch (start us, length us, event | category | flops | bytes accessed | tf_op | source)
XLA Modules:
  0.0 621.3 jit_solution(11061420377114803537)
XLA Ops:
  0.6 0.5 log-plus-one_negate_fusion.rates_ref
  1.2 1.7 copy.29.column_ref
  2.9 93.1 %shard_map.254 = (bf16[4,256,2048]{2,1,0:T(8,128)(2,1)}, bf16[4,256,512]{2,1,0:T(8,128)(2,1)}, bf16[4,256,512]{2,1,0:T(8,128)(2,1)}, bf16[2,4,256,432]{3,2,1,0:T...) custom-call(bf16[256,2048]{1,0:T(8,128)(2,1)} %tokens_ref.3, ...), custom_call_target="tpu_custom_call" | custom-call | flops 8589934592 | bytes 67108864 | tf_op jit(solution)/shard_map/pallas_call | solution.py:1588
  96.0 203.8 %shard_map.255 = (bf16[4,256,2048]{2,1,0:T(8,128)(2,1)}, bf16[4,256,2048]{2,1,0:T(8,128)(2,1)}, bf16[4,256,864]{2,1,0:T(8,128)(2,1)}, bf16[4,256,864]{2,1,0:T(8,...) custom-call(bf16[4,256,864]{2,1,0:T(8,128)(2,1)} %get-tuple-element., ...), custom_call_target="tpu_custom_call" | custom-call | flops 25367150592 | bytes 67108864 | tf_op jit(solution)/shard_map/pallas_call | solution.py:772
  299.8 113.9 %shard_map.256 = (bf16[4,256,2048]{2,1,0:T(8,128)(2,1)}, f32[2,4,256,432]{3,2,1,0:T(8,128)}, bf16[256,2048]{1,0:T(8,128)(2,1)}, bf16[864,2048]{1,0:T(8,128)(2,1)...) custom-call(bf16[4,256,2048]{2,1,0:T(8,128)(2,1)} %get-tuple-element.60.outp_hbm, bf16[864,2048]{1,0:T(8,128)(2,1)} %out_hbm.3, ...), custom_call_target="tpu_custom_call" | custom-call | flops 3623878656 | bytes 67108864 | tf_op jit(solution)/shard_map/pallas_call | solution.py:1009
  413.7 54.3 %shard_map.257 = (bf16[4,256,512]{2,1,0:T(8,128)(2,1)}, bf16[4,256,512]{2,1,0:T(8,128)(2,1)}, bf16[4,256,864]{2,1,0:T(8,128)(2,1)}, bf16[4,256,864]{2,1,0:T(8,128)(2,1)}, bf16[864,2048]{1,0:T(8,128)(2,1)}) custom-call(bf16[4,256,512]{2,1,0:T(8,128)(2,1)} %get-tuple-element.72.queries_hbm, bf16[4,256,512]{2,1,0:T(8,128)(2,1)} %get-tuple-element.73.keys_hbm, ...), custom_call_target="tpu_custom_call" | custom-call | flops 17179869184 | bytes 67108864 | tf_op jit(solution)/shard_map/pallas_call | solution.py:1840
  468.0 122.1 %shard_map.258 = (f32[256,2048]{1,0:T(8,128)}, f32[8,2048]{1,0:T(8,128)}, bf16[864,2048]{1,0:T(8,128)(2,1)}, bf16[864,2048]{1,0:T(8,128)(2,1)}, bf16[2048,512]{1,0:T(8,128)(2,1)}, /*index=5*/bf16[2048,512]{1,0:T(8,128)(2,1)}) custom-call(bf16[2048,512]{1,0:T(8,128)(2,1)} %query_hbm.3, bf16[2048,512]{1,0:T(8,128)(2,1)} %key_hbm.3, ...), custom_call_target="tpu_custom_call" | custom-call | flops 1073741824 | bytes 67108864 | tf_op jit(solution)/shard_map/pallas_call | solution.py:1289
  590.1 1.6 fusion
  591.8 0.0 copy-start.1
  591.8 25.8 %shard_map.259 = (f32[864,2048]{1,0:T(8,128)}, f32[864,2048]{1,0:T(8,128)}, f32[864,2048]{1,0:T(8,128)}, f32[2048,512]{1,0:T(8,128)}, f32[2048,512]{1,0:T(8,128)...) custom-call(bf16[864,2048]{1,0:T(8,128)(2,1)} %get-tuple-element.86.refs_0_, ...), custom_call_target="tpu_custom_call" | custom-call | tf_op jit(solution)/shard_map/pallas_call | solution.py:1883
  617.6 0.0 copy-start
  617.6 0.0 copy-done.1
  617.6 1.0 copy.32
  618.6 1.0 copy-done
  619.5 1.3 copy.33
Async XLA Ops:
  591.8 25.8 %copy-start.1 = (bf16[256,2048]{1,0:T(8,128)(2,1)S(1)}, bf16[256,2048]{1,0:T(8,128)(2,1)}, u32[]{:S(2)}) copy-start(bf16[256,2048]{1,0:T(8,128)(2,1)} %get-tuple-element.120) | copy-start | bytes 3145732
  617.6 2.0 copy-start

commit v7 on v6

--- a/solution.py
+++ b/solution.py
@@ -24,6 +24,7 @@
 BAND = 64
 ACT = 64
 WHOLE = 256
+BLOCKS = (1, 8, 9, 16, 18)
 
 
 def for_columns(width, body):
@@ -396,13 +397,15 @@
     return count // (2 * LINE) * LINE
 
 
+def halves(rows):
+    first = rows // 2 // LINE * LINE
+    return ((0, first), (first, rows - first))
+
+
 def for_blocks(count, columns, body):
-    size = LINE
-    while count % (2 * size) == 0 and 2 * size * columns <= 2**14:
-        size *= 2
-    for factor in (3, 5):
-        if count % (factor * size) == 0 and factor * size * columns <= 2**14:
-            size *= factor
+    lines = count // LINE
+    fits = [part for part in range(1, lines + 1) if lines % part == 0 and part * LINE * columns <= 2**16]
+    size = fits[-1] * LINE
 
     def step(index, carry):
         body(pl.multiple_of(index * size, LINE), size)
@@ -463,7 +466,8 @@
         3, 3, 4, 7, 7, 8, 7, 2, 9, 4, 6, 6, 7, 5, 8, 6, 2, 10, 7, 3, 9, 10, 6,
     ),
     ("retain", 4, 3, 2): (
-        0, 0, 0, 0, 0, 1, 1, 0, 0, 1, 0, 0, 0, 0, 1, 1, 1, 1, 0, 1, 0,
+        0, 0, 0, 0, 1, 1, 1, 0, 2, 1, 2, 2, 0, 0, 2, 1, 1, 0, 0, 1, 1, 0, 0, 2,
+        1, 1, 2, 2, 0, 2, 1, 0, 1,
     ),
     ("last", 4, 4, 3): (
         4, 4, 4, 4, 0, 6, 6, 4, 6, 6, 7, 5, 6, 2, 7, 5, 5, 5, 4, 4, 6, 0, 7, 7,
@@ -1717,7 +1721,7 @@
     cube = CubeSum(
         bits,
         lax.axis_index("dp"),
-        totals_hbm,
+        [ref.at[pl.ds(*half)] for ref in totals_hbm for half in halves(ref.shape[0])],
         cube_parts,
         cube_firsts,
         cube_nexts,
@@ -1808,8 +1812,13 @@
     steps = [
         functools.partial(attend, head, block) for head in range(heads) for block in range(size)
     ]
-    sums = [turn, *cube.make_wide(0, turned, branch_columns), *cube.calls(0)]
-    run_streams([sums, steps], ORDERS.get(("retain", size, bits, heads)), {})
+    streams = []
+    for index, (start, count) in enumerate(halves(turned.shape[0])):
+        part = turned.at[pl.ds(start, count)]
+        streams.append([*cube.make_wide(index, part, branch_columns), *cube.calls(index)])
+    streams[0].insert(0, turn)
+    streams.append(steps)
+    run_streams(streams, ORDERS.get(("retain", size, bits, heads)), {(1, 0): ((0, 1),)})
     for block in range(size):
         for kind in range(4):
             store(kind, block).wait()
@@ -1857,7 +1866,7 @@
             dma((5, heads, size)),
             dma((4, size)),
         ]
-        + cube_scratch(bits, [total.shape]),
+        + cube_scratch(bits, [(half[1], depth) for half in halves(total.shape[0])]),
         compiler_params=pltpu.CompilerParams(
             collective_id=4, has_side_effects=True, vmem_limit_bytes=VMEM_BYTES
         ),
@@ -1867,13 +1876,16 @@
 
 def cast_kernel(count, *refs):
     for src, dst in zip(refs[:count], refs[count:]):
-        dst[...] = src[...].astype(jnp.float32)
-
-
-def cast_all(items):
+        dst[...] = src[...].astype(dst.dtype)
+
+
+def cast_all(items, kept):
     specs = []
+    shapes = [jax.ShapeDtypeStruct(item.shape, jnp.float32) for item in items]
+    shapes += [jax.ShapeDtypeStruct(item.shape, item.dtype) for item in kept]
+    items = [*items, *kept]
     for item in items:
-        blocks = 9 if item.shape[0] % (9 * LINE) == 0 else 8
+        blocks = max(count for count in BLOCKS if item.shape[0] % (count * LINE) == 0)
         specs.append(
             pl.BlockSpec(
                 (item.shape[0] // blocks, item.shape[1]),
@@ -1882,8 +1894,8 @@
         )
     return pl.pallas_call(
         functools.partial(cast_kernel, len(items)),
-        out_shape=[jax.ShapeDtypeStruct(item.shape, jnp.float32) for item in items],
-        grid=(9,),
+        out_shape=shapes,
+        grid=(max(BLOCKS),),
         in_specs=specs,
         out_specs=specs,
         compiler_params=pltpu.CompilerParams(vmem_limit_bytes=VMEM_BYTES),
@@ -2003,7 +2015,9 @@
         grad_hdown,
         grad_hgate,
         grad_hup,
-    ) = cast_all([grad_outw, *grads, *feed_grads])
+        output,
+        grad_tokens,
+    ) = cast_all([grad_outw, *grads, *feed_grads], [output, grad_tokens])
     grad_valuew, grad_gatew, grad_hgate, grad_hup = (
         item.T for item in (grad_valuew, grad_gatew, grad_hgate, grad_hup)
     )

time: 631 us -> 624 us (0.989)
    pallas_call x1, Pallas kernels: 54.3 us -> 44.3 us  [retain_back(): pl.pallas_call(functools.partial(retain_kernel, size, bits, heads), out_s...]
where the time goes in v7:
time: 624 us; the launch traced here: 614 us
  Pallas kernels  609 us (98%)
    pallas_call x1, Pallas kernels, feed_forward(): pl.pallas_call(functools.partial(feed_kernel, size, chunks), out_shape=(b...  204 us
    pallas_call x1, Pallas kernels, last_sums(): pl.pallas_call(functools.partial(last_kernel, size, bits, chunks), out_sh...  124 us
    pallas_call x1, Pallas kernels, feed_back(): pl.pallas_call(functools.partial(back_kernel, size, bits, chunks), out_sh...  114 us
    pallas_call x1, Pallas kernels, first_part(): pl.pallas_call(functools.partial(first_kernel, size, chunks, heads), out_...  93.1 us
    pallas_call x1, Pallas kernels, retain_back(): pl.pallas_call(functools.partial(retain_kernel, size, bits, heads), out_s...  44.3 us
    pallas_call x1, Pallas kernels, cast_all(): pl.pallas_call(functools.partial(cast_kernel, len(items)), out_shape=shap...  29.3 us

profile of v7, /device:TPU:0, one launch (start us, length us, event | category | flops | bytes accessed | tf_op | source)
XLA Modules:
  0.0 614.1 jit_solution(8416600754074741534)
XLA Ops:
  0.6 0.5 log-plus-one_negate_fusion.rates_ref
  1.2 1.7 copy.29.column_ref
  2.9 93.1 %shard_map.254 = (bf16[4,256,2048]{2,1,0:T(8,128)(2,1)}, bf16[4,256,512]{2,1,0:T(8,128)(2,1)}, bf16[4,256,512]{2,1,0:T(8,128)(2,1)}, bf16[2,4,256,432]{3,2,1,0:T...) custom-call(bf16[256,2048]{1,0:T(8,128)(2,1)} %tokens_ref.3, ...), custom_call_target="tpu_custom_call" | custom-call | flops 8589934592 | bytes 67108864 | tf_op jit(solution)/shard_map/pallas_call | solution.py:1592
  96.0 203.8 %shard_map.255 = (bf16[4,256,2048]{2,1,0:T(8,128)(2,1)}, bf16[4,256,2048]{2,1,0:T(8,128)(2,1)}, bf16[4,256,864]{2,1,0:T(8,128)(2,1)}, bf16[4,256,864]{2,1,0:T(8,...) custom-call(bf16[4,256,864]{2,1,0:T(8,128)(2,1)} %get-tuple-element., ...), custom_call_target="tpu_custom_call" | custom-call | flops 25367150592 | bytes 67108864 | tf_op jit(solution)/shard_map/pallas_call | solution.py:776
  299.8 114.4 %shard_map.256 = (bf16[4,256,2048]{2,1,0:T(8,128)(2,1)}, f32[2,4,256,432]{3,2,1,0:T(8,128)}, bf16[256,2048]{1,0:T(8,128)(2,1)}, bf16[864,2048]{1,0:T(8,128)(2,1)...) custom-call(bf16[4,256,2048]{2,1,0:T(8,128)(2,1)} %get-tuple-element.67.outp_hbm, bf16[864,2048]{1,0:T(8,128)(2,1)} %out_hbm.3, ...), custom_call_target="tpu_custom_call" | custom-call | flops 3623878656 | bytes 67108864 | tf_op jit(solution)/shard_map/pallas_call | solution.py:1013
  414.2 44.3 %shard_map.257 = (bf16[4,256,512]{2,1,0:T(8,128)(2,1)}, bf16[4,256,512]{2,1,0:T(8,128)(2,1)}, bf16[4,256,864]{2,1,0:T(8,128)(2,1)}, bf16[4,256,864]{2,1,0:T(8,128)(2,1)}, bf16[864,2048]{1,0:T(8,128)(2,1)}) custom-call(bf16[4,256,512]{2,1,0:T(8,128)(2,1)} %get-tuple-element.60.queries_hbm, bf16[4,256,512]{2,1,0:T(8,128)(2,1)} %get-tuple-element.61.keys_hbm, ...), custom_call_target="tpu_custom_call" | custom-call | flops 17179869184 | bytes 67108864 | tf_op jit(solution)/shard_map/pallas_call | solution.py:1849
  458.6 124.1 %shard_map.258 = (f32[256,2048]{1,0:T(8,128)}, f32[8,2048]{1,0:T(8,128)}, bf16[864,2048]{1,0:T(8,128)(2,1)}, bf16[864,2048]{1,0:T(8,128)(2,1)}, bf16[2048,512]{1,0:T(8,128)(2,1)}, /*index=5*/bf16[2048,512]{1,0:T(8,128)(2,1)}) custom-call(bf16[2048,512]{1,0:T(8,128)(2,1)} %query_hbm.3, bf16[2048,512]{1,0:T(8,128)(2,1)} %key_hbm.3, ...), custom_call_target="tpu_custom_call" | custom-call | flops 1073741824 | bytes 67108864 | tf_op jit(solution)/shard_map/pallas_call | solution.py:1293
  582.7 1.6 fusion
  584.3 29.3 %shard_map.259 = (f32[864,2048]{1,0:T(8,128)}, f32[864,2048]{1,0:T(8,128)}, f32[864,2048]{1,0:T(8,128)}, f32[2048,512]{1,0:T(8,128)}, f32[2048,512]{1,0:T(8,128)...) custom-call(bf16[864,2048]{1,0:T(8,128)(2,1)} %get-tuple-element.78., ...), custom_call_target="tpu_custom_call" | custom-call | tf_op jit(solution)/shard_map/pallas_call | solution.py:1895

commit v8 on v7

--- a/solution.py
+++ b/solution.py
@@ -404,7 +404,7 @@
 
 def for_blocks(count, columns, body):
     lines = count // LINE
-    fits = [part for part in range(1, lines + 1) if lines % part == 0 and part * LINE * columns <= 2**16]
+    fits = [part for part in range(1, lines + 1) if lines % part == 0 and part * LINE * columns <= 2**14]
     size = fits[-1] * LINE
 
     def step(index, carry):
@@ -521,10 +521,13 @@
     dgate_hbm,
     dlin_hbm,
     outp_hbm,
+    middle_hbm,
+    dmiddle_hbm,
+    branch_hbm,
+    sums_ref,
     middle_ref,
     dmiddle_ref,
     branch_ref,
-    sums_ref,
     mixed,
     out_weight,
     tokens,
@@ -544,6 +547,7 @@
     wide,
     load_sem,
     store_sem,
+    own_sem,
     rs_send,
     rs_recv,
     back_send,
@@ -732,6 +736,16 @@
             branch_ref[here, :] = dmiddle.astype(jnp.bfloat16)
 
         for_rows(rows, body)
+        for kind in range(3):
+            store_own(kind, chunk).start()
+
+    def store_own(kind, chunk):
+        src, dst = (
+            (middle_ref, middle_hbm),
+            (dmiddle_ref, dmiddle_hbm),
+            (branch_ref, branch_hbm),
+        )[kind]
+        return pltpu.make_async_copy(src.at[at(chunk)], dst.at[at(chunk)], own_sem.at[kind, chunk])
 
     def begin_seed(chunk):
         need(2)
@@ -760,6 +774,8 @@
             gather_seed.drain(chunk)
         for kind in range(6 if chunk >= chunks - 2 else 2):
             store(kind, chunk).wait()
+        for kind in range(3):
+            store_own(kind, chunk).wait()
 
 
 def feed_forward(size, chunks, mixed, out_weight, tokens, cotangent, seed_first, hidden_gate, hidden_up, hidden_down, gain, bias):
@@ -789,9 +805,12 @@
         ),
         in_specs=[pl.BlockSpec(memory_space=pl.ANY)] * 8
         + [pl.BlockSpec(memory_space=pltpu.VMEM)] * 2,
-        out_specs=(pl.BlockSpec(memory_space=pl.ANY),) * 6
-        + (pl.BlockSpec(memory_space=pltpu.VMEM),) * 4,
+        out_specs=(pl.BlockSpec(memory_space=pl.ANY),) * 9
+        + (pl.BlockSpec(memory_space=pltpu.VMEM),),
         scratch_shapes=[
+            pltpu.VMEM((own, depth), full),
+            pltpu.VMEM((own, depth), full),
+            pltpu.VMEM((own, depth), low),
             pltpu.VMEM((size, own, mixed.shape[-1]), low),
             pltpu.VMEM(out_weight.shape, low),
             pltpu.VMEM((own, depth), low),
@@ -811,6 +830,7 @@
             pltpu.VMEM((2, size, rows, depth), low),
             dma((8,)),
             dma((6, chunks)),
+            dma((3, chunks)),
             dma((size, chunks)),
             dma((size + 1, chunks)),
             dma((size, chunks)),
@@ -1065,9 +1085,11 @@
     dgates_hbm,
     dqueries_hbm,
     dkeys_hbm,
-    dtokens_ref,
+    dtokens_hbm,
     totals_ref,
     totals_hbm,
+    dtokens_ref,
+    own_sem,
     first_part,
     first_inbox,
     line_box,
@@ -1158,6 +1180,11 @@
             )
 
         for_rows(rows, body)
+        store_own(chunk).start()
+
+    def store_own(chunk):
+        here = pl.ds(chunk * rows, rows)
+        return pltpu.make_async_copy(dtokens_ref.at[here], dtokens_hbm.at[here], own_sem.at[chunk])
 
     def line_copy(step, slot):
         return pltpu.make_async_remote_copy(
@@ -1272,6 +1299,7 @@
     run_streams(streams, ORDERS.get(("last", size, chunks, bits)), after)
     for chunk in range(chunks):
         first.drain(chunk)
+        store_own(chunk).wait()
     for step in range(1, size):
         line_copy(step, me).wait_send()
     for step in range(1, groups):
@@ -1298,8 +1326,10 @@
             grads,
         ),
         in_specs=[anywhere] * 4 + [vmem] * 4 + [anywhere] * 5,
-        out_specs=(vmem, vmem, many),
+        out_specs=(anywhere, vmem, many),
         scratch_shapes=[
+            pltpu.VMEM((own, depth), full),
+            dma((chunks,)),
             pltpu.VMEM((size, own, depth), low),
             pltpu.VMEM((size + 1, own, depth), low),
             pltpu.VMEM((size, 8, depth), full),

time: 624 us -> 622 us (level)
  no operation moved by 1% of the time
where the time goes in v8:
time: 622 us; the launch traced here: 612 us
  Pallas kernels  607 us (98%)
    pallas_call x1, Pallas kernels, feed_forward(): pl.pallas_call(functools.partial(feed_kernel, size, chunks), out_shape=(b...  203 us
    pallas_call x1, Pallas kernels, last_sums(): pl.pallas_call(functools.partial(last_kernel, size, bits, chunks), out_sh...  124 us
    pallas_call x1, Pallas kernels, feed_back(): pl.pallas_call(functools.partial(back_kernel, size, bits, chunks), out_sh...  114 us
    pallas_call x1, Pallas kernels, first_part(): pl.pallas_call(functools.partial(first_kernel, size, chunks, heads), out_...  93.1 us
    pallas_call x1, Pallas kernels, retain_back(): pl.pallas_call(functools.partial(retain_kernel, size, bits, heads), out_s...  44.5 us
    pallas_call x1, Pallas kernels, cast_all(): pl.pallas_call(functools.partial(cast_kernel, len(items)), out_shape=shap...  29.3 us

profile of v8, /device:TPU:0, one launch (start us, length us, event | category | flops | bytes accessed | tf_op | source)
XLA Modules:
  0.0 612.3 jit_solution(10474595690334357290)
XLA Ops:
  0.6 0.5 log-plus-one_negate_fusion.rates_ref
  1.2 1.7 copy.29.column_ref
  2.9 93.1 %shard_map.254 = (bf16[4,256,2048]{2,1,0:T(8,128)(2,1)}, bf16[4,256,512]{2,1,0:T(8,128)(2,1)}, bf16[4,256,512]{2,1,0:T(8,128)(2,1)}, bf16[2,4,256,432]{3,2,1,0:T...) custom-call(bf16[256,2048]{1,0:T(8,128)(2,1)} %tokens_ref.3, ...), custom_call_target="tpu_custom_call" | custom-call | flops 8589934592 | bytes 67108864 | tf_op jit(solution)/shard_map/pallas_call | solution.py:1622
  96.0 202.9 %shard_map.255 = (bf16[4,256,2048]{2,1,0:T(8,128)(2,1)}, bf16[4,256,2048]{2,1,0:T(8,128)(2,1)}, bf16[4,256,864]{2,1,0:T(8,128)(2,1)}, bf16[4,256,864]{2,1,0:T(8,...) custom-call(bf16[4,256,864]{2,1,0:T(8,128)(2,1)} %get-tuple-element., ...), custom_call_target="tpu_custom_call" | custom-call | flops 25367150592 | bytes 67108864 | tf_op jit(solution)/shard_map/pallas_call | solution.py:792
  298.9 113.9 %shard_map.256 = (bf16[4,256,2048]{2,1,0:T(8,128)(2,1)}, f32[2,4,256,432]{3,2,1,0:T(8,128)}, bf16[256,2048]{1,0:T(8,128)(2,1)}, bf16[864,2048]{1,0:T(8,128)(2,1)...) custom-call(bf16[4,256,2048]{2,1,0:T(8,128)(2,1)} %get-tuple-element.67.outp_hbm, bf16[864,2048]{1,0:T(8,128)(2,1)} %out_hbm.3, ...), custom_call_target="tpu_custom_call" | custom-call | flops 3623878656 | bytes 67108864 | tf_op jit(solution)/shard_map/pallas_call | solution.py:1033
  412.9 44.5 %shard_map.257 = (bf16[4,256,512]{2,1,0:T(8,128)(2,1)}, bf16[4,256,512]{2,1,0:T(8,128)(2,1)}, bf16[4,256,864]{2,1,0:T(8,128)(2,1)}, bf16[4,256,864]{2,1,0:T(8,128)(2,1)}, bf16[864,2048]{1,0:T(8,128)(2,1)}) custom-call(bf16[4,256,512]{2,1,0:T(8,128)(2,1)} %get-tuple-element.60.queries_hbm, bf16[4,256,512]{2,1,0:T(8,128)(2,1)} %get-tuple-element.61.keys_hbm, ...), custom_call_target="tpu_custom_call" | custom-call | flops 17179869184 | bytes 67108864 | tf_op jit(solution)/shard_map/pallas_call | solution.py:1879
  457.4 123.5 %shard_map.258 = (f32[256,2048]{1,0:T(8,128)}, f32[8,2048]{1,0:T(8,128)}, bf16[864,2048]{1,0:T(8,128)(2,1)}, bf16[864,2048]{1,0:T(8,128)(2,1)}, bf16[2048,512]{1,0:T(8,128)(2,1)}, /*index=5*/bf16[2048,512]{1,0:T(8,128)(2,1)}) custom-call(bf16[2048,512]{1,0:T(8,128)(2,1)} %query_hbm.3, bf16[2048,512]{1,0:T(8,128)(2,1)} %key_hbm.3, ...), custom_call_target="tpu_custom_call" | custom-call | flops 1073741824 | bytes 67108864 | tf_op jit(solution)/shard_map/pallas_call | solution.py:1321
  580.9 1.6 fusion
  582.5 29.3 %shard_map.259 = (f32[864,2048]{1,0:T(8,128)}, f32[864,2048]{1,0:T(8,128)}, f32[864,2048]{1,0:T(8,128)}, f32[2048,512]{1,0:T(8,128)}, f32[2048,512]{1,0:T(8,128)...) custom-call(bf16[864,2048]{1,0:T(8,128)(2,1)} %get-tuple-element.78., ...), custom_call_target="tpu_custom_call" | custom-call | tf_op jit(solution)/shard_map/pallas_call | solution.py:1925
